TPU v7x, 32 devices: a whole 2x2x4 slice. The times are simulated.
32 devices in a mesh: groups: 2 (over y), blk: 16 (over z, x, core).
Axes of the slice: x: 2, y: 2, z: 4, core: 2. Of those that a mesh axis runs over, the one named last changes fastest.
Arguments:
- tokens: bfloat16 [4096, 16384], P(('groups', 'blk')), parts along dimension 0, may hold values from -6 to 6
- gain: float32 [16384], replicated, may hold values from 0.1 to 1.9
- w_query: bfloat16 [16384, 256], P('blk'), may hold values from -0.046875 to 0.046875
- w_key_value: bfloat16 [16384, 256], P('blk'), may hold values from -0.046875 to 0.046875
- w_out: bfloat16 [256, 16384], P(None, 'blk'), may hold values from -0.375 to 0.375
- cache_kv: bfloat16 [32, 8192, 256], P(('groups', 'blk')), parts along dimension 0, may hold values from -288 to 288
- cached_len: int32 [32], P('groups'), parts along dimension 0, may hold values from 1 to 8192, as said below
Outputs:
- mixed: bfloat16 [4096, 16384], P(('groups', 'blk')), parts along dimension 0
There are 2 independent parts, one for each index of `groups`. A program takes and returns all parts, laid end to end along the dimension named above; an argument that names none is the same for every part. Nothing has to cross between parts.
Inputs may be any that keep to these rules, and one draw needn't show every extreme that they name: `cached_len`: in every draw some prompt has all 8192 slots cached.
All inputs are finite; a program needn't handle non-finite values.
Results may differ from a plain program's by a relative error of at most 0.0065.
Values may be sent and summed in bfloat16 or wider, within the bound.
No kernel may reach another device: no remote copies, remote signals or barrier semaphores. Data moves between devices by JAX's collectives and lax.ppermute only.
A program may use at most 128 MiB of HBM per device.

v0:
```python
import jax
import jax.numpy as jnp
from jax import lax
from jax.sharding import PartitionSpec as P


def rotate(values, positions):
    half_size = values.shape[-1] // 2
    steps = jnp.arange(half_size, dtype=jnp.float32) * (2.0 / values.shape[-1])
    freqs = jnp.exp(-jnp.log(jnp.float32(500000.0)) * steps)
    angles = positions[:, None] * freqs[None, :]
    cosine = jnp.cos(angles)[:, None, :]
    sine = jnp.sin(angles)[:, None, :]
    first = values[..., :half_size]
    second = values[..., half_size:]
    return jnp.concatenate(
        [first * cosine - second * sine, second * cosine + first * sine], axis=-1
    )


def body(tokens, gain, w_query, w_key_value, w_out, cache_kv, cached_len):
    tok_rows = tokens.shape[0]
    head_size = w_key_value.shape[1] // 2
    heads = w_query.shape[1] // head_size
    prompt = lax.axis_index("blk")
    length = jnp.sum(
        jnp.where(jnp.arange(cached_len.shape[0], dtype=jnp.int32) == prompt, cached_len, 0)
    )
    widened = tokens.astype(jnp.float32)
    normed = (
        widened * lax.rsqrt(jnp.mean(widened * widened, axis=-1, keepdims=True) + 1e-05) * gain
    ).astype(jnp.bfloat16)

    def add_rows(piece):
        return jnp.dot(normed, piece, preferred_element_type=jnp.float32)

    query = add_rows(lax.all_gather(w_query, "blk", axis=0, tiled=True))
    keyval = add_rows(lax.all_gather(w_key_value, "blk", axis=0, tiled=True))
    positions = length.astype(jnp.float32) + jnp.arange(tok_rows, dtype=jnp.float32)
    q_rot = rotate(query.reshape(tok_rows, heads, head_size), positions).astype(jnp.bfloat16)
    k_rot = rotate(keyval[:, None, :head_size], positions)[:, 0, :].astype(jnp.bfloat16)
    val = keyval[:, head_size:].astype(jnp.bfloat16)
    new_kv = jnp.concatenate([k_rot, val], axis=1)
    cache_rows = cache_kv[0]
    everything = jnp.concatenate([cache_rows, new_kv], axis=0)
    keys = everything[:, :head_size]
    values = everything[:, head_size:]
    scores = jnp.einsum(
        "tqh,kh->qtk", q_rot, keys, preferred_element_type=jnp.float32
    ) * head_size ** (-0.5)
    slots = jnp.arange(cache_rows.shape[0], dtype=jnp.int32)
    cache_mask = jnp.broadcast_to((slots < length)[None, :], (tok_rows, cache_rows.shape[0]))
    steps_new = jnp.arange(tok_rows, dtype=jnp.int32)
    own_mask = steps_new[None, :] <= steps_new[:, None]
    mask = jnp.concatenate([cache_mask, own_mask], axis=1)[None, :, :]
    scores = jnp.where(mask, scores, -1e30)
    top = jnp.max(scores, axis=-1, keepdims=True)
    expo = jnp.where(mask, jnp.exp(scores - top), 0.0)
    weights = (expo / jnp.sum(expo, axis=-1, keepdims=True)).astype(jnp.bfloat16)
    attended = jnp.einsum("qtk,kh->tqh", weights, values, preferred_element_type=jnp.float32)
    attended = attended.astype(jnp.bfloat16).reshape(tok_rows, heads * head_size)
    projected = jnp.dot(
        attended,
        lax.all_gather(w_out, "blk", axis=1, tiled=True),
        preferred_element_type=jnp.float32,
    )
    return (widened + projected).astype(jnp.bfloat16)


def solution(mesh):
    placed = (
        P(("groups", "blk"), None),
        P(),
        P("blk", None),
        P("blk", None),
        P(None, "blk"),
        P(("groups", "blk"), None, None),
        P("groups"),
    )
    return jax.shard_map(
        body, mesh=mesh, in_specs=placed, out_specs=P(("groups", "blk"), None), check_vma=False
    )
```

profile of v0, /device:TPU:0, one launch (start us, length us, event | category | flops | bytes accessed | tf_op | source)
XLA Modules:
  0.0 252.3 jit_solution(2671591584792278351)
XLA Ops:
  6.5 0.0 all-gather.4.cloned.1.call-start
  6.5 0.7 all-gather.4.cloned.1.call-update
  7.3 0.0 all-gather.6.cloned.1.call-start
  7.3 0.7 all-gather.6.cloned.1.call-update
  8.0 0.0 all-gather.8.cloned.1.call-start
  8.1 0.7 all-gather.8.cloned.1.call-update
  8.7 1.3 fusion.32
  10.7 0.7 iota_compare_fusion.1
  11.4 3.1 %fusion.3 = f32[128]{0:T(128)S(1)} fusion(bf16[128,16384]{1,0:T(8,128)(2,1)} %param.7), kind=kLoop, calls=%fused_computation.9 | loop fusion | flops 6291328 | bytes 4194816 | tf_op jit(solution)/shard_map/reduce_sum | solution.py:31
  14.5 0.0 copy-start.1
  14.5 0.3 multiply_cosine_fusion
  14.8 8.3 %pad_add_fusion = pred[128,8320]{0,1:T(8,128)(4,1)S(1)} fusion(pred[128,128]{0,1:T(8,128)(4,1)S(1)} %iota_compare_fusion, pred[8320]{0:T(1024)(128)(4,1)S(1)} %pad.2.clone), kind=kLoop, calls=%fused_computation.15 | loop fusion | flops 1064960 | bytes 1089664 | tf_op jit(solution)/shard_map/concatenate | solution.py:55
  23.2 64.0 %all-gather.4.cloned.1.call-done = bf16[16384,256]{1,0:T(8,128)(2,1)} async-done(((bf16[1024,256]{1,0:T(8,128)(2,1)}), bf16[16384,256]{1,0:T(8,128)(2,1)}) %all-gather.4.cloned.1.call-update) | async-done | bytes 8388624 | tf_op jit(solution)/shard_map/all_gather | solution.py:38
  87.1 8.2 %fusion.16 = f32[128,256]{0,1:T(8,128)S(1)} fusion(bf16[16384,256]{1,0:T(8,128)(2,1)} %all-gather.4.cloned.1.call-done, bf16[128,16384]{1,0:T(8,128)(2,1)} %param.7, f32[16384]{0:T(1024)} %param.8, f32[128]{0:T(128)S(1)} %add_rsqrt_fusion), kind=kOutput, calls=%fused_computation.23 | convolution fusion | flops 1082130432 | bytes 12780032 | tf_op jit(solution)/shard_map/dot_general | solution.py:35
  95.4 0.2 fusion.29
  95.6 0.1 copy.14
  95.7 66.7 %all-gather.6.cloned.1.call-done = bf16[16384,256]{1,0:T(8,128)(2,1)} async-done(((bf16[1024,256]{1,0:T(8,128)(2,1)}), bf16[16384,256]{1,0:T(8,128)(2,1)}) %all-gather.6.cloned.1.call-update) | async-done | bytes 8388624 | tf_op jit(solution)/shard_map/all_gather | solution.py:37
  162.5 0.0 copy-done.1
  162.5 6.0 %fusion.14 = f32[128,256]{1,0:T(8,128)S(1)} fusion(bf16[16384,256]{1,0:T(8,128)(2,1)} %all-gather.6.cloned.1.call-done, bf16[128,16384]{1,0:T(8,128)(2,1)} %param.7, f32[16384]{0:T(1024)S(1)} %copy-done.1, f32[128]{0:T(128)S(1)} %add_rsqrt_fusion), kind=kOutput, calls=%fused_computation.22 | convolution fusion | flops 1082130432 | bytes 12780032 | tf_op jit(solution)/shard_map/dot_general | solution.py:35
  168.4 0.1 reshape.125
  168.5 0.2 fusion.36
  168.8 5.5 %fusion.37 = (f32[2,128]{1,0:T(2,128)S(1)}, f32[2,128,8320]{1,2,0:T(8,128)S(1)}) fusion(bf16[128,2,64]{2,0,1:T(8,128)(2,1)S(1)} %get-tuple-element.6, bf16[128,2,64]{2,0,1:T(8,128)(2,1)S(1)} %get-tuple-element.5, bf16[128,256]{1,0:T(8,128)(2,1)S(1)} %copy.14, bf16[8192,256]{1,0:T(8,128)(2,1)} %bitcast.27, pred[128,8320]{0,1:T(8,128)(4,1)S(1)} %pad_add_fusion), kind=kOutput, calls=%fused_computation.57 | convolution fusion | flops 556039936 | bytes 13911040 | tf_op jit(solution)/shard_map/tqh,kh->qtk/dot_general | solution.py:48
  174.3 0.0 copy-start
  174.3 1.9 fusion.6
  176.2 0.3 copy-done
  176.5 2.1 fusion.18
  178.6 59.3 %all-gather.8.cloned.1.call-done = bf16[256,16384]{1,0:T(8,128)(2,1)} async-done(((bf16[256,1024]{1,0:T(8,128)(2,1)}), bf16[256,16384]{1,0:T(8,128)(2,1)}) %all-gather.8.cloned.1.call-update) | async-done | bytes 8388624 | tf_op jit(solution)/shard_map/all_gather | solution.py:64
  237.9 7.9 %fusion = bf16[128,16384]{1,0:T(8,128)(2,1)} fusion(bf16[128,256]{0,1:T(8,128)(2,1)S(1)} %bitcast.26, bf16[256,16384]{1,0:T(8,128)(2,1)} %all-gather.8.cloned.1.call-done, bf16[128,16384]{1,0:T(8,128)(2,1)} %param.7), kind=kOutput, calls=%fused_computation.1 | convolution fusion | flops 1080033280 | bytes 16842752 | tf_op jit(solution)/shard_map/dot_general | solution.py:62
  (10 shorter events, 0.1 us)
Async XLA Ops:
  6.5 80.6 %all-gather.4.cloned.1.call-start = ((), (), s32[]{:S(2)}) async-start(), calls=%async_computation | async-start | bytes 8912896 | tf_op jit(solution)/shard_map/all_gather | solution.py:38
  7.3 155.2 %all-gather.6.cloned.1.call-start = ((), (), s32[]{:S(2)}) async-start(), calls=%async_computation.1 | async-start | bytes 8912896 | tf_op jit(solution)/shard_map/all_gather | solution.py:37
  8.0 229.9 %all-gather.8.cloned.1.call-start = ((), (), s32[]{:S(2)}) async-start(), calls=%async_computation.2 | async-start | bytes 8912896 | tf_op jit(solution)/shard_map/all_gather | solution.py:64
  14.5 148.0 %copy-start.1 = (f32[16384]{0:T(1024)S(1)}, f32[16384]{0:T(1024)}, u32[]{:S(2)}) copy-start(f32[16384]{0:T(1024)} %param.8) | copy-start | bytes 196612
  174.3 2.2 copy-start
Sparse Core Ops, SparseCore 0:
  9.5 77.5 all-gather.3
  89.3 73.1 all-gather.5
  164.7 73.1 all-gather.7
where the time goes:
time: 253 us; the launch traced here: 252 us
  waiting for transfers between devices  192 us (76%)
  matrix products  29.7 us (12%)
  other arithmetic  15.9 us (6%)
  between operations  13.9 us (5%)
    all_gather x1, waiting for transfers between devices, body(): query = add_rows(lax.all_gather(w_query, 'blk', axis=0, tiled=True))  66.7 us
    all_gather x1, waiting for transfers between devices, body(): keyval = add_rows(lax.all_gather(w_key_value, 'blk', axis=0, tiled=True))  64 us
    all_gather x1, waiting for transfers between devices, body(): lax.all_gather(w_out, 'blk', axis=1, tiled=True)  59.3 us
    dot_general x2, matrix products, add_rows(): return jnp.dot(normed, piece, preferred_element_type=jnp.float32)  14.2 us
    concatenate x1, other arithmetic, body(): mask = jnp.concatenate([cache_mask, own_mask], axis=1)[None, :, :]  8.32 us
    dot_general x1, matrix products, body(): jnp.dot(attended, lax.all_gather(w_out, 'blk', axis=1, tiled=True), prefe...  7.88 us
    dot_general x1, matrix products, body(): jnp.einsum('tqh,kh->qtk', q_rot, keys, preferred_element_type=jnp.float32)  5.52 us
  transfers between devices with their start and end apart: 3, of which 3 were waited for; matrix products, arithmetic and copies ran while one was open for 15% of the time, Pallas kernels for 0%

commit v1 on v0

v1 whole, which is shorter than its diff:
```python
import functools

import jax
import jax.numpy as jnp
from jax import lax
from jax.experimental import pallas as pl
from jax.experimental.pallas import tpu as pltpu
from jax.sharding import Mesh, PartitionSpec as P

F32 = jnp.float32
BF16 = jnp.bfloat16
AXES = ("y", "z", "r", "x", "c")
VMEM_LIMIT = 56 * 1024 * 1024


def params():
    return pltpu.CompilerParams(vmem_limit_bytes=VMEM_LIMIT)


def norm_kernel(idx, tok, gain, *outs, nz, nr, bs):
    x, c = idx[1], idx[2]
    width = tok.shape[1]
    step = 1024
    for r0 in range(0, tok.shape[0], 16):
        rows = pl.ds(r0, 16)
        acc = jnp.zeros((16, step), F32)
        for j in range(width // step):
            v = tok[rows, pl.ds(j * step, step)].astype(F32)
            acc = acc + v * v
        inv = lax.rsqrt(jnp.sum(acc, axis=1, keepdims=True) * (1.0 / width) + 1e-05)
        for k, out in enumerate(outs):
            part = (x ^ (k // 2)) * 2 + (c ^ (k % 2))
            for g in range(nz * nr):
                cols = pl.ds(pl.multiple_of((g * 4 + part) * bs, bs), bs)
                v = tok[rows, cols].astype(F32) * inv * gain[:, cols]
                out[rows, pl.ds(g * bs, bs)] = v.astype(BF16)


def normalise(idx, tokens, gain, nz, nr, bs):
    rows, width = tokens.shape
    block = 32
    quarter = width // 4
    return pl.pallas_call(
        functools.partial(norm_kernel, nz=nz, nr=nr, bs=bs),
        grid_spec=pltpu.PrefetchScalarGridSpec(
            num_scalar_prefetch=1,
            grid=(rows // block,),
            in_specs=[
                pl.BlockSpec((block, width), lambda i, s: (i, 0)),
                pl.BlockSpec((1, width), lambda i, s: (0, 0)),
            ],
            out_specs=[pl.BlockSpec((block, quarter), lambda i, s: (i, 0))] * 4,
        ),
        out_shape=[jax.ShapeDtypeStruct((rows, quarter), BF16)] * 4,
        compiler_params=params(),
        cost_estimate=pl.CostEstimate(flops=8 * rows * width, bytes_accessed=4 * rows * width, transcendentals=0),
        name="norm",
    )(idx, tokens, gain.reshape(1, width))


def project_kernel(idx, *refs, nz, half, lead):
    toks, refs = refs[:4], refs[4:]
    own_q, own_kv = refs[:2]
    near = refs[2 : 2 + nz - 1]
    far = refs[2 + nz - 1 : 2 * nz]
    outs = refs[2 * nz : 2 * nz + 4]
    tbuf, wbuf, qbuf, tsem, wsem = refs[2 * nz + 4 :]
    y, z = idx[3], idx[0]
    copies = []
    for i in range(4):
        copies.append(pltpu.make_async_copy(toks[i], tbuf.at[i], tsem.at[i]))
    own = [
        pltpu.make_async_copy(own_q, qbuf.at[0], wsem.at[0]),
        pltpu.make_async_copy(own_kv, qbuf.at[1], wsem.at[1]),
    ]
    rest = [
        pltpu.make_async_copy(ref, wbuf.at[i], wsem.at[2 + i]) for i, ref in enumerate(list(near) + list(far))
    ]
    for cp in own + copies + rest:
        cp.start()
    for cp in own + copies:
        cp.wait()
    start = pl.multiple_of(z * 2 * half, 2 * half)
    for i in range(4):
        t = tbuf[i, :, pl.ds(start, 2 * half)]
        outs[i][:, :lead] = jnp.dot(t, qbuf[0], preferred_element_type=F32)
        outs[i][:, lead:] = jnp.dot(t, qbuf[1], preferred_element_type=F32)
    for n in range(2 * (nz - 1)):
        rest[n].wait()
        s = n % (nz - 1) + 1
        side = y if n < nz - 1 else 1 - y
        start = pl.multiple_of(lax.rem(z - s + nz, nz) * 2 * half + side * half, half)
        w = wbuf[n]
        for i in range(4):
            outs[i][...] += jnp.dot(tbuf[i, :, pl.ds(start, half)], w, preferred_element_type=F32)


def project(idx, toks, own_q, own_kv, near, far):
    nz = len(near) + 1
    rows = toks[0].shape[0]
    half, width = near[0].shape
    anywhere = pl.BlockSpec(memory_space=pl.ANY)
    lead = own_q.shape[1]
    return pl.pallas_call(
        functools.partial(project_kernel, nz=nz, half=half, lead=lead),
        in_specs=[pl.BlockSpec(memory_space=pltpu.SMEM)] + [anywhere] * (4 + 2 * nz),
        out_specs=[pl.BlockSpec(memory_space=pltpu.VMEM)] * 4,
        out_shape=[jax.ShapeDtypeStruct((rows, width), F32)] * 4,
        scratch_shapes=[
            pltpu.VMEM((4,) + toks[0].shape, BF16),
            pltpu.VMEM((2 * (nz - 1), half, width), BF16),
            pltpu.VMEM((2, 2 * half, lead), BF16),
            pltpu.SemaphoreType.DMA((4,)),
            pltpu.SemaphoreType.DMA((2 * nz,)),
        ],
        compiler_params=params(),
        cost_estimate=pl.CostEstimate(
            flops=2 * 4 * rows * toks[0].shape[1] * width, bytes_accessed=16 * 1024 * 1024, transcendentals=0
        ),
        name="project",
    )(idx, *toks, own_q, own_kv, *near, *far)


def attend_kernel(idx, mine, other, cos, sin, cache, out, kvbuf, sem, *, heads, head):
    length = idx[4]
    slots = kvbuf.shape[0]
    rows = mine.shape[0]
    chunk = 1024
    copies = [
        pltpu.make_async_copy(
            cache.at[0, pl.ds(i * chunk, chunk)], kvbuf.at[pl.ds(i * chunk, chunk)], sem.at[i]
        )
        for i in range(slots // chunk)
    ]
    for cp in copies:
        cp.start()
    total = mine[...] + other[...]

    def turn(v):
        return (v * cos[...] + pltpu.roll(v, head // 2, 1) * sin[...]).astype(BF16)

    q = jnp.concatenate([turn(total[:, i * head : (i + 1) * head]) for i in range(heads)], axis=0)
    k_new = turn(total[:, heads * head : (heads + 1) * head])
    v_new = total[:, (heads + 1) * head :].astype(BF16)
    scale = (head ** -0.5) * 1.4426950408889634

    def scores(keys):
        return lax.dot_general(q, keys, (((1,), (1,)), ((), ())), preferred_element_type=F32)

    s = scores(k_new)
    row = lax.broadcasted_iota(jnp.int32, s.shape, 0) % rows
    col = lax.broadcasted_iota(jnp.int32, s.shape, 1)
    s = jnp.where(col <= row, s, -1e30)
    top = jnp.max(s, axis=1, keepdims=True)
    p = jnp.exp2((s - top) * scale)
    total_p = jnp.sum(p, axis=1, keepdims=True)
    acc = jnp.dot(p.astype(BF16), v_new, preferred_element_type=F32)
    for i, cp in enumerate(copies):
        cp.wait()
        s = scores(kvbuf[pl.ds(i * chunk, chunk), :head])
        col = lax.broadcasted_iota(jnp.int32, (1, chunk), 1) + i * chunk
        s = jnp.where(col < length, s, -1e30)
        new_top = jnp.maximum(top, jnp.max(s, axis=1, keepdims=True))
        p = jnp.exp2((s - new_top) * scale)
        fade = jnp.exp2((top - new_top) * scale)
        top = new_top
        total_p = total_p * fade + jnp.sum(p, axis=1, keepdims=True)
        acc = acc * fade + jnp.dot(
            p.astype(BF16), kvbuf[pl.ds(i * chunk, chunk), head:], preferred_element_type=F32
        )
    acc = (acc / total_p).astype(BF16)
    for i in range(heads):
        out[:, i * head : (i + 1) * head] = acc[i * rows : (i + 1) * rows]


def attend(idx, mine, other, cos, sin, cache, heads, head):
    vmem = pl.BlockSpec(memory_space=pltpu.VMEM)
    rows = mine.shape[0]
    slots = cache.shape[1]
    return pl.pallas_call(
        functools.partial(attend_kernel, heads=heads, head=head),
        in_specs=[pl.BlockSpec(memory_space=pltpu.SMEM)] + [vmem] * 4 + [pl.BlockSpec(memory_space=pl.ANY)],
        out_specs=vmem,
        out_shape=jax.ShapeDtypeStruct((rows, heads * head), BF16),
        scratch_shapes=[pltpu.VMEM(cache.shape[1:], BF16), pltpu.SemaphoreType.DMA((slots // 1024,))],
        compiler_params=params(),
        cost_estimate=pl.CostEstimate(
            flops=4 * rows * heads * head * slots, bytes_accessed=12 * 1024 * 1024, transcendentals=rows * heads * slots
        ),
        name="attend",
    )(idx, mine, other, cos, sin, cache)


def out_kernel(idx, att, tok, *refs, plan, nz, nr, bs):
    n = len(refs) - 6 - 1
    weights, out = refs[:n], refs[n]
    wbuf, tbuf, obuf, wsem, tsem, osem = refs[n + 1 :]
    z, x, c, y = idx[0], idx[1], idx[2], idx[3]
    half = att.shape[1] // 2
    rows = att.shape[0]
    flip = y == 1
    low, high = att[:, :half], att[:, half:]
    left = jnp.concatenate([jnp.where(flip, high, low), jnp.where(flip, low, high)], axis=1)
    slots = wbuf.shape[0]

    def cols(s, dx, dc, r):
        zz = lax.rem(z - s + nz, nz)
        return pl.ds(pl.multiple_of(((zz * nr + r) * 4 + (x ^ dx) * 2 + (c ^ dc)) * bs, bs), bs)

    def load(b):
        (s, dx, dc), halves = plan[b]
        slot = b % slots
        cps = []
        for h, (ref, lead, pos) in enumerate(halves):
            src = weights[ref] if lead is None else weights[ref].at[lead]
            if pos is not None:
                side = y if pos == 0 else 1 - y
                src = src.at[pl.ds(pl.multiple_of(side * half, half), half)]
            cps.append(pltpu.make_async_copy(src, wbuf.at[slot, pl.ds(h * half, half)], wsem.at[slot, h]))
        for r in range(nr):
            cps.append(
                pltpu.make_async_copy(tok.at[:, cols(s, dx, dc, r)], tbuf.at[slot, :, pl.ds(r * bs, bs)], tsem.at[slot, r])
            )
        return cps

    def store(b):
        (s, dx, dc), _ = plan[b]
        slot = b % slots
        return [
            pltpu.make_async_copy(obuf.at[slot, :, pl.ds(r * bs, bs)], out.at[:, cols(s, dx, dc, r)], osem.at[slot, r])
            for r in range(nr)
        ]

    for b in range(min(slots, len(plan))):
        for cp in load(b):
            cp.start()
    for b in range(len(plan)):
        slot = b % slots
        for cp in load(b):
            cp.wait()
        if b >= slots:
            for cp in store(b - slots):
                cp.wait()
        v = jnp.dot(left, wbuf[slot], preferred_element_type=F32)
        obuf[slot] = (tbuf[slot].astype(F32) + v).astype(BF16)
        for cp in store(b):
            cp.start()
        if b + slots < len(plan):
            for cp in load(b + slots):
                cp.start()
    for b in range(max(0, len(plan) - slots), len(plan)):
        for cp in store(b):
            cp.wait()


def output(idx, att, tokens, weights, plan, nz, nr, bs):
    anywhere = pl.BlockSpec(memory_space=pl.ANY)
    slots = 4
    rows, width = tokens.shape
    return pl.pallas_call(
        functools.partial(out_kernel, plan=plan, nz=nz, nr=nr, bs=bs),
        in_specs=[pl.BlockSpec(memory_space=pltpu.SMEM), pl.BlockSpec(memory_space=pltpu.VMEM)]
        + [anywhere] * (1 + len(weights)),
        out_specs=anywhere,
        out_shape=jax.ShapeDtypeStruct(tokens.shape, BF16),
        scratch_shapes=[
            pltpu.VMEM((slots, att.shape[1], nr * bs), BF16),
            pltpu.VMEM((slots, rows, nr * bs), BF16),
            pltpu.VMEM((slots, rows, nr * bs), BF16),
            pltpu.SemaphoreType.DMA((slots, 2)),
            pltpu.SemaphoreType.DMA((slots, nr)),
            pltpu.SemaphoreType.DMA((slots, nr)),
        ],
        compiler_params=params(),
        cost_estimate=pl.CostEstimate(
            flops=2 * rows * width * att.shape[1], bytes_accessed=16 * 1024 * 1024, transcendentals=0
        ),
        name="output",
    )(idx, att, tokens, *weights)


def body(tokens, gain, w_query, w_key_value, w_out, cache_kv, cached_len, *, nz, nr):
    rows = tokens.shape[0]
    head = w_key_value.shape[1] // 2
    heads = w_query.shape[1] // head
    bs = w_query.shape[0]
    y, z, x, c = (lax.axis_index(a) for a in ("y", "z", "x", "c"))
    prompt = ((z * nr + lax.axis_index("r")) * 2 + x) * 2 + c
    length = jnp.sum(jnp.where(jnp.arange(cached_len.shape[0], dtype=jnp.int32) == prompt, cached_len, 0))
    idx = jnp.stack([z, x, c, y, length]).astype(jnp.int32)

    def swap(v, axis):
        return lax.ppermute(v, axis, [(0, 1), (1, 0)])

    def across(v):
        return lax.ppermute(v, ("x", "c"), [(i, i ^ 3) for i in range(4)])

    def ring(v):
        return lax.ppermute(v, "z", [(i, (i + 1) % nz) for i in range(nz)])

    own_q, own_kv, own_o = w_query, w_key_value, w_out
    if nr > 1:
        own_q = lax.all_gather(own_q, "r", axis=0, tiled=True)
        own_kv = lax.all_gather(own_kv, "r", axis=0, tiled=True)
        own_o = lax.all_gather(own_o, "r", axis=1, tiled=True)
    half = own_q.shape[0] // 2
    ohalf = own_o.shape[0] // 2

    w_near = [
        jnp.concatenate(
            [lax.dynamic_slice_in_dim(own_q, y * half, half), lax.dynamic_slice_in_dim(own_kv, y * half, half)], axis=1
        )
    ]
    o_mine = lax.dynamic_slice_in_dim(own_o, y * ohalf, ohalf)
    o_else = lax.dynamic_slice_in_dim(own_o, (1 - y) * ohalf, ohalf)
    o_mine_x = swap(o_mine, "x")
    toks = normalise(idx, tokens, gain, nz, nr, bs)
    w_far = []
    o_near = [jnp.stack([o_mine, o_mine_x])]
    o_far = []
    for s in range(1, nz):
        w_near.append(ring(w_near[-1]))
        w_far.append(swap(w_near[-1], "y"))
        o_near.append(ring(o_near[-1]))
        o_far.append(swap(o_near[-1], "y"))
    held = [toks[0], swap(toks[1], "c"), swap(toks[2], "x"), across(toks[3])]
    parts = project(idx, held, own_q, own_kv, w_near[1:], w_far)
    from_c0 = swap(parts[1], "c")
    from_c1 = swap(parts[3], "c")
    other = swap(parts[2] + from_c1, "x")
    o_else_x = swap(o_else, "x")
    mine = parts[0] + from_c0

    positions = length.astype(F32) + jnp.arange(rows, dtype=F32)
    steps = jnp.arange(head // 2, dtype=F32) * (2.0 / head)
    freqs = jnp.exp(-jnp.log(jnp.float32(500000.0)) * steps)
    angles = positions[:, None] * freqs[None, :]
    cos, sin = jnp.cos(angles), jnp.sin(angles)
    att = attend(
        idx,
        mine,
        other,
        jnp.concatenate([cos, cos], axis=1),
        jnp.concatenate([-sin, sin], axis=1),
        cache_kv,
        heads,
        head,
    )

    weights, plan = [], []

    def add(v):
        weights.append(v)
        return len(weights) - 1

    for dc in range(2):
        over = (lambda v: swap(v, "c")) if dc else (lambda v: v)
        own = add(over(own_o))
        mx, ex = add(over(o_mine_x)), add(over(o_else_x))
        plan.append(((0, 0, dc), [(own, None, 0), (own, None, 1)]))
        plan.append(((0, 1, dc), [(mx, None, None), (ex, None, None)]))
    for s in range(1, nz):
        for dc in range(2):
            over = (lambda v: swap(v, "c")) if dc else (lambda v: v)
            near, far = add(over(o_near[s])), add(over(o_far[s - 1]))
            for dx in range(2):
                plan.append(((s, dx, dc), [(near, dx, None), (far, dx, None)]))
    return output(idx, att, tokens, weights, plan, nz, nr, bs)


def solution(mesh):
    groups, blk = mesh.shape["groups"], mesh.shape["blk"]
    nz = 4
    nr = blk // (4 * nz)
    wide = Mesh(mesh.devices.reshape(groups, nz, nr, 2, 2), AXES)
    blocks = ("z", "r", "x", "c")
    placed = (
        P(AXES, None),
        P(),
        P(blocks, None),
        P(blocks, None),
        P(None, blocks),
        P(AXES, None, None),
        P("y"),
    )
    return jax.shard_map(
        functools.partial(body, nz=nz, nr=nr),
        mesh=wide,
        in_specs=placed,
        out_specs=P(AXES, None),
        check_vma=False,
    )
```

time: 253 us -> 134 us (0.53)
  waiting for transfers between devices: 192 us -> 66.5 us
  Pallas kernels: 0 us -> 29.8 us
  matrix products: 29.7 us -> 0 us
  starting transfers between devices: 0.08 us -> 23.6 us
  between operations: 13.9 us -> 0.87 us
  other arithmetic: 15.9 us -> 5.83 us
  local copies, waits for them, and re-layouts: 0.69 us -> 6.97 us
    all_gather x3 -> x0, waiting for transfers between devices: 190 us -> none  [the longest x1 66.7 us: body(): query = add_rows(lax.all_gather(w_query, 'blk', axis=0, tiled=True))]
    ppermute x0 -> x29, waiting for transfers between devices: none -> 66.5 us  [the longest x22 31.2 us: swap(): return lax.ppermute(v, axis, [(0, 1), (1, 0)])]
    pallas_call x0 -> x4, Pallas kernels: none -> 29.8 us  [the longest x1 8.44 us: output(): pl.pallas_call(functools.partial(out_kernel, plan=plan, nz=nz, nr=nr, bs=...]
    dot_general x5 -> x0, matrix products: 29.7 us -> none  [the longest x2 14.2 us: add_rows(): return jnp.dot(normed, piece, preferred_element_type=jnp.float32)]
    ppermute x0 -> x29, starting transfers between devices: none -> 23.6 us  [the longest x22 15.7 us: swap(): return lax.ppermute(v, axis, [(0, 1), (1, 0)])]
    concatenate x2, other arithmetic: 8.33 us -> 0.79 us  [the longest x1 0.76 us: body(): jnp.concatenate([cos, cos], axis=1)]
    reduce_sum x2 -> x0, other arithmetic: 4.97 us -> none  [the longest x1 3.08 us: body(): jnp.mean(widened * widened, axis=-1, keepdims=True) + 1e-05]
    add x1 -> x3, other arithmetic: 0.01 us -> 3.39 us  [the longest x1 1.69 us: body(): other = swap(parts[2] + from_c1, 'x')]
  transfers between devices with their start and end apart: 3 -> 29, of which waited for: 3 -> 10; matrix products, arithmetic and copies ran while one was open for 15% -> 6% of each run, Pallas kernels for 0% -> 16%
where the time goes in v1:
time: 134 us
  waiting for transfers between devices  66.5 us (50%)
  Pallas kernels  29.8 us (22%)
  starting transfers between devices  23.6 us (18%)
  local copies, waits for them, and re-layouts  6.97 us (5%)
  other arithmetic  5.83 us (4%)
    ppermute x22, waiting for transfers between devices, swap(): return lax.ppermute(v, axis, [(0, 1), (1, 0)])  31.2 us
    ppermute x6, waiting for transfers between devices, ring(): return lax.ppermute(v, 'z', [(i, (i + 1) % nz) for i in range(nz)])  28.3 us
    ppermute x22, starting transfers between devices, swap(): return lax.ppermute(v, axis, [(0, 1), (1, 0)])  15.7 us
    pallas_call x1, Pallas kernels, output(): pl.pallas_call(functools.partial(out_kernel, plan=plan, nz=nz, nr=nr, bs=...  8.44 us
    pallas_call x1, Pallas kernels, attend(): pl.pallas_call(functools.partial(attend_kernel, heads=heads, head=head),...  8.08 us
    ppermute x6, starting transfers between devices, ring(): return lax.ppermute(v, 'z', [(i, (i + 1) % nz) for i in range(nz)])  7.86 us
    pallas_call x1, Pallas kernels, project(): pl.pallas_call(functools.partial(project_kernel, nz=nz, half=half, lead=l...  7.48 us
    ppermute x1, waiting for transfers between devices, across(): return lax.ppermute(v, ('x', 'c'), [(i, i ^ 3) for i in range(4)])  7.04 us
  transfers between devices with their start and end apart: 29, of which 10 were waited for; matrix products, arithmetic and copies ran while one was open for 6% of the time, Pallas kernels for 16%

profile of v1, /device:TPU:0, one launch (start us, length us, event | category | flops | bytes accessed | tf_op | source)
XLA Modules:
  0.0 133.6 jit_solution(16203464782511185004)
XLA Ops:
  0.0 1.1 constant_dynamic-slice_fusion.2
  1.2 3.1 %collective-permute-start.3 = (bf16[512,512]{1,0:T(8,128)(2,1)S(1)}, bf16[512,512]{1,0:T(8,128)(2,1)S(1)}, u32[]{:S(2)}, u32[]{:S(2)}) collective-permute-start(bf16[512,512]{1,0:T(8,128)(2,1)S(1)} %pad_maximum_fusion), channel_id=1, source_target_pairs={{0,4},{4,8},{8,12},{12,0},{1,5},{5,9},{9,13},{13,1},{2,6},{6,10},{... | collective-permute-start | bytes 1572872 | tf_op jit(solution)/shard_map/ppermute | solution.py:299
  4.2 1.1 constant_dynamic-slice_fusion
  5.3 1.6 %collective-permute-start.12 = (bf16[128,1024]{1,0:T(8,128)(2,1)S(1)}, bf16[128,1024]{1,0:T(8,128)(2,1)S(1)}, u32[]{:S(2)}, u32[]{:S(2)}) collective-permute-start(bf16[128,1024]{1,0:T(8,128)(2,1)S(1)} %get-tuple-element.22), channel_id=1, source_target_pairs={{0,2},{2,0},{1,3},{3,1},{4,6},{6,4},{5,7},{7,5},{8,10},{10,8},{9,1... | collective-permute-start | bytes 786440 | tf_op jit(solution)/shard_map/ppermute | solution.py:293
  6.9 1.3 fusion.1
  8.2 1.2 stack.32.idx
  9.4 3.7 %collective-permute-done.12.refs_1_ = bf16[128,1024]{1,0:T(8,128)(2,1)S(1)} collective-permute-done((bf16[128,1024]{1,0:T(8,128)(2,1)S(1)}, bf16[128,1024]{1,0:T(8,128)(2,1)S(1)}, u32[]{:S(2)}, u32[]{:S(2)}) %collective-permute-start.12) | collective-permute-done | bytes 262176 | tf_op jit(solution)/shard_map/ppermute | solution.py:293
  13.2 1.6 %collective-permute-start.17 = (bf16[2,128,1024]{2,1,0:T(8,128)(2,1)S(1)}, bf16[2,128,1024]{2,1,0:T(8,128)(2,1)S(1)}, u32[]{:S(2)}, u32[]{:S(2)}) collective-permute-start(bf16[2,128,1024]{2,1,0:T(8,128)(2,1)S(1)} %pad_maximum_fusion.1), channel_id=1, source_target_pairs={{0,4},{4,8},{8,12},{12,0},{1,5},{5,9},{9,13},{13,1},{2,6},{6,10},{... | collective-permute-start | bytes 1572872 | tf_op jit(solution)/shard_map/ppermute | solution.py:299
  14.8 5.8 %norm.1 = (bf16[128,4096]{1,0:T(8,128)(2,1)}, bf16[128,4096]{1,0:T(8,128)(2,1)}, bf16[128,4096]{1,0:T(8,128)(2,1)}, bf16[128,4096]{1,0:T(8,128)(2,1)}) custom-call(s32[5]{0:T(128)} %stack.32.idx, bf16[128,16384]{1,0:T(8,128)(2,1)} %tok.3, f32[1,16384]{1,0:T(1,128)} %bitcast.10), custom_call_target="tpu_custom_call" | custom-call | flops 16777216 | bytes 8388608 | tf_op jit(solution)/shard_map/norm/pallas_call | solution.py:43
  20.6 1.5 %collective-permute-start.13 = (bf16[128,1024]{1,0:T(8,128)(2,1)S(1)}, bf16[128,1024]{1,0:T(8,128)(2,1)}, u32[]{:S(2)}, u32[]{:S(2)}) collective-permute-start(bf16[128,1024]{1,0:T(8,128)(2,1)S(1)} %get-tuple-element.21), channel_id=1, source_target_pairs={{0,2},{2,0},{1,3},{3,1},{4,6},{6,4},{5,7},{7,5},{8,10},{10,8},{9,1... | collective-permute-start | bytes 786440 | tf_op jit(solution)/shard_map/ppermute | solution.py:293
  22.2 1.6 %collective-permute-start.4 = (bf16[512,512]{1,0:T(8,128)(2,1)S(1)}, bf16[512,512]{1,0:T(8,128)(2,1)S(1)}, u32[]{:S(2)}, u32[]{:S(2)}) collective-permute-start(bf16[512,512]{1,0:T(8,128)(2,1)S(1)} %collective-permute-done.3.refs_6_), channel_id=1, source_target_pairs={{0,4},{4,8},{8,12},{12,0},{1,5},{5,9},{9,13},{13,1},{2,6},{6,10},{... | collective-permute-start | bytes 1572872 | tf_op jit(solution)/shard_map/ppermute | solution.py:299
  24.3 5.6 %collective-permute-done.13.refs_2_ = bf16[128,1024]{1,0:T(8,128)(2,1)} collective-permute-done((bf16[128,1024]{1,0:T(8,128)(2,1)S(1)}, bf16[128,1024]{1,0:T(8,128)(2,1)}, u32[]{:S(2)}, u32[]{:S(2)}) %collective-permute-start.13) | collective-permute-done | bytes 262176 | tf_op jit(solution)/shard_map/ppermute | solution.py:293
  29.9 1.5 %collective-permute-start.6 = (bf16[512,512]{1,0:T(8,128)(2,1)S(1)}, bf16[512,512]{1,0:T(8,128)(2,1)S(1)}, u32[]{:S(2)}, u32[]{:S(2)}) collective-permute-start(bf16[512,512]{1,0:T(8,128)(2,1)S(1)} %collective-permute-done.3.refs_6_), channel_id=1, source_target_pairs={{0,16},{16,0},{1,17},{17,1},{2,18},{18,2},{3,19},{19,3},{4,20},{20... | collective-permute-start | bytes 1572872 | tf_op jit(solution)/shard_map/ppermute | solution.py:293
  31.5 9.2 %collective-permute-done.4.refs_7_ = bf16[512,512]{1,0:T(8,128)(2,1)S(1)} collective-permute-done((bf16[512,512]{1,0:T(8,128)(2,1)S(1)}, bf16[512,512]{1,0:T(8,128)(2,1)S(1)}, u32[]{:S(2)}, u32[]{:S(2)}) %collective-permute-start.4) | collective-permute-done | bytes 524320 | tf_op jit(solution)/shard_map/ppermute | solution.py:299
  40.7 2.3 %collective-permute-done.6.refs_9_ = bf16[512,512]{1,0:T(8,128)(2,1)S(1)} collective-permute-done((bf16[512,512]{1,0:T(8,128)(2,1)S(1)}, bf16[512,512]{1,0:T(8,128)(2,1)S(1)}, u32[]{:S(2)}, u32[]{:S(2)}) %collective-permute-start.6) | collective-permute-done | bytes 524320 | tf_op jit(solution)/shard_map/ppermute | solution.py:293
  43.0 1.6 %collective-permute-start.21 = (bf16[2,128,1024]{2,1,0:T(8,128)(2,1)S(1)}, bf16[2,128,1024]{2,1,0:T(8,128)(2,1)S(1)}, u32[]{:S(2)}, u32[]{:S(2)}) collective-permute-start(bf16[2,128,1024]{2,1,0:T(8,128)(2,1)S(1)} %collective-permute-done.17.refs_6_), channel_id=1, source_target_pairs={{0,4},{4,8},{8,12},{12,0},{1,5},{5,9},{9,13},{13,1},{2,6},{6,10},{... | collective-permute-start | bytes 1572872 | tf_op jit(solution)/shard_map/ppermute | solution.py:299
  44.6 1.5 %collective-permute-start.7 = (bf16[512,512]{1,0:T(8,128)(2,1)S(1)}, bf16[512,512]{1,0:T(8,128)(2,1)S(1)}, u32[]{:S(2)}, u32[]{:S(2)}) collective-permute-start(bf16[512,512]{1,0:T(8,128)(2,1)S(1)} %collective-permute-done.4.refs_7_), channel_id=1, source_target_pairs={{0,16},{16,0},{1,17},{17,1},{2,18},{18,2},{3,19},{19,3},{4,20},{20... | collective-permute-start | bytes 1572872 | tf_op jit(solution)/shard_map/ppermute | solution.py:293
  46.1 11.3 %collective-permute-done.5.refs_8_ = bf16[512,512]{1,0:T(8,128)(2,1)S(1)} collective-permute-done((bf16[512,512]{1,0:T(8,128)(2,1)S(1)}, bf16[512,512]{1,0:T(8,128)(2,1)S(1)}, u32[]{:S(2)}, u32[]{:S(2)}) %collective-permute-start.5) | collective-permute-done | bytes 524320 | tf_op jit(solution)/shard_map/ppermute | solution.py:299
  57.3 1.5 %collective-permute-start.8 = (bf16[512,512]{1,0:T(8,128)(2,1)S(1)}, bf16[512,512]{1,0:T(8,128)(2,1)S(1)}, u32[]{:S(2)}, u32[]{:S(2)}) collective-permute-start(bf16[512,512]{1,0:T(8,128)(2,1)S(1)} %collective-permute-done.5.refs_8_), channel_id=1, source_target_pairs={{0,16},{16,0},{1,17},{17,1},{2,18},{18,2},{3,19},{19,3},{4,20},{20... | collective-permute-start | bytes 1572872 | tf_op jit(solution)/shard_map/ppermute | solution.py:293
  58.9 7.9 %collective-permute-done.21.refs_10_ = bf16[2,128,1024]{2,1,0:T(8,128)(2,1)S(1)} collective-permute-done((bf16[2,128,1024]{2,1,0:T(8,128)(2,1)S(1)}, bf16[2,128,1024]{2,1,0:T(8,128)(2,1)S(1)}, u32[]{:S(2)}, u32[]{:S(2)}) %collective-permute-start.21) | collective-permute-done | bytes 524320 | tf_op jit(solution)/shard_map/ppermute | solution.py:299
  66.8 7.0 %collective-permute-done.2.refs_3_ = bf16[128,4096]{1,0:T(8,128)(2,1)S(1)} collective-permute-done((bf16[128,4096]{1,0:T(8,128)(2,1)}, bf16[128,4096]{1,0:T(8,128)(2,1)S(1)}, u32[]{:S(2)}, u32[]{:S(2)}) %collective-permute-start.2) | collective-permute-done | bytes 1048608 | tf_op jit(solution)/shard_map/ppermute | solution.py:296
  75.2 1.5 %collective-permute-start.18 = (bf16[2,128,1024]{2,1,0:T(8,128)(2,1)S(1)}, bf16[2,128,1024]{2,1,0:T(8,128)(2,1)S(1)}, u32[]{:S(2)}, u32[]{:S(2)}) collective-permute-start(bf16[2,128,1024]{2,1,0:T(8,128)(2,1)S(1)} %collective-permute-done.17.refs_6_), channel_id=1, source_target_pairs={{0,16},{16,0},{1,17},{17,1},{2,18},{18,2},{3,19},{19,3},{4,20},{20... | collective-permute-start | bytes 1572872 | tf_op jit(solution)/shard_map/ppermute | solution.py:293
  76.8 7.5 %project.1 = (f32[128,512]{1,0:T(8,128)}, f32[128,512]{1,0:T(8,128)}, f32[128,512]{1,0:T(8,128)}, f32[128,512]{1,0:T(8,128)}) custom-call(s32[5]{0:T(128)} %stack.32.idx, bf16[128,4096]{1,0:T(8,128)(2,1)} %get-tuple-element.13.refs_0_, bf16[128,4096]{1,0:T(8,128)(2,1)} %copy-done.2, bf16[128,4096]{1,0:T(8,128)(2,1)} %copy-done.3, ...), custom_call_target="tpu_custom_call" | custom-call | flops 2147483648 | bytes 16777216 | tf_op jit(solution)/shard_map/project/pallas_call | solution.py:104
  85.7 1.2 collective-permute-start.26
  87.0 1.7 %add.37 = f32[128,512]{1,0:T(8,128)} add(f32[128,512]{1,0:T(8,128)} %get-tuple-element.19, f32[128,512]{1,0:T(8,128)S(1)} %collective-permute-done.10) | non-fusion elementwise | flops 65536 | bytes 786432 | tf_op jit(solution)/shard_map/add | solution.py:330
  88.7 1.3 collective-permute-done.18.refs_7_
  90.8 1.5 %collective-permute-start.11 = (f32[128,512]{1,0:T(8,128)}, f32[128,512]{1,0:T(8,128)}, u32[]{:S(2)}, u32[]{:S(2)}) collective-permute-start(f32[128,512]{1,0:T(8,128)} %add.37), channel_id=1, source_target_pairs={{0,2},{2,0},{1,3},{3,1},{4,6},{6,4},{5,7},{7,5},{8,10},{10,8},{9,1... | collective-permute-start | bytes 786440 | tf_op jit(solution)/shard_map/ppermute | solution.py:293
  93.0 8.3 %collective-permute-done.22.refs_11_ = bf16[2,128,1024]{2,1,0:T(8,128)(2,1)S(1)} collective-permute-done((bf16[2,128,1024]{2,1,0:T(8,128)(2,1)S(1)}, bf16[2,128,1024]{2,1,0:T(8,128)(2,1)S(1)}, u32[]{:S(2)}, u32[]{:S(2)}) %collective-permute-start.22) | collective-permute-done | bytes 524320 | tf_op jit(solution)/shard_map/ppermute | solution.py:293
  101.8 9.9 %collective-permute-done.26.refs_15_ = bf16[2,128,1024]{2,1,0:T(8,128)(2,1)} collective-permute-done((bf16[2,128,1024]{2,1,0:T(8,128)(2,1)S(1)}, bf16[2,128,1024]{2,1,0:T(8,128)(2,1)}, u32[]{:S(2)}, u32[]{:S(2)}) %collective-permute-start.26) | collective-permute-done | bytes 524320 | tf_op jit(solution)/shard_map/ppermute | solution.py:293
  113.2 1.7 %add.36.mine = f32[128,512]{1,0:T(8,128)} add(f32[128,512]{1,0:T(8,128)} %get-tuple-element.17, f32[128,512]{1,0:T(8,128)S(1)} %collective-permute-done.9) | non-fusion elementwise | flops 65536 | bytes 786432 | tf_op jit(solution)/shard_map/add | solution.py:332
  114.9 8.1 %attend.1.att = bf16[128,256]{1,0:T(8,128)(2,1)} custom-call(s32[5]{0:T(128)} %stack.32.idx, f32[128,512]{1,0:T(8,128)} %add.36.mine, f32[128,512]{1,0:T(8,128)} %collective-permute-done.11.other, f32[128,128]{1,0:T(8,128)} %get-tuple-element.28.cos, f32[128,128]{1,0:T(8,128)} %get-tuple-element.29.sin, bf16[1,8192,256]{2,1,0:T(8,128)(2,1)} %cache.1), custom_call_target="tpu_custom_call" | custom-call | flops 1073741824 | bytes 12582912 | tf_op jit(solution)/shard_map/attend/pallas_call | solution.py:180
  125.2 8.4 %output.1 = bf16[128,16384]{1,0:T(8,128)(2,1)} custom-call(s32[5]{0:T(128)} %stack.32.idx, bf16[128,256]{1,0:T(8,128)(2,1)} %attend.1.att, bf16[128,16384]{1,0:T(8,128)(2,1)} %tok.3, bf16[256,1024]{1,0:T(8,128)(2,1)} %refs_0_.1, bf16[128,1024]{1,0:T(8,128)(2,1)} %copy-done.1, bf16[128,1024]{1,0:T(8,128)(2,1)} %collective-permute-done.13.refs_2_, ...), custom_call_target="tpu_custom_call" | custom-call | flops 1073741824 | bytes 16777216 | tf_op jit(solution)/shard_map/output/pallas_call | solution.py:260
  (88 shorter events, 8.6 us)
Async XLA Ops:
  0.0 58.9 %copy-start = (bf16[256,1024]{1,0:T(8,128)(2,1)S(1)}, bf16[256,1024]{1,0:T(8,128)(2,1)}, u32[]{:S(2)}) copy-start(bf16[256,1024]{1,0:T(8,128)(2,1)} %refs_0_.1) | copy-start | bytes 1572868
  1.2 21.0 %collective-permute-start.3 = (bf16[512,512]{1,0:T(8,128)(2,1)S(1)}, bf16[512,512]{1,0:T(8,128)(2,1)S(1)}, u32[]{:S(2)}, u32[]{:S(2)}) collective-permute-start(bf16[512,512]{1,0:T(8,128)(2,1)S(1)} %pad_maximum_fusion), channel_id=1, source_target_pairs={{0,4},{4,8},{8,12},{12,0},{1,5},{5,9},{9,13},{13,1},{2,6},{6,10},{... | collective-permute-start | bytes 1572872 | tf_op jit(solution)/shard_map/ppermute | solution.py:299
  5.3 7.8 %collective-permute-start.12 = (bf16[128,1024]{1,0:T(8,128)(2,1)S(1)}, bf16[128,1024]{1,0:T(8,128)(2,1)S(1)}, u32[]{:S(2)}, u32[]{:S(2)}) collective-permute-start(bf16[128,1024]{1,0:T(8,128)(2,1)S(1)} %get-tuple-element.22), channel_id=1, source_target_pairs={{0,2},{2,0},{1,3},{3,1},{4,6},{6,4},{5,7},{7,5},{8,10},{10,8},{9,1... | collective-permute-start | bytes 786440 | tf_op jit(solution)/shard_map/ppermute | solution.py:293
  13.1 71.1 %copy-start.1 = (bf16[128,1024]{1,0:T(8,128)(2,1)}, bf16[128,1024]{1,0:T(8,128)(2,1)S(1)}, u32[]{:S(2)}) copy-start(bf16[128,1024]{1,0:T(8,128)(2,1)S(1)} %collective-permute-done.12.refs_1_) | copy-start | bytes 786436
  13.2 18.2 %collective-permute-start.17 = (bf16[2,128,1024]{2,1,0:T(8,128)(2,1)S(1)}, bf16[2,128,1024]{2,1,0:T(8,128)(2,1)S(1)}, u32[]{:S(2)}, u32[]{:S(2)}) collective-permute-start(bf16[2,128,1024]{2,1,0:T(8,128)(2,1)S(1)} %pad_maximum_fusion.1), channel_id=1, source_target_pairs={{0,4},{4,8},{8,12},{12,0},{1,5},{5,9},{9,13},{13,1},{2,6},{6,10},{... | collective-permute-start | bytes 1572872 | tf_op jit(solution)/shard_map/ppermute | solution.py:299
  20.6 23.9 %collective-permute-start = (bf16[128,4096]{1,0:T(8,128)(2,1)}, bf16[128,4096]{1,0:T(8,128)(2,1)S(1)}, u32[]{:S(2)}, u32[]{:S(2)}) collective-permute-start(bf16[128,4096]{1,0:T(8,128)(2,1)} %get-tuple-element.14), channel_id=1, source_target_pairs={{0,1},{1,0},{2,3},{3,2},{4,5},{5,4},{6,7},{7,6},{8,9},{9,8},{10,11... | collective-permute-start | bytes 3145736 | tf_op jit(solution)/shard_map/ppermute | solution.py:293
  20.6 9.3 %collective-permute-start.13 = (bf16[128,1024]{1,0:T(8,128)(2,1)S(1)}, bf16[128,1024]{1,0:T(8,128)(2,1)}, u32[]{:S(2)}, u32[]{:S(2)}) collective-permute-start(bf16[128,1024]{1,0:T(8,128)(2,1)S(1)} %get-tuple-element.21), channel_id=1, source_target_pairs={{0,2},{2,0},{1,3},{3,1},{4,6},{6,4},{5,7},{7,5},{8,10},{10,8},{9,1... | collective-permute-start | bytes 786440 | tf_op jit(solution)/shard_map/ppermute | solution.py:293
  22.2 18.5 %collective-permute-start.4 = (bf16[512,512]{1,0:T(8,128)(2,1)S(1)}, bf16[512,512]{1,0:T(8,128)(2,1)S(1)}, u32[]{:S(2)}, u32[]{:S(2)}) collective-permute-start(bf16[512,512]{1,0:T(8,128)(2,1)S(1)} %collective-permute-done.3.refs_6_), channel_id=1, source_target_pairs={{0,4},{4,8},{8,12},{12,0},{1,5},{5,9},{9,13},{13,1},{2,6},{6,10},{... | collective-permute-start | bytes 1572872 | tf_op jit(solution)/shard_map/ppermute | solution.py:299
  23.8 35.1 %collective-permute-start.1 = (bf16[128,4096]{1,0:T(8,128)(2,1)}, bf16[128,4096]{1,0:T(8,128)(2,1)S(1)}, u32[]{:S(2)}, u32[]{:S(2)}) collective-permute-start(bf16[128,4096]{1,0:T(8,128)(2,1)} %get-tuple-element.15), channel_id=1, source_target_pairs={{0,2},{2,0},{1,3},{3,1},{4,6},{6,4},{5,7},{7,5},{8,10},{10,8},{9,1... | collective-permute-start | bytes 3145736 | tf_op jit(solution)/shard_map/ppermute | solution.py:293
  29.9 13.1 %collective-permute-start.6 = (bf16[512,512]{1,0:T(8,128)(2,1)S(1)}, bf16[512,512]{1,0:T(8,128)(2,1)S(1)}, u32[]{:S(2)}, u32[]{:S(2)}) collective-permute-start(bf16[512,512]{1,0:T(8,128)(2,1)S(1)} %collective-permute-done.3.refs_6_), channel_id=1, source_target_pairs={{0,16},{16,0},{1,17},{17,1},{2,18},{18,2},{3,19},{19,3},{4,20},{20... | collective-permute-start | bytes 1572872 | tf_op jit(solution)/shard_map/ppermute | solution.py:293
  31.4 91.7 %copy-start.5 = (bf16[2,128,1024]{2,1,0:T(8,128)(2,1)}, bf16[2,128,1024]{2,1,0:T(8,128)(2,1)S(1)}, u32[]{:S(2)}) copy-start(bf16[2,128,1024]{2,1,0:T(8,128)(2,1)S(1)} %collective-permute-done.17.refs_6_) | copy-start | bytes 1572868
  31.4 42.4 %collective-permute-start.2 = (bf16[128,4096]{1,0:T(8,128)(2,1)}, bf16[128,4096]{1,0:T(8,128)(2,1)S(1)}, u32[]{:S(2)}, u32[]{:S(2)}) collective-permute-start(bf16[128,4096]{1,0:T(8,128)(2,1)} %get-tuple-element.16), channel_id=1, source_target_pairs={{0,3},{1,2},{2,1},{3,0},{4,7},{5,6},{6,5},{7,4},{8,11},{9,10},{10,... | collective-permute-start | bytes 3145736 | tf_op jit(solution)/shard_map/ppermute | solution.py:296
  40.7 16.7 %collective-permute-start.5 = (bf16[512,512]{1,0:T(8,128)(2,1)S(1)}, bf16[512,512]{1,0:T(8,128)(2,1)S(1)}, u32[]{:S(2)}, u32[]{:S(2)}) collective-permute-start(bf16[512,512]{1,0:T(8,128)(2,1)S(1)} %collective-permute-done.4.refs_7_), channel_id=1, source_target_pairs={{0,4},{4,8},{8,12},{12,0},{1,5},{5,9},{9,13},{13,1},{2,6},{6,10},{... | collective-permute-start | bytes 1572872 | tf_op jit(solution)/shard_map/ppermute | solution.py:299
  43.0 23.8 %collective-permute-start.21 = (bf16[2,128,1024]{2,1,0:T(8,128)(2,1)S(1)}, bf16[2,128,1024]{2,1,0:T(8,128)(2,1)S(1)}, u32[]{:S(2)}, u32[]{:S(2)}) collective-permute-start(bf16[2,128,1024]{2,1,0:T(8,128)(2,1)S(1)} %collective-permute-done.17.refs_6_), channel_id=1, source_target_pairs={{0,4},{4,8},{8,12},{12,0},{1,5},{5,9},{9,13},{13,1},{2,6},{6,10},{... | collective-permute-start | bytes 1572872 | tf_op jit(solution)/shard_map/ppermute | solution.py:299
  44.6 29.9 %collective-permute-start.7 = (bf16[512,512]{1,0:T(8,128)(2,1)S(1)}, bf16[512,512]{1,0:T(8,128)(2,1)S(1)}, u32[]{:S(2)}, u32[]{:S(2)}) collective-permute-start(bf16[512,512]{1,0:T(8,128)(2,1)S(1)} %collective-permute-done.4.refs_7_), channel_id=1, source_target_pairs={{0,16},{16,0},{1,17},{17,1},{2,18},{18,2},{3,19},{19,3},{4,20},{20... | collective-permute-start | bytes 1572872 | tf_op jit(solution)/shard_map/ppermute | solution.py:293
  57.3 17.2 %collective-permute-start.8 = (bf16[512,512]{1,0:T(8,128)(2,1)S(1)}, bf16[512,512]{1,0:T(8,128)(2,1)S(1)}, u32[]{:S(2)}, u32[]{:S(2)}) collective-permute-start(bf16[512,512]{1,0:T(8,128)(2,1)S(1)} %collective-permute-done.5.refs_8_), channel_id=1, source_target_pairs={{0,16},{16,0},{1,17},{17,1},{2,18},{18,2},{3,19},{19,3},{4,20},{20... | collective-permute-start | bytes 1572872 | tf_op jit(solution)/shard_map/ppermute | solution.py:293
  58.9 26.0 %collective-permute-start.14 = (bf16[256,1024]{1,0:T(8,128)(2,1)S(1)}, bf16[256,1024]{1,0:T(8,128)(2,1)S(1)}, u32[]{:S(2)}, u32[]{:S(2)}) collective-permute-start(bf16[256,1024]{1,0:T(8,128)(2,1)S(1)} %copy-done), channel_id=1, source_target_pairs={{0,1},{1,0},{2,3},{3,2},{4,5},{5,4},{6,7},{7,6},{8,9},{9,8},{10,11... | collective-permute-start | bytes 1572872 | tf_op jit(solution)/shard_map/ppermute | solution.py:293
  66.8 18.8 %collective-permute-start.25 = (bf16[2,128,1024]{2,1,0:T(8,128)(2,1)S(1)}, bf16[2,128,1024]{2,1,0:T(8,128)(2,1)S(1)}, u32[]{:S(2)}, u32[]{:S(2)}) collective-permute-start(bf16[2,128,1024]{2,1,0:T(8,128)(2,1)S(1)} %collective-permute-done.21.refs_10_), channel_id=1, source_target_pairs={{0,4},{4,8},{8,12},{12,0},{1,5},{5,9},{9,13},{13,1},{2,6},{6,10},{... | collective-permute-start | bytes 1572872 | tf_op jit(solution)/shard_map/ppermute | solution.py:299
  73.9 10.4 %collective-permute-start.15 = (bf16[128,1024]{1,0:T(8,128)(2,1)S(1)}, bf16[128,1024]{1,0:T(8,128)(2,1)}, u32[]{:S(2)}, u32[]{:S(2)}) collective-permute-start(bf16[128,1024]{1,0:T(8,128)(2,1)S(1)} %collective-permute-done.12.refs_1_), channel_id=1, source_target_pairs={{0,1},{1,0},{2,3},{3,2},{4,5},{5,4},{6,7},{7,6},{8,9},{9,8},{10,11... | collective-permute-start | bytes 786440 | tf_op jit(solution)/shard_map/ppermute | solution.py:293
  74.4 9.9 %collective-permute-start.16 = (bf16[128,1024]{1,0:T(8,128)(2,1)}, bf16[128,1024]{1,0:T(8,128)(2,1)}, u32[]{:S(2)}, u32[]{:S(2)}) collective-permute-start(bf16[128,1024]{1,0:T(8,128)(2,1)} %collective-permute-done.13.refs_2_), channel_id=1, source_target_pairs={{0,1},{1,0},{2,3},{3,2},{4,5},{5,4},{6,7},{7,6},{8,9},{9,8},{10,11... | collective-permute-start | bytes 786440 | tf_op jit(solution)/shard_map/ppermute | solution.py:293
  75.2 14.8 %collective-permute-start.18 = (bf16[2,128,1024]{2,1,0:T(8,128)(2,1)S(1)}, bf16[2,128,1024]{2,1,0:T(8,128)(2,1)S(1)}, u32[]{:S(2)}, u32[]{:S(2)}) collective-permute-start(bf16[2,128,1024]{2,1,0:T(8,128)(2,1)S(1)} %collective-permute-done.17.refs_6_), channel_id=1, source_target_pairs={{0,16},{16,0},{1,17},{17,1},{2,18},{18,2},{3,19},{19,3},{4,20},{20... | collective-permute-start | bytes 1572872 | tf_op jit(solution)/shard_map/ppermute | solution.py:293
  84.3 8.6 %collective-permute-start.19 = (bf16[2,128,1024]{2,1,0:T(8,128)(2,1)S(1)}, bf16[2,128,1024]{2,1,0:T(8,128)(2,1)S(1)}, u32[]{:S(2)}, u32[]{:S(2)}) collective-permute-start(bf16[2,128,1024]{2,1,0:T(8,128)(2,1)S(1)} %collective-permute-done.17.refs_6_), channel_id=1, source_target_pairs={{0,1},{1,0},{2,3},{3,2},{4,5},{5,4},{6,7},{7,6},{8,9},{9,8},{10,11... | collective-permute-start | bytes 1572872 | tf_op jit(solution)/shard_map/ppermute | solution.py:293
  84.4 2.5 %collective-permute-start.10 = (f32[128,512]{1,0:T(8,128)}, f32[128,512]{1,0:T(8,128)S(1)}, u32[]{:S(2)}, u32[]{:S(2)}) collective-permute-start(f32[128,512]{1,0:T(8,128)} %get-tuple-element.20), channel_id=1, source_target_pairs={{0,1},{1,0},{2,3},{3,2},{4,5},{5,4},{6,7},{7,6},{8,9},{9,8},{10,11... | collective-permute-start | bytes 786440 | tf_op jit(solution)/shard_map/ppermute | solution.py:293
  84.9 16.4 %collective-permute-start.22 = (bf16[2,128,1024]{2,1,0:T(8,128)(2,1)S(1)}, bf16[2,128,1024]{2,1,0:T(8,128)(2,1)S(1)}, u32[]{:S(2)}, u32[]{:S(2)}) collective-permute-start(bf16[2,128,1024]{2,1,0:T(8,128)(2,1)S(1)} %collective-permute-done.21.refs_10_), channel_id=1, source_target_pairs={{0,16},{16,0},{1,17},{17,1},{2,18},{18,2},{3,19},{19,3},{4,20},{20... | collective-permute-start | bytes 1572872 | tf_op jit(solution)/shard_map/ppermute | solution.py:293
  85.7 26.0 %collective-permute-start.26 = (bf16[2,128,1024]{2,1,0:T(8,128)(2,1)S(1)}, bf16[2,128,1024]{2,1,0:T(8,128)(2,1)}, u32[]{:S(2)}, u32[]{:S(2)}) collective-permute-start(bf16[2,128,1024]{2,1,0:T(8,128)(2,1)S(1)} %collective-permute-done.25.refs_14_), channel_id=1, source_target_pairs={{0,16},{16,0},{1,17},{17,1},{2,18},{18,2},{3,19},{19,3},{4,20},{20... | collective-permute-start | bytes 1572872 | tf_op jit(solution)/shard_map/ppermute | solution.py:293
  86.9 14.3 %collective-permute-start.9 = (f32[128,512]{1,0:T(8,128)}, f32[128,512]{1,0:T(8,128)S(1)}, u32[]{:S(2)}, u32[]{:S(2)}) collective-permute-start(f32[128,512]{1,0:T(8,128)} %get-tuple-element.18), channel_id=1, source_target_pairs={{0,1},{1,0},{2,3},{3,2},{4,5},{5,4},{6,7},{7,6},{8,9},{9,8},{10,11... | collective-permute-start | bytes 786440 | tf_op jit(solution)/shard_map/ppermute | solution.py:293
  90.8 20.9 %collective-permute-start.11 = (f32[128,512]{1,0:T(8,128)}, f32[128,512]{1,0:T(8,128)}, u32[]{:S(2)}, u32[]{:S(2)}) collective-permute-start(f32[128,512]{1,0:T(8,128)} %add.37), channel_id=1, source_target_pairs={{0,2},{2,0},{1,3},{3,1},{4,6},{6,4},{5,7},{7,5},{8,10},{10,8},{9,1... | collective-permute-start | bytes 786440 | tf_op jit(solution)/shard_map/ppermute | solution.py:293
  92.9 30.1 %collective-permute-start.23 = (bf16[2,128,1024]{2,1,0:T(8,128)(2,1)S(1)}, bf16[2,128,1024]{2,1,0:T(8,128)(2,1)S(1)}, u32[]{:S(2)}, u32[]{:S(2)}) collective-permute-start(bf16[2,128,1024]{2,1,0:T(8,128)(2,1)S(1)} %collective-permute-done.21.refs_10_), channel_id=1, source_target_pairs={{0,1},{1,0},{2,3},{3,2},{4,5},{5,4},{6,7},{7,6},{8,9},{9,8},{10,11... | collective-permute-start | bytes 1572872 | tf_op jit(solution)/shard_map/ppermute | solution.py:293
  101.2 21.8 %collective-permute-start.20 = (bf16[2,128,1024]{2,1,0:T(8,128)(2,1)}, bf16[2,128,1024]{2,1,0:T(8,128)(2,1)S(1)}, u32[]{:S(2)}, u32[]{:S(2)}) collective-permute-start(bf16[2,128,1024]{2,1,0:T(8,128)(2,1)} %copy-done.10), channel_id=1, source_target_pairs={{0,1},{1,0},{2,3},{3,2},{4,5},{5,4},{6,7},{7,6},{8,9},{9,8},{10,11... | collective-permute-start | bytes 1572872 | tf_op jit(solution)/shard_map/ppermute | solution.py:293
  101.2 21.8 %collective-permute-start.27 = (bf16[2,128,1024]{2,1,0:T(8,128)(2,1)S(1)}, bf16[2,128,1024]{2,1,0:T(8,128)(2,1)S(1)}, u32[]{:S(2)}, u32[]{:S(2)}) collective-permute-start(bf16[2,128,1024]{2,1,0:T(8,128)(2,1)S(1)} %collective-permute-done.25.refs_14_), channel_id=1, source_target_pairs={{0,1},{1,0},{2,3},{3,2},{4,5},{5,4},{6,7},{7,6},{8,9},{9,8},{10,11... | collective-permute-start | bytes 1572872 | tf_op jit(solution)/shard_map/ppermute | solution.py:293
  111.7 11.4 %collective-permute-start.24 = (bf16[2,128,1024]{2,1,0:T(8,128)(2,1)S(1)}, bf16[2,128,1024]{2,1,0:T(8,128)(2,1)S(1)}, u32[]{:S(2)}, u32[]{:S(2)}) collective-permute-start(bf16[2,128,1024]{2,1,0:T(8,128)(2,1)S(1)} %collective-permute-done.22.refs_11_), channel_id=1, source_target_pairs={{0,1},{1,0},{2,3},{3,2},{4,5},{5,4},{6,7},{7,6},{8,9},{9,8},{10,11... | collective-permute-start | bytes 1572872 | tf_op jit(solution)/shard_map/ppermute | solution.py:293
  111.7 11.5 %collective-permute-start.28 = (bf16[2,128,1024]{2,1,0:T(8,128)(2,1)}, bf16[2,128,1024]{2,1,0:T(8,128)(2,1)S(1)}, u32[]{:S(2)}, u32[]{:S(2)}) collective-permute-start(bf16[2,128,1024]{2,1,0:T(8,128)(2,1)} %collective-permute-done.26.refs_15_), channel_id=1, source_target_pairs={{0,1},{1,0},{2,3},{3,2},{4,5},{5,4},{6,7},{7,6},{8,9},{9,8},{10,11... | collective-permute-start | bytes 1572872 | tf_op jit(solution)/shard_map/ppermute | solution.py:293
  (20 other events, 386.9 us)

commit v2 on v1

v2 whole, which is shorter than its diff:
```python
import functools

import jax
import jax.numpy as jnp
from jax import lax
from jax.experimental import pallas as pl
from jax.experimental.pallas import tpu as pltpu
from jax.sharding import Mesh, PartitionSpec as P

F32 = jnp.float32
BF16 = jnp.bfloat16
AXES = ("y", "z", "r", "x", "c")
VMEM_LIMIT = 56 * 1024 * 1024


def params():
    return pltpu.CompilerParams(vmem_limit_bytes=VMEM_LIMIT)


def norm_kernel(tok, gain, *outs, nz, nr, bs):
    z, x, c = (lax.axis_index(a) for a in ("z", "x", "c"))
    width = tok.shape[1]
    step = 1024
    for r0 in range(0, tok.shape[0], 16):
        rows = pl.ds(r0, 16)
        acc = jnp.zeros((16, step), F32)
        for j in range(width // step):
            v = tok[rows, pl.ds(j * step, step)].astype(F32)
            acc = acc + v * v
        inv = lax.rsqrt(jnp.sum(acc, axis=1, keepdims=True) * (1.0 / width) + 1e-05)
        for k, out in enumerate(outs):
            part = (x ^ (k // 2)) * 2 + (c ^ (k % 2))
            for s in range(nz):
                zz = lax.rem(z - s + nz, nz)
                for r in range(nr):
                    cols = pl.ds(pl.multiple_of(((zz * nr + r) * 4 + part) * bs, bs), bs)
                    v = tok[rows, cols].astype(F32) * inv * gain[:, cols]
                    out[rows, pl.ds((s * nr + r) * bs, bs)] = v.astype(BF16)


def normalise(tokens, gain, nz, nr, bs):
    rows, width = tokens.shape
    block = 32
    quarter = width // 4
    return pl.pallas_call(
        functools.partial(norm_kernel, nz=nz, nr=nr, bs=bs),
        grid=(rows // block,),
        in_specs=[pl.BlockSpec((block, width), lambda i: (i, 0)), pl.BlockSpec((1, width), lambda i: (0, 0))],
        out_specs=[pl.BlockSpec((block, quarter), lambda i: (i, 0))] * 4,
        out_shape=[jax.ShapeDtypeStruct((rows, quarter), BF16)] * 4,
        compiler_params=params(),
        cost_estimate=pl.CostEstimate(flops=8 * rows * width, bytes_accessed=4 * rows * width, transcendentals=0),
        name="norm",
    )(tokens, gain.reshape(1, width))


def project_kernel(*refs, halves):
    toks, refs = refs[:4], refs[4:]
    count = sum(pieces for _, _, pieces in halves)
    weights, refs = list(refs[:count]), refs[count:]
    (mine, core, square), (tbuf, wbuf, tsem, wsem) = refs[:3], refs[3:]
    outs = (mine, core.at[0], square, core.at[1])
    y = lax.axis_index("y")
    rows = mine.shape[0]
    steps, both, width = wbuf.shape
    half = both // 2
    tcopies, wcopies = [], [[] for _ in range(steps)]
    for step in range(steps):
        cols = pl.ds(step * both, both)
        tcopies.append(
            [
                pltpu.make_async_copy(
                    toks[i].at[:, cols], tbuf.at[pl.ds(i * rows, rows), cols], tsem.at[step, i]
                )
                for i in range(4)
            ]
        )
    for n, (step, far, pieces) in enumerate(halves):
        if far is None:
            span = pl.ds(0, both)
        else:
            span = pl.ds(pl.multiple_of((1 - y if far else y) * half, half), half)
        for j in range(pieces):
            size = width // pieces
            to = wbuf.at[step, span, pl.ds(j * size, size)]
            wcopies[step].append(pltpu.make_async_copy(weights.pop(0), to, wsem.at[n, j]))
    for step in range(steps):
        for cp in tcopies[step] + wcopies[step]:
            cp.start()
    for step in range(steps):
        for cp in tcopies[step] + wcopies[step]:
            cp.wait()
        v = jnp.dot(tbuf[:, step * both : (step + 1) * both], wbuf[step], preferred_element_type=F32)
        for i in range(4):
            part = v[i * rows : (i + 1) * rows]
            if step:
                outs[i][...] += part
            else:
                outs[i][...] = part


def project(toks, weights, halves):
    rows, depth = toks[0].shape
    steps = 1 + max(step for step, _, _ in halves)
    both = depth // steps
    width = sum(w.shape[1] for w in weights[0])
    anywhere = pl.BlockSpec(memory_space=pl.ANY)
    vmem = pl.BlockSpec(memory_space=pltpu.VMEM)
    flat = [w for pair in weights for w in pair]
    shapes = [(rows, width), (2, rows, width), (rows, width)]
    return pl.pallas_call(
        functools.partial(project_kernel, halves=halves),
        in_specs=[anywhere] * (4 + len(flat)),
        out_specs=[vmem] * 3,
        out_shape=[jax.ShapeDtypeStruct(shape, F32) for shape in shapes],
        scratch_shapes=[
            pltpu.VMEM((4 * rows, depth), BF16),
            pltpu.VMEM((steps, both, width), BF16),
            pltpu.SemaphoreType.DMA((steps, 4)),
            pltpu.SemaphoreType.DMA((len(halves), 2)),
        ],
        compiler_params=params(),
        cost_estimate=pl.CostEstimate(
            flops=2 * 4 * rows * depth * width, bytes_accessed=20 * 1024 * 1024, transcendentals=0
        ),
        name="project",
    )(*toks, *flat)


def prompt_index(nr):
    z, r, x, c = (lax.axis_index(a) for a in ("z", "r", "x", "c"))
    return ((z * nr + r) * 2 + x) * 2 + c


def attend_kernel(lens, mine, core, other, cos, sin, cache, out, kvbuf, sem, *, heads, head, nr):
    length = lens[prompt_index(nr)]
    slots = kvbuf.shape[0]
    rows = mine.shape[0]
    chunk = 1024
    copies = [
        pltpu.make_async_copy(
            cache.at[0, pl.ds(i * chunk, chunk)], kvbuf.at[pl.ds(i * chunk, chunk)], sem.at[i]
        )
        for i in range(slots // chunk)
    ]
    for cp in copies:
        cp.start()
    total = (mine[...] + core[0]) + other[...]

    def turn(v):
        return (v * cos[...] + pltpu.roll(v, head // 2, 1) * sin[...]).astype(BF16)

    q = jnp.concatenate([turn(total[:, i * head : (i + 1) * head]) for i in range(heads)], axis=0)
    k_new = turn(total[:, heads * head : (heads + 1) * head])
    v_new = total[:, (heads + 1) * head :].astype(BF16)
    scale = (head ** -0.5) * 1.4426950408889634

    def scores(keys):
        return lax.dot_general(q, keys, (((1,), (1,)), ((), ())), preferred_element_type=F32)

    s = scores(k_new)
    row = lax.broadcasted_iota(jnp.int32, s.shape, 0) % rows
    col = lax.broadcasted_iota(jnp.int32, s.shape, 1)
    s = jnp.where(col <= row, s, -1e30)
    top = jnp.max(s, axis=1, keepdims=True)
    p = jnp.exp2((s - top) * scale)
    total_p = jnp.sum(p, axis=1, keepdims=True)
    acc = jnp.dot(p.astype(BF16), v_new, preferred_element_type=F32)
    for i, cp in enumerate(copies):
        cp.wait()
        s = scores(kvbuf[pl.ds(i * chunk, chunk), :head])
        col = lax.broadcasted_iota(jnp.int32, (1, chunk), 1) + i * chunk
        s = jnp.where(col < length, s, -1e30)
        new_top = jnp.maximum(top, jnp.max(s, axis=1, keepdims=True))
        p = jnp.exp2((s - new_top) * scale)
        fade = jnp.exp2((top - new_top) * scale)
        top = new_top
        total_p = total_p * fade + jnp.sum(p, axis=1, keepdims=True)
        acc = acc * fade + jnp.dot(
            p.astype(BF16), kvbuf[pl.ds(i * chunk, chunk), head:], preferred_element_type=F32
        )
    acc = (acc / total_p).astype(BF16)
    for i in range(heads):
        out[:, i * head : (i + 1) * head] = acc[i * rows : (i + 1) * rows]


def attend(lens, mine, core, other, cos, sin, cache, heads, head, nr):
    vmem = pl.BlockSpec(memory_space=pltpu.VMEM)
    rows = mine.shape[0]
    slots = cache.shape[1]
    return pl.pallas_call(
        functools.partial(attend_kernel, heads=heads, head=head, nr=nr),
        in_specs=[pl.BlockSpec(memory_space=pltpu.SMEM)] + [vmem] * 5 + [pl.BlockSpec(memory_space=pl.ANY)],
        out_specs=vmem,
        out_shape=jax.ShapeDtypeStruct((rows, heads * head), BF16),
        scratch_shapes=[pltpu.VMEM(cache.shape[1:], BF16), pltpu.SemaphoreType.DMA((slots // 1024,))],
        compiler_params=params(),
        cost_estimate=pl.CostEstimate(
            flops=4 * rows * heads * head * slots, bytes_accessed=28 * 1024 * 1024, transcendentals=rows * heads * slots
        ),
        name="attend",
    )(lens, mine, core, other, cos, sin, cache)


def out_kernel(att, tok, *refs, plan, nz, nr, bs, carry):
    n = len(refs) - 6 - 1 - carry
    weights, out = refs[:n], refs[n + carry]
    refs = refs[carry:]
    wbuf, tbuf, obuf, wsem, tsem, osem = refs[n + 1 :]
    z, x, c, y = (lax.axis_index(a) for a in ("z", "x", "c", "y"))
    half = att.shape[1] // 2
    rows = att.shape[0]
    flip = y == 1
    low, high = att[:, :half], att[:, half:]
    left = jnp.concatenate([jnp.where(flip, high, low), jnp.where(flip, low, high)], axis=1)
    slots = wbuf.shape[0]

    def cols(s, dx, dc, r):
        zz = lax.rem(z - s + nz, nz)
        return pl.ds(pl.multiple_of(((zz * nr + r) * 4 + (x ^ dx) * 2 + (c ^ dc)) * bs, bs), bs)

    def load(b):
        (s, dx, dc), halves = plan[b]
        slot = b % slots
        cps = []
        for h, (ref, lead, pos) in enumerate(halves):
            src = weights[ref] if lead is None else weights[ref].at[lead]
            if pos is not None:
                side = y if pos == 0 else 1 - y
                src = src.at[pl.ds(pl.multiple_of(side * half, half), half)]
            cps.append(pltpu.make_async_copy(src, wbuf.at[slot, pl.ds(h * half, half)], wsem.at[slot, h]))
        for r in range(nr):
            cps.append(
                pltpu.make_async_copy(tok.at[:, cols(s, dx, dc, r)], tbuf.at[slot, :, pl.ds(r * bs, bs)], tsem.at[slot, r])
            )
        return cps

    def store(b):
        (s, dx, dc), _ = plan[b]
        slot = b % slots
        return [
            pltpu.make_async_copy(obuf.at[slot, :, pl.ds(r * bs, bs)], out.at[:, cols(s, dx, dc, r)], osem.at[slot, r])
            for r in range(nr)
        ]

    for b in range(min(slots, len(plan))):
        for cp in load(b):
            cp.start()
    for b in range(len(plan)):
        slot = b % slots
        for cp in load(b):
            cp.wait()
        if b >= slots:
            for cp in store(b - slots):
                cp.wait()
        v = jnp.dot(left, wbuf[slot], preferred_element_type=F32)
        obuf[slot] = (tbuf[slot].astype(F32) + v).astype(BF16)
        for cp in store(b):
            cp.start()
        if b + slots < len(plan):
            for cp in load(b + slots):
                cp.start()
    for b in range(max(0, len(plan) - slots), len(plan)):
        for cp in store(b):
            cp.wait()


def output(att, tokens, weights, plan, nz, nr, bs, base=None):
    anywhere = pl.BlockSpec(memory_space=pl.ANY)
    slots = 6
    rows, width = tokens.shape
    return pl.pallas_call(
        functools.partial(out_kernel, plan=plan, nz=nz, nr=nr, bs=bs, carry=int(base is not None)),
        in_specs=[pl.BlockSpec(memory_space=pltpu.VMEM)]
        + [anywhere] * (1 + len(weights) + (base is not None)),
        input_output_aliases={} if base is None else {2 + len(weights): 0},
        out_specs=anywhere,
        out_shape=jax.ShapeDtypeStruct(tokens.shape, BF16),
        scratch_shapes=[
            pltpu.VMEM((slots, att.shape[1], nr * bs), BF16),
            pltpu.VMEM((slots, rows, nr * bs), BF16),
            pltpu.VMEM((slots, rows, nr * bs), BF16),
            pltpu.SemaphoreType.DMA((slots, 2)),
            pltpu.SemaphoreType.DMA((slots, nr)),
            pltpu.SemaphoreType.DMA((slots, nr)),
        ],
        compiler_params=params(),
        cost_estimate=pl.CostEstimate(
            flops=2 * rows * nr * bs * len(plan) * att.shape[1],
            bytes_accessed=(att.shape[1] + 2 * rows) * 2 * nr * bs * len(plan),
            transcendentals=0,
        ),
        name="output",
    )(att, tokens, *weights, *(() if base is None else (base,)))


def body(tokens, gain, w_query, w_key_value, w_out, cache_kv, cached_len, *, nz, nr):
    rows = tokens.shape[0]
    head = w_key_value.shape[1] // 2
    heads = w_query.shape[1] // head
    bs = w_query.shape[0]
    y = lax.axis_index("y")
    length = jnp.sum(
        jnp.where(jnp.arange(cached_len.shape[0], dtype=jnp.int32) == prompt_index(nr), cached_len, 0)
    )

    def swap(v, axis):
        return lax.ppermute(v, axis, [(0, 1), (1, 0)])

    def ring(v):
        return lax.ppermute(v, "z", [(i, (i + 1) % nz) for i in range(nz)])

    own_q, own_kv, own_o = w_query, w_key_value, w_out
    if nr > 1:
        own_q = lax.all_gather(own_q, "r", axis=0, tiled=True)
        own_kv = lax.all_gather(own_kv, "r", axis=0, tiled=True)
        own_o = lax.all_gather(own_o, "r", axis=1, tiled=True)
    half = own_q.shape[0] // 2
    ohalf = own_o.shape[0] // 2

    def tie(v, *after):
        return lax.optimization_barrier((v,) + after)[0]

    w_mine = jnp.concatenate([lax.dynamic_slice_in_dim(w, y * half, half) for w in (own_q, own_kv)], axis=1)
    o_mine = lax.dynamic_slice_in_dim(own_o, y * ohalf, ohalf)
    o_else = lax.dynamic_slice_in_dim(own_o, (1 - y) * ohalf, ohalf)
    gain = tie(gain, w_mine, o_mine)
    with jax.named_scope("Ox"):
        o_mine_x = swap(o_mine, "x")
    toks = normalise(tokens, gain, nz, nr, bs)

    def step_z(v, name, *after):
        with jax.named_scope("Z" + name):
            return ring(tie(v, *after) if after else v)

    def step_y(v, name, *after):
        with jax.named_scope("Y" + name):
            return swap(tie(v, *after) if after else v, "y")

    w_near, w_far = [None], [None]
    with jax.named_scope("Tc"):
        core_toks = swap(toks[1], "c")
    with jax.named_scope("Tx"):
        across = swap(tie(toks[2], o_mine_x), "x")
    with jax.named_scope("Txc"):
        corner = lax.ppermute(toks[3], ("x", "c"), [(i, i ^ 3) for i in range(4)])
    with jax.named_scope("Oc0"):
        own_o_c = swap(own_o, "c")
        o_mine_x_c = swap(o_mine_x, "c")
    v = w_mine
    for s in range(1, nz):
        after = [w_far[s - 2], core_toks, across, own_o_c, o_mine_x_c] if s == 3 else []
        v = step_z(v, f"w{s}", *after)
        w_near.append(v)
        w_far.append(step_y(v, f"w{s}", *(w_far[2:] if s == 3 else [])))

    def weights_of(steps):
        weights, halves = [], []
        for s in steps:
            if s == 0:
                weights.append((own_q, own_kv))
                halves.append((0, None, 2))
                continue
            for side, held in enumerate((w_near, w_far)):
                weights.append((held[s],))
                halves.append((s - steps[0], side, 1))
        return weights, halves

    with jax.named_scope("Oxe"):
        o_else_x = swap(tie(o_else, w_near[3]), "x")
    o_near, o_far = [None], [None]
    o_near.append(step_z(jnp.stack([o_mine, tie(o_mine_x, toks[0])]), "o1", across))
    held = [toks[0], core_toks, across, tie(corner, o_near[1])]
    parts = project(held, *weights_of(range(nz)))
    o_near.append(step_z(o_near[1], "o2"))
    o_far.append(step_y(o_near[1], "o1"))
    with jax.named_scope("Pc"):
        from_c = swap(tie(parts[1], o_else_x), "c")
    total = parts[2] + tie(from_c, o_near[2], o_far[1])[1]
    with jax.named_scope("Px"):
        other = swap(total, "x")
    o_near.append(step_z(o_near[2], "o3", total))
    for s in range(2, nz):
        o_far.append(step_y(o_near[s], f"o{s}", total))
    with jax.named_scope("Oc1"):
        o_else_x_c = swap(tie(o_else_x, other), "c")
        near1_c = swap(tie(o_near[1], other), "c")
        far1_c = swap(tie(o_far[1], other), "c")

    positions = length.astype(F32) + jnp.arange(rows, dtype=F32)
    steps = jnp.arange(head // 2, dtype=F32) * (2.0 / head)
    freqs = jnp.exp(-jnp.log(jnp.float32(500000.0)) * steps)
    angles = positions[:, None] * freqs[None, :]
    cos, sin = jnp.cos(angles), jnp.sin(angles)
    att = attend(
        cached_len,
        parts[0],
        from_c,
        tie(other, o_near[3], o_far[2]),
        jnp.concatenate([cos, cos], axis=1),
        jnp.concatenate([-sin, sin], axis=1),
        cache_kv,
        heads,
        head,
        nr,
    )

    def over(v, dc, *after):
        if not dc:
            return v
        with jax.named_scope("Oc"):
            return swap(tie(v, *after), "c")

    def group(entries):
        weights, plan = [], []
        for place, halves in entries:
            spots = []
            for v, lead, pos in halves:
                at = [i for i, w in enumerate(weights) if w is v]
                if not at:
                    weights.append(v)
                    at = [len(weights) - 1]
                spots.append((at[0], lead, pos))
            plan.append((place, spots))
        return weights, plan

    def blocks(s, dc, near, far):
        return [((s, dx, dc), [(near, dx, None), (far, dx, None)]) for dx in range(2)]

    early, late = [], []
    for dc in range(2):
        own, mx, ex = ((own_o, o_mine_x, o_else_x), (own_o_c, o_mine_x_c, o_else_x_c))[dc]
        early.append(((0, 0, dc), [(own, None, 0), (own, None, 1)]))
        early.append(((0, 1, dc), [(mx, None, None), (ex, None, None)]))
    early += blocks(1, 0, o_near[1], o_far[1]) + blocks(1, 1, near1_c, far1_c) + blocks(2, 0, o_near[2], o_far[2])
    out = output(att, tokens, *group(early), nz, nr, bs)
    late += blocks(2, 1, over(o_near[2], 1, att), over(o_far[2], 1, att))
    for dc in range(2):
        late += blocks(3, dc, over(o_near[3], dc, att), over(o_far[3], dc, out))
    return output(att, tokens, *group(late), nz, nr, bs, out)


def solution(mesh):
    groups, blk = mesh.shape["groups"], mesh.shape["blk"]
    nz = 4
    nr = blk // (4 * nz)
    wide = Mesh(mesh.devices.reshape(groups, nz, nr, 2, 2), AXES)
    blocks = ("z", "r", "x", "c")
    placed = (
        P(AXES, None),
        P(),
        P(blocks, None),
        P(blocks, None),
        P(None, blocks),
        P(AXES, None, None),
        P("y"),
    )
    return jax.shard_map(
        functools.partial(body, nz=nz, nr=nr),
        mesh=wide,
        in_specs=placed,
        out_specs=P(AXES, None),
        check_vma=False,
    )
```

time: 134 us -> 121 us (0.903)
  waiting for transfers between devices: 66.5 us -> 61.1 us
  starting transfers between devices: 23.6 us -> 19.8 us
  other arithmetic: 5.83 us -> 3.02 us
  local copies, waits for them, and re-layouts: 6.97 us -> 4.99 us
    ppermute x22 -> x21, waiting for transfers between devices: 31.2 us -> 16.3 us  [swap(): return lax.ppermute(v, axis, [(0, 1), (1, 0)])]
    ppermute x6, waiting for transfers between devices: 28.3 us -> 42 us  [ring(): return lax.ppermute(v, 'z', [(i, (i + 1) % nz) for i in range(nz)])]
    ppermute x1, waiting for transfers between devices: 7.04 us -> 2.84 us  [body(): corner = lax.ppermute(toks[3], ('x', 'c'), [(i, i ^ 3) for i in range(4)])]
    ppermute x6, starting transfers between devices: 7.86 us -> 5.08 us  [ring(): return lax.ppermute(v, 'z', [(i, (i + 1) % nz) for i in range(nz)])]
    add x2 -> x1, other arithmetic: 3.38 us -> 1.15 us  [body(): total = parts[2] + tie(from_c, o_near[2], o_far[1])[1]]
    pallas_call x3, Pallas kernels: 21.4 us -> 19.2 us  [the longest x1 8.45 us: attend(): pl.pallas_call(functools.partial(attend_kernel, heads=heads, head=head, n...]
    pallas_call x1 -> x2, Pallas kernels: 8.44 us -> 10.5 us  [output(): pl.pallas_call(functools.partial(out_kernel, plan=plan, nz=nz, nr=nr, bs=...]
    ppermute x22 -> x21, starting transfers between devices: 15.7 us -> 14.6 us  [swap(): return lax.ppermute(v, axis, [(0, 1), (1, 0)])]
  transfers between devices with their start and end apart: 29 -> 28, of which waited for: 10 -> 12; matrix products, arithmetic and copies ran while one was open for 6% -> 2% of each run, Pallas kernels for 16% -> 21%
where the time goes in v2:
time: 121 us; the launch traced here: 120 us
  waiting for transfers between devices  61.1 us (50%)
  Pallas kernels  29.7 us (25%)
  starting transfers between devices  19.8 us (16%)
  local copies, waits for them, and re-layouts  4.99 us (4%)
  other arithmetic  3.02 us (2%)
    ppermute x6, waiting for transfers between devices, ring(): return lax.ppermute(v, 'z', [(i, (i + 1) % nz) for i in range(nz)])  42 us
    ppermute x21, waiting for transfers between devices, swap(): return lax.ppermute(v, axis, [(0, 1), (1, 0)])  16.3 us
    ppermute x21, starting transfers between devices, swap(): return lax.ppermute(v, axis, [(0, 1), (1, 0)])  14.6 us
    pallas_call x2, Pallas kernels, output(): pl.pallas_call(functools.partial(out_kernel, plan=plan, nz=nz, nr=nr, bs=...  10.5 us
    pallas_call x1, Pallas kernels, attend(): pl.pallas_call(functools.partial(attend_kernel, heads=heads, head=head, n...  8.45 us
    pallas_call x1, Pallas kernels, project(): pl.pallas_call(functools.partial(project_kernel, halves=halves), in_specs...  5.63 us
    pallas_call x1, Pallas kernels, normalise(): pl.pallas_call(functools.partial(norm_kernel, nz=nz, nr=nr, bs=bs), grid=...  5.16 us
    ppermute x6, starting transfers between devices, ring(): return lax.ppermute(v, 'z', [(i, (i + 1) % nz) for i in range(nz)])  5.08 us
  transfers between devices with their start and end apart: 28, of which 12 were waited for; matrix products, arithmetic and copies ran while one was open for 2% of the time, Pallas kernels for 21%

profile of v2, /device:TPU:0, one launch (start us, length us, event | category | flops | bytes accessed | tf_op | source)
XLA Modules:
  0.0 119.8 jit_solution(12011176568369133298)
XLA Ops:
  0.0 1.1 constant_dynamic-slice_fusion
  1.1 3.0 %collective-permute-start.1 = (bf16[128,1024]{1,0:T(8,128)(2,1)S(1)}, bf16[128,1024]{1,0:T(8,128)(2,1)S(1)}, u32[]{:S(2)}, u32[]{:S(2)}) collective-permute-start(bf16[128,1024]{1,0:T(8,128)(2,1)S(1)} %get-tuple-element.60), channel_id=1, source_target_pairs={{0,2},{2,0},{1,3},{3,1},{4,6},{6,4},{5,7},{7,5},{8,10},{10,8},{9,1... | collective-permute-start | bytes 786440 | tf_op jit(solution)/shard_map/Ox/ppermute | solution.py:308
  4.1 1.1 constant_dynamic-slice_fusion.2
  5.2 1.6 %collective-permute-start.5 = (bf16[512,512]{1,0:T(8,128)(2,1)S(1)}, bf16[512,512]{1,0:T(8,128)(2,1)S(1)}, u32[]{:S(2)}, u32[]{:S(2)}) collective-permute-start(bf16[512,512]{1,0:T(8,128)(2,1)S(1)} %pad_maximum_fusion), channel_id=1, source_target_pairs={{0,4},{4,8},{8,12},{12,0},{1,5},{5,9},{9,13},{13,1},{2,6},{6,10},{... | collective-permute-start | bytes 1572872 | tf_op jit(solution)/shard_map/Zw1/ppermute | solution.py:311
  6.9 5.2 %norm.1 = (bf16[128,4096]{1,0:T(8,128)(2,1)}, bf16[128,4096]{1,0:T(8,128)(2,1)}, bf16[128,4096]{1,0:T(8,128)(2,1)}, bf16[128,4096]{1,0:T(8,128)(2,1)}) custom-call(bf16[128,16384]{1,0:T(8,128)(2,1)} %tok.5, f32[1,16384]{1,0:T(1,128)} %bitcast.7), custom_call_target="tpu_custom_call" | custom-call | flops 16777216 | bytes 8388608 | tf_op jit(solution)/shard_map/norm/pallas_call | solution.py:45
  13.2 7.4 %collective-permute-done.5.refs_6_ = bf16[512,512]{1,0:T(8,128)(2,1)S(1)} collective-permute-done((bf16[512,512]{1,0:T(8,128)(2,1)S(1)}, bf16[512,512]{1,0:T(8,128)(2,1)S(1)}, u32[]{:S(2)}, u32[]{:S(2)}) %collective-permute-start.5) | collective-permute-done | bytes 524320 | tf_op jit(solution)/shard_map/Zw1/ppermute | solution.py:311
  20.6 1.6 %collective-permute-start.6 = (bf16[512,512]{1,0:T(8,128)(2,1)S(1)}, bf16[512,512]{1,0:T(8,128)(2,1)S(1)}, u32[]{:S(2)}, u32[]{:S(2)}) collective-permute-start(bf16[512,512]{1,0:T(8,128)(2,1)S(1)} %collective-permute-done.5.refs_6_), channel_id=1, source_target_pairs={{0,16},{16,0},{1,17},{17,1},{2,18},{18,2},{3,19},{19,3},{4,20},{20... | collective-permute-start | bytes 1572872 | tf_op jit(solution)/shard_map/Yw1/ppermute | solution.py:308
  22.2 12.7 %collective-permute-done.7.refs_8_ = bf16[512,512]{1,0:T(8,128)(2,1)S(1)} collective-permute-done((bf16[512,512]{1,0:T(8,128)(2,1)S(1)}, bf16[512,512]{1,0:T(8,128)(2,1)S(1)}, u32[]{:S(2)}, u32[]{:S(2)}) %collective-permute-start.7) | collective-permute-done | bytes 524320 | tf_op jit(solution)/shard_map/Zw2/ppermute | solution.py:311
  34.9 1.5 %collective-permute-start.8 = (bf16[512,512]{1,0:T(8,128)(2,1)S(1)}, bf16[512,512]{1,0:T(8,128)(2,1)S(1)}, u32[]{:S(2)}, u32[]{:S(2)}) collective-permute-start(bf16[512,512]{1,0:T(8,128)(2,1)S(1)} %collective-permute-done.7.refs_8_), channel_id=1, source_target_pairs={{0,16},{16,0},{1,17},{17,1},{2,18},{18,2},{3,19},{19,3},{4,20},{20... | collective-permute-start | bytes 1572872 | tf_op jit(solution)/shard_map/Yw2/ppermute | solution.py:308
  36.4 1.9 %collective-permute-done.2.refs_2_ = bf16[128,4096]{1,0:T(8,128)(2,1)S(1)} collective-permute-done((bf16[128,4096]{1,0:T(8,128)(2,1)}, bf16[128,4096]{1,0:T(8,128)(2,1)S(1)}, u32[]{:S(2)}, u32[]{:S(2)}) %collective-permute-start.2) | collective-permute-done | bytes 1048608 | tf_op jit(solution)/shard_map/Tx/ppermute | solution.py:308
  38.3 1.6 %collective-permute-start.11 = (bf16[512,512]{1,0:T(8,128)(2,1)S(1)}, bf16[512,512]{1,0:T(8,128)(2,1)S(1)}, u32[]{:S(2)}, u32[]{:S(2)}) collective-permute-start(bf16[512,512]{1,0:T(8,128)(2,1)S(1)} %collective-permute-done.7.refs_8_), channel_id=1, source_target_pairs={{0,4},{4,8},{8,12},{12,0},{1,5},{5,9},{9,13},{13,1},{2,6},{6,10},{... | collective-permute-start | bytes 1572872 | tf_op jit(solution)/shard_map/Zw3/ppermute | solution.py:311
  39.9 1.6 %collective-permute-start.4 = (bf16[2,128,1024]{2,1,0:T(8,128)(2,1)S(1)}, bf16[2,128,1024]{2,1,0:T(8,128)(2,1)S(1)}, u32[]{:S(2)}, u32[]{:S(2)}) collective-permute-start(bf16[2,128,1024]{2,1,0:T(8,128)(2,1)S(1)} %pad_maximum_fusion.1), channel_id=1, source_target_pairs={{0,4},{4,8},{8,12},{12,0},{1,5},{5,9},{9,13},{13,1},{2,6},{6,10},{... | collective-permute-start | bytes 1572872 | tf_op jit(solution)/shard_map/Zo1/ppermute | solution.py:311
  41.5 5.0 %collective-permute-done.8.refs_9_ = bf16[512,512]{1,0:T(8,128)(2,1)S(1)} collective-permute-done((bf16[512,512]{1,0:T(8,128)(2,1)S(1)}, bf16[512,512]{1,0:T(8,128)(2,1)S(1)}, u32[]{:S(2)}, u32[]{:S(2)}) %collective-permute-start.8) | collective-permute-done | bytes 524320 | tf_op jit(solution)/shard_map/Yw2/ppermute | solution.py:308
  46.5 8.4 %collective-permute-done.11.refs_10_ = bf16[512,512]{1,0:T(8,128)(2,1)S(1)} collective-permute-done((bf16[512,512]{1,0:T(8,128)(2,1)S(1)}, bf16[512,512]{1,0:T(8,128)(2,1)S(1)}, u32[]{:S(2)}, u32[]{:S(2)}) %collective-permute-start.11) | collective-permute-done | bytes 524320 | tf_op jit(solution)/shard_map/Zw3/ppermute | solution.py:311
  54.9 1.5 %collective-permute-start.12 = (bf16[512,512]{1,0:T(8,128)(2,1)S(1)}, bf16[512,512]{1,0:T(8,128)(2,1)S(1)}, u32[]{:S(2)}, u32[]{:S(2)}) collective-permute-start(bf16[512,512]{1,0:T(8,128)(2,1)S(1)} %collective-permute-done.11.refs_10_), channel_id=1, source_target_pairs={{0,16},{16,0},{1,17},{17,1},{2,18},{18,2},{3,19},{19,3},{4,20},{20... | collective-permute-start | bytes 1572872 | tf_op jit(solution)/shard_map/Yw3/ppermute | solution.py:308
  57.0 2.8 %collective-permute-done.3.refs_3_ = bf16[128,4096]{1,0:T(8,128)(2,1)S(1)} collective-permute-done((bf16[128,4096]{1,0:T(8,128)(2,1)}, bf16[128,4096]{1,0:T(8,128)(2,1)S(1)}, u32[]{:S(2)}, u32[]{:S(2)}) %collective-permute-start.3) | collective-permute-done | bytes 1048608 | tf_op jit(solution)/shard_map/Txc/ppermute | solution.py:346
  59.9 4.5 %collective-permute-done.4.refs_6_ = bf16[2,128,1024]{2,1,0:T(8,128)(2,1)S(1)} collective-permute-done((bf16[2,128,1024]{2,1,0:T(8,128)(2,1)S(1)}, bf16[2,128,1024]{2,1,0:T(8,128)(2,1)S(1)}, u32[]{:S(2)}, u32[]{:S(2)}) %collective-permute-start.4) | collective-permute-done | bytes 524320 | tf_op jit(solution)/shard_map/Zo1/ppermute | solution.py:311
  64.4 1.5 %collective-permute-start.16 = (bf16[2,128,1024]{2,1,0:T(8,128)(2,1)S(1)}, bf16[2,128,1024]{2,1,0:T(8,128)(2,1)}, u32[]{:S(2)}, u32[]{:S(2)}) collective-permute-start(bf16[2,128,1024]{2,1,0:T(8,128)(2,1)S(1)} %collective-permute-done.4.refs_6_), channel_id=1, source_target_pairs={{0,16},{16,0},{1,17},{17,1},{2,18},{18,2},{3,19},{19,3},{4,20},{20... | collective-permute-start | bytes 1572872 | tf_op jit(solution)/shard_map/Yo1/ppermute | solution.py:308
  66.0 0.8 copy-done.16
  66.8 5.6 %project.1 = (f32[128,512]{1,0:T(8,128)}, f32[2,128,512]{2,1,0:T(8,128)}, f32[128,512]{1,0:T(8,128)}) custom-call(bf16[128,4096]{1,0:T(8,128)(2,1)} %get-tuple-element.33.refs_0_, bf16[128,4096]{1,0:T(8,128)(2,1)} %copy-done.2, bf16[128,4096]{1,0:T(8,128)(2,1)} %copy-done.3, bf16[128,4096]{1,0:T(8,128)(2,1)} %copy-done.4, bf16[1024,256]{1,0:T(8,128)(2,1)} %refs_4_.1, ...), custom_call_target="tpu_custom_call" | custom-call | flops 2147483648 | bytes 20971520 | tf_op jit(solution)/shard_map/project/pallas_call | solution.py:111
  72.5 4.1 %collective-permute-done.16.refs_7_ = bf16[2,128,1024]{2,1,0:T(8,128)(2,1)} collective-permute-done((bf16[2,128,1024]{2,1,0:T(8,128)(2,1)S(1)}, bf16[2,128,1024]{2,1,0:T(8,128)(2,1)}, u32[]{:S(2)}, u32[]{:S(2)}) %collective-permute-start.16) | collective-permute-done | bytes 524320 | tf_op jit(solution)/shard_map/Yo1/ppermute | solution.py:308
  76.6 3.0 %collective-permute-done.15.refs_10_ = bf16[2,128,1024]{2,1,0:T(8,128)(2,1)} collective-permute-done((bf16[2,128,1024]{2,1,0:T(8,128)(2,1)S(1)}, bf16[2,128,1024]{2,1,0:T(8,128)(2,1)}, u32[]{:S(2)}, u32[]{:S(2)}) %collective-permute-start.15) | collective-permute-done | bytes 524320 | tf_op jit(solution)/shard_map/Zo2/ppermute | solution.py:311
  79.6 1.2 bitcast_add_fusion
  83.6 3.9 %collective-permute-done.17.other = f32[128,512]{1,0:T(8,128)S(1)} collective-permute-done((f32[128,512]{1,0:T(8,128)S(1)}, f32[128,512]{1,0:T(8,128)S(1)}, u32[]{:S(2)}, u32[]{:S(2)}) %collective-permute-start.17) | collective-permute-done | bytes 262176 | tf_op jit(solution)/shard_map/Px/ppermute | solution.py:308
  88.0 6.0 %collective-permute-done.18.refs_2_ = bf16[2,128,1024]{2,1,0:T(8,128)(2,1)S(1)} collective-permute-done((bf16[2,128,1024]{2,1,0:T(8,128)(2,1)}, bf16[2,128,1024]{2,1,0:T(8,128)(2,1)S(1)}, u32[]{:S(2)}, u32[]{:S(2)}) %collective-permute-start.18) | collective-permute-done | bytes 524320 | tf_op jit(solution)/shard_map/Zo3/ppermute | solution.py:311
  94.8 0.8 pad_maximum_fusion.2
  95.6 8.4 %attend.1.att = bf16[128,256]{1,0:T(8,128)(2,1)} custom-call(s32[16]{0:T(128)} %lens.1, f32[128,512]{1,0:T(8,128)} %get-tuple-element.43.mine, f32[2,128,512]{2,1,0:T(8,128)} %copy-done.1, f32[128,512]{1,0:T(8,128)} %copy-done.23, f32[128,128]{1,0:T(8,128)} %get-tuple-element.66.cos, f32[128,128]{1,0:T(8,128)} %get-tuple-element.67.sin, ...), custom_call_target="tpu_custom_call" | custom-call | flops 1073741824 | bytes 29360128 | tf_op jit(solution)/shard_map/attend/pallas_call | solution.py:191
  105.5 0.8 copy-done.22
  106.3 5.9 %output.2.refs_6_ = bf16[128,16384]{1,0:T(8,128)(2,1)} custom-call(bf16[128,256]{1,0:T(8,128)(2,1)} %attend.1.att, bf16[128,16384]{1,0:T(8,128)(2,1)} %tok.5, bf16[256,1024]{1,0:T(8,128)(2,1)} %refs_0_.1, bf16[128,1024]{1,0:T(8,128)(2,1)} %copy-done.5, bf16[128,1024]{1,0:T(8,128)(2,1)} %copy-done.25, bf16[256,1024]{1,0:T(8,128)(2,1)} %copy-done.18, ...), custom_call_target="tpu_custom_call" | custom-call | flops 671088640 | bytes 10485760 | tf_op jit(solution)/shard_map/output/pallas_call | solution.py:272
  112.7 1.5 %collective-permute-done.27.refs_5_ = bf16[2,128,1024]{2,1,0:T(8,128)(2,1)S(1)} collective-permute-done((bf16[2,128,1024]{2,1,0:T(8,128)(2,1)S(1)}, bf16[2,128,1024]{2,1,0:T(8,128)(2,1)S(1)}, u32[]{:S(2)}, u32[]{:S(2)}) %collective-permute-start.27) | collective-permute-done | bytes 524320 | tf_op jit(solution)/shard_map/Oc/ppermute | solution.py:308
  114.2 0.8 copy-done.17
  115.0 4.6 %output.3 = bf16[128,16384]{1,0:T(8,128)(2,1)} custom-call(bf16[128,256]{1,0:T(8,128)(2,1)} %attend.1.att, bf16[128,16384]{1,0:T(8,128)(2,1)} %tok.5, bf16[2,128,1024]{2,1,0:T(8,128)(2,1)} %copy-done.13, bf16[2,128,1024]{2,1,0:T(8,128)(2,1)} %copy-done.14, bf16[2,128,1024]{2,1,0:T(8,128)(2,1)} %copy-done.6, ...), custom_call_target="tpu_custom_call", output_to_operand_aliasing={{}: (8, {})} | custom-call | flops 402653184 | bytes 6291456 | tf_op jit(solution)/shard_map/output/pallas_call | solution.py:272
  (95 shorter events, 7.4 us)
Async XLA Ops:
  1.1 10.9 %collective-permute-start.1 = (bf16[128,1024]{1,0:T(8,128)(2,1)S(1)}, bf16[128,1024]{1,0:T(8,128)(2,1)S(1)}, u32[]{:S(2)}, u32[]{:S(2)}) collective-permute-start(bf16[128,1024]{1,0:T(8,128)(2,1)S(1)} %get-tuple-element.60), channel_id=1, source_target_pairs={{0,2},{2,0},{1,3},{3,1},{4,6},{6,4},{5,7},{7,5},{8,10},{10,8},{9,1... | collective-permute-start | bytes 786440 | tf_op jit(solution)/shard_map/Ox/ppermute | solution.py:308
  5.2 15.3 %collective-permute-start.5 = (bf16[512,512]{1,0:T(8,128)(2,1)S(1)}, bf16[512,512]{1,0:T(8,128)(2,1)S(1)}, u32[]{:S(2)}, u32[]{:S(2)}) collective-permute-start(bf16[512,512]{1,0:T(8,128)(2,1)S(1)} %pad_maximum_fusion), channel_id=1, source_target_pairs={{0,4},{4,8},{8,12},{12,0},{1,5},{5,9},{9,13},{13,1},{2,6},{6,10},{... | collective-permute-start | bytes 1572872 | tf_op jit(solution)/shard_map/Zw1/ppermute | solution.py:311
  12.0 24.4 %collective-permute-start = (bf16[128,4096]{1,0:T(8,128)(2,1)}, bf16[128,4096]{1,0:T(8,128)(2,1)S(1)}, u32[]{:S(2)}, u32[]{:S(2)}) collective-permute-start(bf16[128,4096]{1,0:T(8,128)(2,1)} %get-tuple-element.34), channel_id=1, source_target_pairs={{0,1},{1,0},{2,3},{3,2},{4,5},{5,4},{6,7},{7,6},{8,9},{9,8},{10,11... | collective-permute-start | bytes 3145736 | tf_op jit(solution)/shard_map/Tc/ppermute | solution.py:308
  12.0 93.1 %copy-start.5 = (bf16[128,1024]{1,0:T(8,128)(2,1)}, bf16[128,1024]{1,0:T(8,128)(2,1)S(1)}, u32[]{:S(2)}) copy-start(bf16[128,1024]{1,0:T(8,128)(2,1)S(1)} %collective-permute-done.1.refs_1_) | copy-start | bytes 786436
  12.0 26.2 %collective-permute-start.2 = (bf16[128,4096]{1,0:T(8,128)(2,1)}, bf16[128,4096]{1,0:T(8,128)(2,1)S(1)}, u32[]{:S(2)}, u32[]{:S(2)}) collective-permute-start(bf16[128,4096]{1,0:T(8,128)(2,1)} %get-tuple-element.36), channel_id=1, source_target_pairs={{0,2},{2,0},{1,3},{3,1},{4,6},{6,4},{5,7},{7,5},{8,10},{10,8},{9,1... | collective-permute-start | bytes 3145736 | tf_op jit(solution)/shard_map/Tx/ppermute | solution.py:308
  12.7 7.9 %collective-permute-start.10 = (bf16[128,1024]{1,0:T(8,128)(2,1)S(1)}, bf16[128,1024]{1,0:T(8,128)(2,1)S(1)}, u32[]{:S(2)}, u32[]{:S(2)}) collective-permute-start(bf16[128,1024]{1,0:T(8,128)(2,1)S(1)} %collective-permute-done.1.refs_1_), channel_id=1, source_target_pairs={{0,1},{1,0},{2,3},{3,2},{4,5},{5,4},{6,7},{7,6},{8,9},{9,8},{10,11... | collective-permute-start | bytes 786440 | tf_op jit(solution)/shard_map/Oc0/ppermute | solution.py:308
  12.8 9.3 %collective-permute-start.9 = (bf16[256,1024]{1,0:T(8,128)(2,1)S(1)}, bf16[256,1024]{1,0:T(8,128)(2,1)S(1)}, u32[]{:S(2)}, u32[]{:S(2)}) collective-permute-start(bf16[256,1024]{1,0:T(8,128)(2,1)S(1)} %copy-done), channel_id=1, source_target_pairs={{0,1},{1,0},{2,3},{3,2},{4,5},{5,4},{6,7},{7,6},{8,9},{9,8},{10,11... | collective-permute-start | bytes 1572872 | tf_op jit(solution)/shard_map/Oc0/ppermute | solution.py:308
  20.5 45.4 %copy-start.7 = (bf16[512,512]{1,0:T(8,128)(2,1)}, bf16[512,512]{1,0:T(8,128)(2,1)S(1)}, u32[]{:S(2)}) copy-start(bf16[512,512]{1,0:T(8,128)(2,1)S(1)} %collective-permute-done.5.refs_6_) | copy-start | bytes 1572868
  20.5 14.3 %collective-permute-start.7 = (bf16[512,512]{1,0:T(8,128)(2,1)S(1)}, bf16[512,512]{1,0:T(8,128)(2,1)S(1)}, u32[]{:S(2)}, u32[]{:S(2)}) collective-permute-start(bf16[512,512]{1,0:T(8,128)(2,1)S(1)} %collective-permute-done.5.refs_6_), channel_id=1, source_target_pairs={{0,4},{4,8},{8,12},{12,0},{1,5},{5,9},{9,13},{13,1},{2,6},{6,10},{... | collective-permute-start | bytes 1572872 | tf_op jit(solution)/shard_map/Zw2/ppermute | solution.py:311
  20.6 15.8 %collective-permute-start.6 = (bf16[512,512]{1,0:T(8,128)(2,1)S(1)}, bf16[512,512]{1,0:T(8,128)(2,1)S(1)}, u32[]{:S(2)}, u32[]{:S(2)}) collective-permute-start(bf16[512,512]{1,0:T(8,128)(2,1)S(1)} %collective-permute-done.5.refs_6_), channel_id=1, source_target_pairs={{0,16},{16,0},{1,17},{17,1},{2,18},{18,2},{3,19},{19,3},{4,20},{20... | collective-permute-start | bytes 1572872 | tf_op jit(solution)/shard_map/Yw1/ppermute | solution.py:308
  22.2 83.0 %copy-start.18 = (bf16[256,1024]{1,0:T(8,128)(2,1)}, bf16[256,1024]{1,0:T(8,128)(2,1)S(1)}, u32[]{:S(2)}) copy-start(bf16[256,1024]{1,0:T(8,128)(2,1)S(1)} %collective-permute-done.9.refs_3_) | copy-start | bytes 1572868
  22.2 37.7 %collective-permute-start.3 = (bf16[128,4096]{1,0:T(8,128)(2,1)}, bf16[128,4096]{1,0:T(8,128)(2,1)S(1)}, u32[]{:S(2)}, u32[]{:S(2)}) collective-permute-start(bf16[128,4096]{1,0:T(8,128)(2,1)} %get-tuple-element.37), channel_id=1, source_target_pairs={{0,3},{1,2},{2,1},{3,0},{4,7},{5,6},{6,5},{7,4},{8,11},{9,10},{10,... | collective-permute-start | bytes 3145736 | tf_op jit(solution)/shard_map/Txc/ppermute | solution.py:346
  34.9 11.6 %collective-permute-start.8 = (bf16[512,512]{1,0:T(8,128)(2,1)S(1)}, bf16[512,512]{1,0:T(8,128)(2,1)S(1)}, u32[]{:S(2)}, u32[]{:S(2)}) collective-permute-start(bf16[512,512]{1,0:T(8,128)(2,1)S(1)} %collective-permute-done.7.refs_8_), channel_id=1, source_target_pairs={{0,16},{16,0},{1,17},{17,1},{2,18},{18,2},{3,19},{19,3},{4,20},{20... | collective-permute-start | bytes 1572872 | tf_op jit(solution)/shard_map/Yw2/ppermute | solution.py:308
  38.3 16.7 %collective-permute-start.11 = (bf16[512,512]{1,0:T(8,128)(2,1)S(1)}, bf16[512,512]{1,0:T(8,128)(2,1)S(1)}, u32[]{:S(2)}, u32[]{:S(2)}) collective-permute-start(bf16[512,512]{1,0:T(8,128)(2,1)S(1)} %collective-permute-done.7.refs_8_), channel_id=1, source_target_pairs={{0,4},{4,8},{8,12},{12,0},{1,5},{5,9},{9,13},{13,1},{2,6},{6,10},{... | collective-permute-start | bytes 1572872 | tf_op jit(solution)/shard_map/Zw3/ppermute | solution.py:311
  39.9 24.4 %collective-permute-start.4 = (bf16[2,128,1024]{2,1,0:T(8,128)(2,1)S(1)}, bf16[2,128,1024]{2,1,0:T(8,128)(2,1)S(1)}, u32[]{:S(2)}, u32[]{:S(2)}) collective-permute-start(bf16[2,128,1024]{2,1,0:T(8,128)(2,1)S(1)} %pad_maximum_fusion.1), channel_id=1, source_target_pairs={{0,4},{4,8},{8,12},{12,0},{1,5},{5,9},{9,13},{13,1},{2,6},{6,10},{... | collective-permute-start | bytes 1572872 | tf_op jit(solution)/shard_map/Zo1/ppermute | solution.py:311
  54.9 10.9 %collective-permute-start.12 = (bf16[512,512]{1,0:T(8,128)(2,1)S(1)}, bf16[512,512]{1,0:T(8,128)(2,1)S(1)}, u32[]{:S(2)}, u32[]{:S(2)}) collective-permute-start(bf16[512,512]{1,0:T(8,128)(2,1)S(1)} %collective-permute-done.11.refs_10_), channel_id=1, source_target_pairs={{0,16},{16,0},{1,17},{17,1},{2,18},{18,2},{3,19},{19,3},{4,20},{20... | collective-permute-start | bytes 1572872 | tf_op jit(solution)/shard_map/Yw3/ppermute | solution.py:308
  56.5 15.9 %collective-permute-start.13 = (bf16[128,1024]{1,0:T(8,128)(2,1)S(1)}, bf16[128,1024]{1,0:T(8,128)(2,1)S(1)}, u32[]{:S(2)}, u32[]{:S(2)}) collective-permute-start(bf16[128,1024]{1,0:T(8,128)(2,1)S(1)} %get-tuple-element.45), channel_id=1, source_target_pairs={{0,2},{2,0},{1,3},{3,1},{4,6},{6,4},{5,7},{7,5},{8,10},{10,8},{9,1... | collective-permute-start | bytes 786440 | tf_op jit(solution)/shard_map/Oxe/ppermute | solution.py:308
  64.4 40.8 %copy-start.19 = (bf16[2,128,1024]{2,1,0:T(8,128)(2,1)}, bf16[2,128,1024]{2,1,0:T(8,128)(2,1)S(1)}, u32[]{:S(2)}) copy-start(bf16[2,128,1024]{2,1,0:T(8,128)(2,1)S(1)} %collective-permute-done.4.refs_6_) | copy-start | bytes 1572868
  64.4 12.2 %collective-permute-start.16 = (bf16[2,128,1024]{2,1,0:T(8,128)(2,1)S(1)}, bf16[2,128,1024]{2,1,0:T(8,128)(2,1)}, u32[]{:S(2)}, u32[]{:S(2)}) collective-permute-start(bf16[2,128,1024]{2,1,0:T(8,128)(2,1)S(1)} %collective-permute-done.4.refs_6_), channel_id=1, source_target_pairs={{0,16},{16,0},{1,17},{17,1},{2,18},{18,2},{3,19},{19,3},{4,20},{20... | collective-permute-start | bytes 1572872 | tf_op jit(solution)/shard_map/Yo1/ppermute | solution.py:308
  65.9 13.7 %collective-permute-start.15 = (bf16[2,128,1024]{2,1,0:T(8,128)(2,1)S(1)}, bf16[2,128,1024]{2,1,0:T(8,128)(2,1)}, u32[]{:S(2)}, u32[]{:S(2)}) collective-permute-start(bf16[2,128,1024]{2,1,0:T(8,128)(2,1)S(1)} %collective-permute-done.4.refs_6_), channel_id=1, source_target_pairs={{0,4},{4,8},{8,12},{12,0},{1,5},{5,9},{9,13},{13,1},{2,6},{6,10},{... | collective-permute-start | bytes 1572872 | tf_op jit(solution)/shard_map/Zo2/ppermute | solution.py:311
  72.4 7.2 %collective-permute-start.14 = (f32[2,128,512]{2,1,0:T(8,128)}, f32[2,128,512]{2,1,0:T(8,128)S(1)}, u32[]{:S(2)}, u32[]{:S(2)}) collective-permute-start(f32[2,128,512]{2,1,0:T(8,128)} %get-tuple-element.46), channel_id=1, source_target_pairs={{0,1},{1,0},{2,3},{3,2},{4,5},{5,4},{6,7},{7,6},{8,9},{9,8},{10,11... | collective-permute-start | bytes 1572872 | tf_op jit(solution)/shard_map/Pc/ppermute | solution.py:308
  80.8 13.2 %collective-permute-start.18 = (bf16[2,128,1024]{2,1,0:T(8,128)(2,1)}, bf16[2,128,1024]{2,1,0:T(8,128)(2,1)S(1)}, u32[]{:S(2)}, u32[]{:S(2)}) collective-permute-start(bf16[2,128,1024]{2,1,0:T(8,128)(2,1)} %collective-permute-done.15.refs_10_), channel_id=1, source_target_pairs={{0,4},{4,8},{8,12},{12,0},{1,5},{5,9},{9,13},{13,1},{2,6},{6,10},{... | collective-permute-start | bytes 1572872 | tf_op jit(solution)/shard_map/Zo3/ppermute | solution.py:311
  81.0 6.4 %collective-permute-start.17 = (f32[128,512]{1,0:T(8,128)S(1)}, f32[128,512]{1,0:T(8,128)S(1)}, u32[]{:S(2)}, u32[]{:S(2)}) collective-permute-start(f32[128,512]{1,0:T(8,128)S(1)} %bitcast_add_fusion), channel_id=1, source_target_pairs={{0,2},{2,0},{1,3},{3,1},{4,6},{6,4},{5,7},{7,5},{8,10},{10,8},{9,1... | collective-permute-start | bytes 786440 | tf_op jit(solution)/shard_map/Px/ppermute | solution.py:308
  83.0 12.5 %collective-permute-start.19 = (bf16[2,128,1024]{2,1,0:T(8,128)(2,1)}, bf16[2,128,1024]{2,1,0:T(8,128)(2,1)S(1)}, u32[]{:S(2)}, u32[]{:S(2)}) collective-permute-start(bf16[2,128,1024]{2,1,0:T(8,128)(2,1)} %collective-permute-done.15.refs_10_), channel_id=1, source_target_pairs={{0,16},{16,0},{1,17},{17,1},{2,18},{18,2},{3,19},{19,3},{4,20},{20... | collective-permute-start | bytes 1572872 | tf_op jit(solution)/shard_map/Yo2/ppermute | solution.py:308
  87.5 17.2 %collective-permute-start.25 = (bf16[2,128,1024]{2,1,0:T(8,128)(2,1)S(1)}, bf16[2,128,1024]{2,1,0:T(8,128)(2,1)S(1)}, u32[]{:S(2)}, u32[]{:S(2)}) collective-permute-start(bf16[2,128,1024]{2,1,0:T(8,128)(2,1)S(1)} %collective-permute-done.4.refs_6_), channel_id=1, source_target_pairs={{0,1},{1,0},{2,3},{3,2},{4,5},{5,4},{6,7},{7,6},{8,9},{9,8},{10,11... | collective-permute-start | bytes 1572872 | tf_op jit(solution)/shard_map/Oc1/ppermute | solution.py:308
  87.5 17.6 %collective-permute-start.26 = (bf16[2,128,1024]{2,1,0:T(8,128)(2,1)}, bf16[2,128,1024]{2,1,0:T(8,128)(2,1)S(1)}, u32[]{:S(2)}, u32[]{:S(2)}) collective-permute-start(bf16[2,128,1024]{2,1,0:T(8,128)(2,1)} %collective-permute-done.16.refs_7_), channel_id=1, source_target_pairs={{0,1},{1,0},{2,3},{3,2},{4,5},{5,4},{6,7},{7,6},{8,9},{9,8},{10,11... | collective-permute-start | bytes 1572872 | tf_op jit(solution)/shard_map/Oc1/ppermute | solution.py:308
  93.9 18.2 %collective-permute-start.22 = (bf16[2,128,1024]{2,1,0:T(8,128)(2,1)S(1)}, bf16[2,128,1024]{2,1,0:T(8,128)(2,1)S(1)}, u32[]{:S(2)}, u32[]{:S(2)}) collective-permute-start(bf16[2,128,1024]{2,1,0:T(8,128)(2,1)S(1)} %collective-permute-done.18.refs_2_), channel_id=1, source_target_pairs={{0,16},{16,0},{1,17},{17,1},{2,18},{18,2},{3,19},{19,3},{4,20},{20... | collective-permute-start | bytes 1572872 | tf_op jit(solution)/shard_map/Yo3/ppermute | solution.py:308
  94.5 10.1 %collective-permute-start.24 = (bf16[128,1024]{1,0:T(8,128)(2,1)}, bf16[128,1024]{1,0:T(8,128)(2,1)S(1)}, u32[]{:S(2)}, u32[]{:S(2)}) collective-permute-start(bf16[128,1024]{1,0:T(8,128)(2,1)} %copy-done.25), channel_id=1, source_target_pairs={{0,1},{1,0},{2,3},{3,2},{4,5},{5,4},{6,7},{7,6},{8,9},{9,8},{10,11... | collective-permute-start | bytes 786440 | tf_op jit(solution)/shard_map/Oc1/ppermute | solution.py:308
  104.0 8.6 %collective-permute-start.20 = (bf16[2,128,1024]{2,1,0:T(8,128)(2,1)}, bf16[2,128,1024]{2,1,0:T(8,128)(2,1)S(1)}, u32[]{:S(2)}, u32[]{:S(2)}) collective-permute-start(bf16[2,128,1024]{2,1,0:T(8,128)(2,1)} %collective-permute-done.15.refs_10_), channel_id=1, source_target_pairs={{0,1},{1,0},{2,3},{3,2},{4,5},{5,4},{6,7},{7,6},{8,9},{9,8},{10,11... | collective-permute-start | bytes 1572872 | tf_op jit(solution)/shard_map/Oc/ppermute | solution.py:308
  104.6 8.1 %collective-permute-start.21 = (bf16[2,128,1024]{2,1,0:T(8,128)(2,1)S(1)}, bf16[2,128,1024]{2,1,0:T(8,128)(2,1)S(1)}, u32[]{:S(2)}, u32[]{:S(2)}) collective-permute-start(bf16[2,128,1024]{2,1,0:T(8,128)(2,1)S(1)} %collective-permute-done.19.refs_11_), channel_id=1, source_target_pairs={{0,1},{1,0},{2,3},{3,2},{4,5},{5,4},{6,7},{7,6},{8,9},{9,8},{10,11... | collective-permute-start | bytes 1572872 | tf_op jit(solution)/shard_map/Oc/ppermute | solution.py:308
  104.7 8.0 %collective-permute-start.23 = (bf16[2,128,1024]{2,1,0:T(8,128)(2,1)S(1)}, bf16[2,128,1024]{2,1,0:T(8,128)(2,1)S(1)}, u32[]{:S(2)}, u32[]{:S(2)}) collective-permute-start(bf16[2,128,1024]{2,1,0:T(8,128)(2,1)S(1)} %collective-permute-done.18.refs_2_), channel_id=1, source_target_pairs={{0,1},{1,0},{2,3},{3,2},{4,5},{5,4},{6,7},{7,6},{8,9},{9,8},{10,11... | collective-permute-start | bytes 1572872 | tf_op jit(solution)/shard_map/Oc/ppermute | solution.py:308
  112.2 2.0 %collective-permute-start.27 = (bf16[2,128,1024]{2,1,0:T(8,128)(2,1)S(1)}, bf16[2,128,1024]{2,1,0:T(8,128)(2,1)S(1)}, u32[]{:S(2)}, u32[]{:S(2)}) collective-permute-start(bf16[2,128,1024]{2,1,0:T(8,128)(2,1)S(1)} %collective-permute-done.22.refs_3_), channel_id=1, source_target_pairs={{0,1},{1,0},{2,3},{3,2},{4,5},{5,4},{6,7},{7,6},{8,9},{9,8},{10,11... | collective-permute-start | bytes 1572872 | tf_op jit(solution)/shard_map/Oc/ppermute | solution.py:308
  (24 other events, 263.3 us)

commit v3 on v2

--- a/solution.py
+++ b/solution.py
@@ -1,4 +1,5 @@
 import functools
+import math
 
 import jax
 import jax.numpy as jnp
@@ -10,18 +11,64 @@
 F32 = jnp.float32
 BF16 = jnp.bfloat16
 AXES = ("y", "z", "r", "x", "c")
-VMEM_LIMIT = 56 * 1024 * 1024
-
-
-def params():
-    return pltpu.CompilerParams(vmem_limit_bytes=VMEM_LIMIT)
-
-
-def norm_kernel(tok, gain, *outs, nz, nr, bs):
+
+
+def params(mib):
+    return pltpu.CompilerParams(vmem_limit_bytes=mib * 1024 * 1024)
+
+
+def gather_kernel(*refs, jobs):
+    y = lax.axis_index("y")
+    sem = refs[-1]
+    copies = []
+    for i, (src, side, rows, dst, lead, cols) in enumerate(jobs):
+        ref, to = refs[src], refs[dst]
+        if side is not None:
+            ref = ref.at[pl.ds(pl.multiple_of((y if side == 0 else 1 - y) * rows, rows), rows)]
+        if lead is not None:
+            to = to.at[lead]
+        if cols is not None:
+            to = to.at[:, pl.ds(*cols)]
+        copies.append(pltpu.make_async_copy(ref, to, sem.at[i]))
+    for cp in copies:
+        cp.start()
+    for cp in copies:
+        cp.wait()
+
+
+def gather(arrays, shapes, jobs, name, limit, space):
+    anywhere = pl.BlockSpec(memory_space=pl.ANY)
+    size = sum(math.prod(shape) for shape in shapes)
+    return pl.pallas_call(
+        functools.partial(gather_kernel, jobs=jobs),
+        in_specs=[anywhere] * len(arrays),
+        out_specs=[pl.BlockSpec(memory_space=space)] * len(shapes),
+        out_shape=[jax.ShapeDtypeStruct(shape, BF16) for shape in shapes],
+        scratch_shapes=[pltpu.SemaphoreType.DMA((len(jobs),))],
+        compiler_params=params(limit),
+        cost_estimate=pl.CostEstimate(flops=0, bytes_accessed=4 * size, transcendentals=0),
+        name=name,
+    )(*arrays)
+
+
+def norm_kernel(tokens, gain, *refs, nz, nr, bs, block):
     z, x, c = (lax.axis_index(a) for a in ("z", "x", "c"))
+    outs, tbuf, sem = refs[:4], refs[4], refs[5]
+    n = pl.program_id(0)
+
+    def load(i):
+        return pltpu.make_async_copy(tokens.at[pl.ds(i * block, block)], tbuf.at[i], sem.at[i])
+
+    @pl.when(n == 0)
+    def _():
+        for i in range(tbuf.shape[0]):
+            load(i).start()
+
+    load(n).wait()
+    tok = tbuf.at[n]
     width = tok.shape[1]
     step = 1024
-    for r0 in range(0, tok.shape[0], 16):
+    for r0 in range(0, block, 16):
         rows = pl.ds(r0, 16)
         acc = jnp.zeros((16, step), F32)
         for j in range(width // step):
@@ -43,13 +90,14 @@
     block = 32
     quarter = width // 4
     return pl.pallas_call(
-        functools.partial(norm_kernel, nz=nz, nr=nr, bs=bs),
+        functools.partial(norm_kernel, nz=nz, nr=nr, bs=bs, block=block),
         grid=(rows // block,),
-        in_specs=[pl.BlockSpec((block, width), lambda i: (i, 0)), pl.BlockSpec((1, width), lambda i: (0, 0))],
+        in_specs=[pl.BlockSpec(memory_space=pl.ANY), pl.BlockSpec((1, width), lambda i: (0, 0))],
         out_specs=[pl.BlockSpec((block, quarter), lambda i: (i, 0))] * 4,
         out_shape=[jax.ShapeDtypeStruct((rows, quarter), BF16)] * 4,
-        compiler_params=params(),
-        cost_estimate=pl.CostEstimate(flops=8 * rows * width, bytes_accessed=4 * rows * width, transcendentals=0),
+        scratch_shapes=[pltpu.VMEM((rows // block, block, width), BF16), pltpu.SemaphoreType.DMA((rows // block,))],
+        compiler_params=params(56),
+        cost_estimate=pl.CostEstimate(flops=8 * rows * width, bytes_accessed=rows * width, transcendentals=0),
         name="norm",
     )(tokens, gain.reshape(1, width))
 
@@ -119,9 +167,9 @@
             pltpu.SemaphoreType.DMA((steps, 4)),
             pltpu.SemaphoreType.DMA((len(halves), 2)),
         ],
-        compiler_params=params(),
+        compiler_params=params(16),
         cost_estimate=pl.CostEstimate(
-            flops=2 * 4 * rows * depth * width, bytes_accessed=20 * 1024 * 1024, transcendentals=0
+            flops=2 * 4 * rows * depth * width, bytes_accessed=2 * 1024 * 1024, transcendentals=0
         ),
         name="project",
     )(*toks, *flat)
@@ -132,7 +180,8 @@
     return ((z * nr + r) * 2 + x) * 2 + c
 
 
-def attend_kernel(lens, mine, core, other, cos, sin, cache, out, kvbuf, sem, *, heads, head, nr):
+def attend_kernel(lens, *refs, heads, head, nr):
+    mine, core, other, turns, cache, out, pbuf, kvbuf, psem, sem = refs
     length = lens[prompt_index(nr)]
     slots = kvbuf.shape[0]
     rows = mine.shape[0]
@@ -143,12 +192,17 @@
         )
         for i in range(slots // chunk)
     ]
-    for cp in copies:
+    sums = [
+        pltpu.make_async_copy(ref, pbuf.at[i], psem.at[i]) for i, ref in enumerate((mine, core.at[0], other))
+    ]
+    for cp in sums + copies:
         cp.start()
-    total = (mine[...] + core[0]) + other[...]
+    for cp in sums:
+        cp.wait()
+    total = (pbuf[0] + pbuf[1]) + pbuf[2]
 
     def turn(v):
-        return (v * cos[...] + pltpu.roll(v, head // 2, 1) * sin[...]).astype(BF16)
+        return (v * turns[0] + pltpu.roll(v, head // 2, 1) * turns[1]).astype(BF16)
 
     q = jnp.concatenate([turn(total[:, i * head : (i + 1) * head]) for i in range(heads)], axis=0)
     k_new = turn(total[:, heads * head : (heads + 1) * head])
@@ -184,22 +238,28 @@
         out[:, i * head : (i + 1) * head] = acc[i * rows : (i + 1) * rows]
 
 
-def attend(lens, mine, core, other, cos, sin, cache, heads, head, nr):
+def attend(lens, mine, core, other, turns, cache, heads, head, nr):
     vmem = pl.BlockSpec(memory_space=pltpu.VMEM)
     rows = mine.shape[0]
     slots = cache.shape[1]
+    anywhere = pl.BlockSpec(memory_space=pl.ANY)
     return pl.pallas_call(
         functools.partial(attend_kernel, heads=heads, head=head, nr=nr),
-        in_specs=[pl.BlockSpec(memory_space=pltpu.SMEM)] + [vmem] * 5 + [pl.BlockSpec(memory_space=pl.ANY)],
+        in_specs=[pl.BlockSpec(memory_space=pltpu.SMEM)] + [anywhere] * 3 + [vmem, anywhere],
         out_specs=vmem,
         out_shape=jax.ShapeDtypeStruct((rows, heads * head), BF16),
-        scratch_shapes=[pltpu.VMEM(cache.shape[1:], BF16), pltpu.SemaphoreType.DMA((slots // 1024,))],
-        compiler_params=params(),
+        scratch_shapes=[
+            pltpu.VMEM((3,) + mine.shape, F32),
+            pltpu.VMEM(cache.shape[1:], BF16),
+            pltpu.SemaphoreType.DMA((3,)),
+            pltpu.SemaphoreType.DMA((slots // 1024,)),
+        ],
+        compiler_params=params(20),
         cost_estimate=pl.CostEstimate(
             flops=4 * rows * heads * head * slots, bytes_accessed=28 * 1024 * 1024, transcendentals=rows * heads * slots
         ),
         name="attend",
-    )(lens, mine, core, other, cos, sin, cache)
+    )(lens, mine, core, other, turns, cache)
 
 
 def out_kernel(att, tok, *refs, plan, nz, nr, bs, carry):
@@ -284,7 +344,7 @@
             pltpu.SemaphoreType.DMA((slots, nr)),
             pltpu.SemaphoreType.DMA((slots, nr)),
         ],
-        compiler_params=params(),
+        compiler_params=params(12),
         cost_estimate=pl.CostEstimate(
             flops=2 * rows * nr * bs * len(plan) * att.shape[1],
             bytes_accessed=(att.shape[1] + 2 * rows) * 2 * nr * bs * len(plan),
@@ -294,16 +354,22 @@
     )(att, tokens, *weights, *(() if base is None else (base,)))
 
 
+def trig(lens, rows, head, nr):
+    length = jnp.sum(jnp.where(jnp.arange(lens.shape[0], dtype=jnp.int32) == prompt_index(nr), lens, 0))
+    positions = length.astype(F32) + jnp.arange(rows, dtype=F32)
+    steps = jnp.arange(head // 2, dtype=F32) * (2.0 / head)
+    freqs = jnp.exp(-jnp.log(jnp.float32(500000.0)) * steps)
+    angles = positions[:, None] * freqs[None, :]
+    cos, sin = jnp.cos(angles), jnp.sin(angles)
+    return jnp.stack([jnp.concatenate([cos, cos], axis=1), jnp.concatenate([-sin, sin], axis=1)])
+
+
 def body(tokens, gain, w_query, w_key_value, w_out, cache_kv, cached_len, *, nz, nr):
     rows = tokens.shape[0]
     head = w_key_value.shape[1] // 2
     heads = w_query.shape[1] // head
     bs = w_query.shape[0]
     y = lax.axis_index("y")
-    length = jnp.sum(
-        jnp.where(jnp.arange(cached_len.shape[0], dtype=jnp.int32) == prompt_index(nr), cached_len, 0)
-    )
-
     def swap(v, axis):
         return lax.ppermute(v, axis, [(0, 1), (1, 0)])
 
@@ -321,13 +387,18 @@
     def tie(v, *after):
         return lax.optimization_barrier((v,) + after)[0]
 
-    w_mine = jnp.concatenate([lax.dynamic_slice_in_dim(w, y * half, half) for w in (own_q, own_kv)], axis=1)
-    o_mine = lax.dynamic_slice_in_dim(own_o, y * ohalf, ohalf)
-    o_else = lax.dynamic_slice_in_dim(own_o, (1 - y) * ohalf, ohalf)
-    gain = tie(gain, w_mine, o_mine)
+    width = own_q.shape[1]
     with jax.named_scope("Ox"):
-        o_mine_x = swap(o_mine, "x")
-    toks = normalise(tokens, gain, nz, nr, bs)
+        x_o = swap(own_o, "x")
+    (w_mine,) = gather(
+        (own_q, own_kv),
+        ((half, 2 * width),),
+        ((0, 0, half, 2, None, (0, width)), (1, 0, half, 2, None, (width, width))),
+        "pick",
+        56,
+        pltpu.VMEM,
+    )
+    toks = normalise(tokens, tie(gain, w_mine), nz, nr, bs)
 
     def step_z(v, name, *after):
         with jax.named_scope("Z" + name):
@@ -341,15 +412,26 @@
     with jax.named_scope("Tc"):
         core_toks = swap(toks[1], "c")
     with jax.named_scope("Tx"):
-        across = swap(tie(toks[2], o_mine_x), "x")
+        across = swap(toks[2], "x")
     with jax.named_scope("Txc"):
         corner = lax.ppermute(toks[3], ("x", "c"), [(i, i ^ 3) for i in range(4)])
     with jax.named_scope("Oc0"):
         own_o_c = swap(own_o, "c")
-        o_mine_x_c = swap(o_mine_x, "c")
+        x_o_c = swap(x_o, "c")
+    (pair,) = gather(
+        (own_o, x_o),
+        ((2, ohalf, own_o.shape[1]),),
+        ((0, 0, ohalf, 2, 0, None), (1, 0, ohalf, 2, 1, None)),
+        "pair",
+        4,
+        pltpu.VMEM,
+    )
     v = w_mine
+    turns = None
     for s in range(1, nz):
-        after = [w_far[s - 2], core_toks, across, own_o_c, o_mine_x_c] if s == 3 else []
+        if s == nz - 1:
+            turns = trig(tie(cached_len, w_near[1]), rows, head, nr)
+        after = [w_far[s - 2], core_toks, own_o_c, x_o_c, turns] if s == 3 else []
         v = step_z(v, f"w{s}", *after)
         w_near.append(v)
         w_far.append(step_y(v, f"w{s}", *(w_far[2:] if s == 3 else [])))
@@ -366,39 +448,30 @@
                 halves.append((s - steps[0], side, 1))
         return weights, halves
 
-    with jax.named_scope("Oxe"):
-        o_else_x = swap(tie(o_else, w_near[3]), "x")
     o_near, o_far = [None], [None]
-    o_near.append(step_z(jnp.stack([o_mine, tie(o_mine_x, toks[0])]), "o1", across))
+    o_near.append(step_z(pair, "o1", across))
     held = [toks[0], core_toks, across, tie(corner, o_near[1])]
     parts = project(held, *weights_of(range(nz)))
     o_near.append(step_z(o_near[1], "o2"))
     o_far.append(step_y(o_near[1], "o1"))
     with jax.named_scope("Pc"):
-        from_c = swap(tie(parts[1], o_else_x), "c")
-    total = parts[2] + tie(from_c, o_near[2], o_far[1])[1]
+        from_c = swap(tie(parts[1], o_near[2], o_far[1]), "c")
+    total = parts[2] + from_c[1]
     with jax.named_scope("Px"):
         other = swap(total, "x")
-    o_near.append(step_z(o_near[2], "o3", total))
+    o_near.append(step_z(o_near[2], "o3"))
     for s in range(2, nz):
-        o_far.append(step_y(o_near[s], f"o{s}", total))
+        o_far.append(step_y(o_near[s], f"o{s}"))
     with jax.named_scope("Oc1"):
-        o_else_x_c = swap(tie(o_else_x, other), "c")
         near1_c = swap(tie(o_near[1], other), "c")
         far1_c = swap(tie(o_far[1], other), "c")
 
-    positions = length.astype(F32) + jnp.arange(rows, dtype=F32)
-    steps = jnp.arange(head // 2, dtype=F32) * (2.0 / head)
-    freqs = jnp.exp(-jnp.log(jnp.float32(500000.0)) * steps)
-    angles = positions[:, None] * freqs[None, :]
-    cos, sin = jnp.cos(angles), jnp.sin(angles)
     att = attend(
         cached_len,
         parts[0],
         from_c,
-        tie(other, o_near[3], o_far[2]),
-        jnp.concatenate([cos, cos], axis=1),
-        jnp.concatenate([-sin, sin], axis=1),
+        tie(other, o_near[3]),
+        turns,
         cache_kv,
         heads,
         head,
@@ -429,9 +502,8 @@
 
     early, late = [], []
     for dc in range(2):
-        own, mx, ex = ((own_o, o_mine_x, o_else_x), (own_o_c, o_mine_x_c, o_else_x_c))[dc]
-        early.append(((0, 0, dc), [(own, None, 0), (own, None, 1)]))
-        early.append(((0, 1, dc), [(mx, None, None), (ex, None, None)]))
+        for dx, v in enumerate(((own_o, x_o), (own_o_c, x_o_c))[dc]):
+            early.append(((0, dx, dc), [(v, None, 0), (v, None, 1)]))
     early += blocks(1, 0, o_near[1], o_far[1]) + blocks(1, 1, near1_c, far1_c) + blocks(2, 0, o_near[2], o_far[2])
     out = output(att, tokens, *group(early), nz, nr, bs)
     late += blocks(2, 1, over(o_near[2], 1, att), over(o_far[2], 1, att))

time: 121 us -> 109 us (0.901)
  Pallas kernels: 29.7 us -> 24.6 us
  local copies, waits for them, and re-layouts: 4.99 us -> 1.24 us
  starting transfers between devices: 19.8 us -> 17.6 us
  waiting for transfers between devices: 61.1 us -> 63.1 us
  other arithmetic: 3.02 us -> 1.1 us
    ppermute x6, waiting for transfers between devices: 42 us -> 46.4 us  [ring(): return lax.ppermute(v, 'z', [(i, (i + 1) % nz) for i in range(nz)])]
    pallas_call x2, Pallas kernels: 10.5 us -> 6.85 us  [output(): pl.pallas_call(functools.partial(out_kernel, plan=plan, nz=nz, nr=nr, bs=...]
    ppermute x21 -> x19, starting transfers between devices: 14.6 us -> 12.1 us  [swap(): return lax.ppermute(v, axis, [(0, 1), (1, 0)])]
    dynamic_slice x2 -> x0, local copies, waits for them, and re-layouts: 2.18 us -> none  [the longest x1 1.12 us: body(): o_else = lax.dynamic_slice_in_dim(own_o, (1 - y) * ohalf, ohalf)]
    ppermute x1, waiting for transfers between devices: 2.84 us -> 0.83 us  [body(): corner = lax.ppermute(toks[3], ('x', 'c'), [(i, i ^ 3) for i in range(4)])]
    pallas_call x1 -> x3, Pallas kernels: 5.16 us -> 7.04 us  [the longest x1 5.01 us: normalise(): pl.pallas_call(functools.partial(norm_kernel, nz=nz, nr=nr, bs=bs, block=...]
    pallas_call x1, Pallas kernels: 5.63 us -> 3.91 us  [project(): pl.pallas_call(functools.partial(project_kernel, halves=halves), in_specs...]
    pallas_call x1, Pallas kernels: 8.45 us -> 6.76 us  [attend(): pl.pallas_call(functools.partial(attend_kernel, heads=heads, head=head, n...]
  transfers between devices with their start and end apart: 28 -> 26, of which waited for: 12 -> 12; matrix products, arithmetic and copies ran while one was open for 2% -> 1% of each run, Pallas kernels for 21% -> 18%
where the time goes in v3:
time: 109 us
  waiting for transfers between devices  63.1 us (58%)
  Pallas kernels  24.6 us (23%)
  starting transfers between devices  17.6 us (16%)
  local copies, waits for them, and re-layouts  1.24 us (1%)
  other arithmetic  1.1 us (1%)
    ppermute x6, waiting for transfers between devices, ring(): return lax.ppermute(v, 'z', [(i, (i + 1) % nz) for i in range(nz)])  46.4 us
    ppermute x19, waiting for transfers between devices, swap(): return lax.ppermute(v, axis, [(0, 1), (1, 0)])  15.9 us
    ppermute x19, starting transfers between devices, swap(): return lax.ppermute(v, axis, [(0, 1), (1, 0)])  12.1 us
    pallas_call x2, Pallas kernels, output(): pl.pallas_call(functools.partial(out_kernel, plan=plan, nz=nz, nr=nr, bs=...  6.85 us
    pallas_call x1, Pallas kernels, attend(): pl.pallas_call(functools.partial(attend_kernel, heads=heads, head=head, n...  6.76 us
    ppermute x6, starting transfers between devices, ring(): return lax.ppermute(v, 'z', [(i, (i + 1) % nz) for i in range(nz)])  5.5 us
    pallas_call x1, Pallas kernels, normalise(): pl.pallas_call(functools.partial(norm_kernel, nz=nz, nr=nr, bs=bs, block=...  5.01 us
    pallas_call x1, Pallas kernels, project(): pl.pallas_call(functools.partial(project_kernel, halves=halves), in_specs...  3.91 us
  transfers between devices with their start and end apart: 26, of which 12 were waited for; matrix products, arithmetic and copies ran while one was open for 1% of the time, Pallas kernels for 18%

profile of v3, /device:TPU:0, one launch (start us, length us, event | category | flops | bytes accessed | tf_op | source)
XLA Modules:
  0.0 108.6 jit_solution(5516938277058766999)
XLA Ops:
  0.0 2.0 %pick.1 = bf16[512,512]{1,0:T(8,128)(2,1)} custom-call(bf16[1024,256]{1,0:T(8,128)(2,1)} %refs_4_.2, bf16[1024,256]{1,0:T(8,128)(2,1)} %refs_5_.1), custom_call_target="tpu_custom_call" | custom-call | bytes 1048576 | tf_op jit(solution)/shard_map/pick/pallas_call | solution.py:42
  2.0 3.1 %collective-permute-start.5 = (bf16[512,512]{1,0:T(8,128)(2,1)}, bf16[512,512]{1,0:T(8,128)(2,1)}, u32[]{:S(2)}, u32[]{:S(2)}) collective-permute-start(bf16[512,512]{1,0:T(8,128)(2,1)} %pick.1), channel_id=1, source_target_pairs={{0,4},{4,8},{8,12},{12,0},{1,5},{5,9},{9,13},{13,1},{2,6},{6,10},{... | collective-permute-start | bytes 1572872 | tf_op jit(solution)/shard_map/Zw1/ppermute | solution.py:377
  5.1 1.5 %collective-permute-start.3 = (bf16[256,1024]{1,0:T(8,128)(2,1)}, bf16[256,1024]{1,0:T(8,128)(2,1)S(1)}, u32[]{:S(2)}, u32[]{:S(2)}) collective-permute-start(bf16[256,1024]{1,0:T(8,128)(2,1)} %refs_0_.5), channel_id=1, source_target_pairs={{0,2},{2,0},{1,3},{3,1},{4,6},{6,4},{5,7},{7,5},{8,10},{10,8},{9,1... | collective-permute-start | bytes 1572872 | tf_op jit(solution)/shard_map/Ox/ppermute | solution.py:374
  6.6 5.0 %norm.1 = (bf16[128,4096]{1,0:T(8,128)(2,1)}, bf16[128,4096]{1,0:T(8,128)(2,1)}, bf16[128,4096]{1,0:T(8,128)(2,1)}, bf16[128,4096]{1,0:T(8,128)(2,1)}) custom-call(bf16[128,16384]{1,0:T(8,128)(2,1)} %tok.3, f32[1,16384]{1,0:T(1,128)} %bitcast.9), custom_call_target="tpu_custom_call" | custom-call | flops 16777216 | bytes 2097152 | tf_op jit(solution)/shard_map/norm/pallas_call | solution.py:92
  11.6 0.6 collective-permute-start
  12.2 0.5 collective-permute-start.1
  12.7 6.6 %collective-permute-done.5.refs_6_ = bf16[512,512]{1,0:T(8,128)(2,1)} collective-permute-done((bf16[512,512]{1,0:T(8,128)(2,1)}, bf16[512,512]{1,0:T(8,128)(2,1)}, u32[]{:S(2)}, u32[]{:S(2)}) %collective-permute-start.5) | collective-permute-done | bytes 524320 | tf_op jit(solution)/shard_map/Zw1/ppermute | solution.py:377
  19.3 0.6 fusion.2
  20.6 1.6 %collective-permute-start.6 = (bf16[512,512]{1,0:T(8,128)(2,1)}, bf16[512,512]{1,0:T(8,128)(2,1)S(1)}, u32[]{:S(2)}, u32[]{:S(2)}) collective-permute-start(bf16[512,512]{1,0:T(8,128)(2,1)} %collective-permute-done.5.refs_6_), channel_id=1, source_target_pairs={{0,16},{16,0},{1,17},{17,1},{2,18},{18,2},{3,19},{19,3},{4,20},{20... | collective-permute-start | bytes 1572872 | tf_op jit(solution)/shard_map/Yw1/ppermute | solution.py:374
  22.7 13.1 %collective-permute-done.7.refs_8_ = bf16[512,512]{1,0:T(8,128)(2,1)S(1)} collective-permute-done((bf16[512,512]{1,0:T(8,128)(2,1)}, bf16[512,512]{1,0:T(8,128)(2,1)S(1)}, u32[]{:S(2)}, u32[]{:S(2)}) %collective-permute-start.7) | collective-permute-done | bytes 524320 | tf_op jit(solution)/shard_map/Zw2/ppermute | solution.py:377
  35.8 1.3 %collective-permute-start.8 = (bf16[512,512]{1,0:T(8,128)(2,1)S(1)}, bf16[512,512]{1,0:T(8,128)(2,1)S(1)}, u32[]{:S(2)}, u32[]{:S(2)}) collective-permute-start(bf16[512,512]{1,0:T(8,128)(2,1)S(1)} %collective-permute-done.7.refs_8_), channel_id=1, source_target_pairs={{0,16},{16,0},{1,17},{17,1},{2,18},{18,2},{3,19},{19,3},{4,20},{20... | collective-permute-start | bytes 1572872 | tf_op jit(solution)/shard_map/Yw2/ppermute | solution.py:374
  37.2 4.8 %collective-permute-done.1.refs_2_ = bf16[128,4096]{1,0:T(8,128)(2,1)} collective-permute-done((bf16[128,4096]{1,0:T(8,128)(2,1)}, bf16[128,4096]{1,0:T(8,128)(2,1)}, u32[]{:S(2)}, u32[]{:S(2)}) %collective-permute-start.1) | collective-permute-done | bytes 1048608 | tf_op jit(solution)/shard_map/Tx/ppermute | solution.py:374
  42.0 2.3 %collective-permute-start.4 = (bf16[2,128,1024]{2,1,0:T(8,128)(2,1)S(1)}, bf16[2,128,1024]{2,1,0:T(8,128)(2,1)S(1)}, u32[]{:S(2)}, u32[]{:S(2)}) collective-permute-start(bf16[2,128,1024]{2,1,0:T(8,128)(2,1)S(1)} %pair.1), channel_id=1, source_target_pairs={{0,4},{4,8},{8,12},{12,0},{1,5},{5,9},{9,13},{13,1},{2,6},{6,10},{... | collective-permute-start | bytes 1572872 | tf_op jit(solution)/shard_map/Zo1/ppermute | solution.py:377
  44.3 8.1 %collective-permute-done.11.refs_10_ = bf16[512,512]{1,0:T(8,128)(2,1)S(1)} collective-permute-done((bf16[512,512]{1,0:T(8,128)(2,1)S(1)}, bf16[512,512]{1,0:T(8,128)(2,1)S(1)}, u32[]{:S(2)}, u32[]{:S(2)}) %collective-permute-start.11) | collective-permute-done | bytes 524320 | tf_op jit(solution)/shard_map/Zw3/ppermute | solution.py:377
  52.4 1.3 %collective-permute-start.12 = (bf16[512,512]{1,0:T(8,128)(2,1)S(1)}, bf16[512,512]{1,0:T(8,128)(2,1)S(1)}, u32[]{:S(2)}, u32[]{:S(2)}) collective-permute-start(bf16[512,512]{1,0:T(8,128)(2,1)S(1)} %collective-permute-done.11.refs_10_), channel_id=1, source_target_pairs={{0,16},{16,0},{1,17},{17,1},{2,18},{18,2},{3,19},{19,3},{4,20},{20... | collective-permute-start | bytes 1572872 | tf_op jit(solution)/shard_map/Yw3/ppermute | solution.py:374
  53.7 7.3 %collective-permute-done.4.refs_4_ = bf16[2,128,1024]{2,1,0:T(8,128)(2,1)S(1)} collective-permute-done((bf16[2,128,1024]{2,1,0:T(8,128)(2,1)S(1)}, bf16[2,128,1024]{2,1,0:T(8,128)(2,1)S(1)}, u32[]{:S(2)}, u32[]{:S(2)}) %collective-permute-start.4) | collective-permute-done | bytes 524320 | tf_op jit(solution)/shard_map/Zo1/ppermute | solution.py:377
  61.0 1.0 collective-permute-start.14
  62.0 0.8 collective-permute-done.2.refs_3_
  62.9 1.2 %copy-done.5 = bf16[128,4096]{1,0:T(8,128)(2,1)S(1)} copy-done((bf16[128,4096]{1,0:T(8,128)(2,1)S(1)}, bf16[128,4096]{1,0:T(8,128)(2,1)}, u32[]{:S(2)}) %copy-start.5) | copy-done | bytes 1048600
  64.1 3.9 %project.1 = (f32[128,512]{1,0:T(8,128)S(1)}, f32[2,128,512]{2,1,0:T(8,128)S(1)}, f32[128,512]{1,0:T(8,128)S(1)}) custom-call(bf16[128,4096]{1,0:T(8,128)(2,1)S(1)} %copy-done.5, bf16[128,4096]{1,0:T(8,128)(2,1)S(1)} %collective-permute-done.refs_1_, bf16[128,4096]{1,0:T(8,128)(2,1)} %collective-permute-done.1.refs_2_, ...), custom_call_target="tpu_custom_call" | custom-call | flops 2147483648 | bytes 2097152 | tf_op jit(solution)/shard_map/project/pallas_call | solution.py:159
  68.0 6.0 %collective-permute-done.13.refs_8_ = bf16[2,128,1024]{2,1,0:T(8,128)(2,1)S(1)} collective-permute-done((bf16[2,128,1024]{2,1,0:T(8,128)(2,1)S(1)}, bf16[2,128,1024]{2,1,0:T(8,128)(2,1)S(1)}, u32[]{:S(2)}, u32[]{:S(2)}) %collective-permute-start.13) | collective-permute-done | bytes 524320 | tf_op jit(solution)/shard_map/Zo2/ppermute | solution.py:377
  74.1 1.9 %collective-permute-done.15.refs_1_ = f32[2,128,512]{2,1,0:T(8,128)S(1)} collective-permute-done((f32[2,128,512]{2,1,0:T(8,128)S(1)}, f32[2,128,512]{2,1,0:T(8,128)S(1)}, u32[]{:S(2)}, u32[]{:S(2)}) %collective-permute-start.15) | collective-permute-done | bytes 524320 | tf_op jit(solution)/shard_map/Pc/ppermute | solution.py:374
  76.0 0.8 collective-permute-start.16
  76.8 1.5 %collective-permute-start.19 = (bf16[2,128,1024]{2,1,0:T(8,128)(2,1)S(1)}, bf16[2,128,1024]{2,1,0:T(8,128)(2,1)S(1)}, u32[]{:S(2)}, u32[]{:S(2)}) collective-permute-start(bf16[2,128,1024]{2,1,0:T(8,128)(2,1)S(1)} %collective-permute-done.13.refs_8_), channel_id=1, source_target_pairs={{0,16},{16,0},{1,17},{17,1},{2,18},{18,2},{3,19},{19,3},{4,20},{20... | collective-permute-start | bytes 1572872 | tf_op jit(solution)/shard_map/Yo2/ppermute | solution.py:374
  78.4 6.1 %collective-permute-done.16.refs_2_ = f32[128,512]{1,0:T(8,128)S(1)} collective-permute-done((f32[128,512]{1,0:T(8,128)S(1)}, f32[128,512]{1,0:T(8,128)S(1)}, u32[]{:S(2)}, u32[]{:S(2)}) %collective-permute-start.16) | collective-permute-done | bytes 262176 | tf_op jit(solution)/shard_map/Px/ppermute | solution.py:374
  84.9 5.3 %collective-permute-done.17.refs_2_ = bf16[2,128,1024]{2,1,0:T(8,128)(2,1)S(1)} collective-permute-done((bf16[2,128,1024]{2,1,0:T(8,128)(2,1)S(1)}, bf16[2,128,1024]{2,1,0:T(8,128)(2,1)S(1)}, u32[]{:S(2)}, u32[]{:S(2)}) %collective-permute-start.17) | collective-permute-done | bytes 524320 | tf_op jit(solution)/shard_map/Zo3/ppermute | solution.py:377
  90.2 0.8 collective-permute-start.21
  91.0 6.8 %attend.1.att = bf16[128,256]{1,0:T(8,128)(2,1)S(1)} custom-call(s32[16]{0:T(128)S(1)} %copy-done.6, f32[128,512]{1,0:T(8,128)S(1)} %get-tuple-element.36.refs_0_, f32[2,128,512]{2,1,0:T(8,128)S(1)} %collective-permute-done.15.refs_1_, f32[128,512]{1,0:T(8,128)S(1)} %collective-permute-done.16.refs_2_, f32[2,128,128]{2,1,0:T(8,128)S(1)} %pad_maximum_fusion.refs_3_, ...), custom_call_target="tpu_custom_call" | custom-call | flops 1073741824 | bytes 29360128 | tf_op jit(solution)/shard_map/attend/pallas_call | solution.py:246
  98.4 4.1 %output.2.refs_6_ = bf16[128,16384]{1,0:T(8,128)(2,1)} custom-call(bf16[128,256]{1,0:T(8,128)(2,1)S(1)} %attend.1.att, bf16[128,16384]{1,0:T(8,128)(2,1)S(1)} %copy-done, bf16[256,1024]{1,0:T(8,128)(2,1)S(1)} %copy-done.4, bf16[256,1024]{1,0:T(8,128)(2,1)S(1)} %collective-permute-done.3.refs_1_, bf16[256,1024]{1,0:T(8,128)(2,1)} %collective-permute-done.9.refs_2_, ...), custom_call_target="tpu_custom_call" | custom-call | flops 671088640 | bytes 10485760 | tf_op jit(solution)/shard_map/output/pallas_call | solution.py:332
  102.6 1.2 %collective-permute-done.21.refs_3_ = bf16[2,128,1024]{2,1,0:T(8,128)(2,1)S(1)} collective-permute-done((bf16[2,128,1024]{2,1,0:T(8,128)(2,1)S(1)}, bf16[2,128,1024]{2,1,0:T(8,128)(2,1)S(1)}, u32[]{:S(2)}, u32[]{:S(2)}) %collective-permute-start.21) | collective-permute-done | bytes 524320 | tf_op jit(solution)/shard_map/Yo3/ppermute | solution.py:374
  103.8 1.9 %collective-permute-done.25.refs_5_ = bf16[2,128,1024]{2,1,0:T(8,128)(2,1)S(1)} collective-permute-done((bf16[2,128,1024]{2,1,0:T(8,128)(2,1)S(1)}, bf16[2,128,1024]{2,1,0:T(8,128)(2,1)S(1)}, u32[]{:S(2)}, u32[]{:S(2)}) %collective-permute-start.25) | collective-permute-done | bytes 524320 | tf_op jit(solution)/shard_map/Oc/ppermute | solution.py:374
  105.7 2.7 %output.3 = bf16[128,16384]{1,0:T(8,128)(2,1)} custom-call(bf16[128,256]{1,0:T(8,128)(2,1)S(1)} %attend.1.att, bf16[128,16384]{1,0:T(8,128)(2,1)S(1)} %copy-done, bf16[2,128,1024]{2,1,0:T(8,128)(2,1)S(1)} %collective-permute-done.18.refs_0_, bf16[2,128,1024]{2,1,0:T(8,128)(2,1)S(1)} %collective-permute-done.20.refs_1_, ...), custom_call_target="tpu_custom_call", output_to_operand_aliasing={{}: (8, {})} | custom-call | flops 402653184 | bytes 6291456 | tf_op jit(solution)/shard_map/output/pallas_call | solution.py:332
  (48 shorter events, 1.9 us)
Async XLA Ops:
  0.0 62.9 %copy-start.3 = (bf16[1024,256]{1,0:T(8,128)(2,1)S(1)}, bf16[1024,256]{1,0:T(8,128)(2,1)}, u32[]{:S(2)}) copy-start(bf16[1024,256]{1,0:T(8,128)(2,1)} %refs_5_.1) | copy-start | bytes 1572868
  0.0 62.9 %copy-start.2 = (bf16[1024,256]{1,0:T(8,128)(2,1)S(1)}, bf16[1024,256]{1,0:T(8,128)(2,1)}, u32[]{:S(2)}) copy-start(bf16[1024,256]{1,0:T(8,128)(2,1)} %refs_4_.2) | copy-start | bytes 1572868
  0.0 37.1 %copy-start.4 = (bf16[256,1024]{1,0:T(8,128)(2,1)S(1)}, bf16[256,1024]{1,0:T(8,128)(2,1)}, u32[]{:S(2)}) copy-start(bf16[256,1024]{1,0:T(8,128)(2,1)} %refs_0_.5) | copy-start | bytes 1572868
  0.0 19.3 %copy-start.6 = (s32[16]{0:T(128)S(1)}, s32[16]{0:T(128)}, u32[]{:S(2)}) copy-start(s32[16]{0:T(128)} %lens.1) | copy-start | bytes 196
  2.0 17.3 %collective-permute-start.5 = (bf16[512,512]{1,0:T(8,128)(2,1)}, bf16[512,512]{1,0:T(8,128)(2,1)}, u32[]{:S(2)}, u32[]{:S(2)}) collective-permute-start(bf16[512,512]{1,0:T(8,128)(2,1)} %pick.1), channel_id=1, source_target_pairs={{0,4},{4,8},{8,12},{12,0},{1,5},{5,9},{9,13},{13,1},{2,6},{6,10},{... | collective-permute-start | bytes 1572872 | tf_op jit(solution)/shard_map/Zw1/ppermute | solution.py:377
  5.1 15.5 %collective-permute-start.3 = (bf16[256,1024]{1,0:T(8,128)(2,1)}, bf16[256,1024]{1,0:T(8,128)(2,1)S(1)}, u32[]{:S(2)}, u32[]{:S(2)}) collective-permute-start(bf16[256,1024]{1,0:T(8,128)(2,1)} %refs_0_.5), channel_id=1, source_target_pairs={{0,2},{2,0},{1,3},{3,1},{4,6},{6,4},{5,7},{7,5},{8,10},{10,8},{9,1... | collective-permute-start | bytes 1572872 | tf_op jit(solution)/shard_map/Ox/ppermute | solution.py:374
  6.6 15.6 %collective-permute-start.9 = (bf16[256,1024]{1,0:T(8,128)(2,1)}, bf16[256,1024]{1,0:T(8,128)(2,1)}, u32[]{:S(2)}, u32[]{:S(2)}) collective-permute-start(bf16[256,1024]{1,0:T(8,128)(2,1)} %refs_0_.5), channel_id=1, source_target_pairs={{0,1},{1,0},{2,3},{3,2},{4,5},{5,4},{6,7},{7,6},{8,9},{9,8},{10,11... | collective-permute-start | bytes 1572872 | tf_op jit(solution)/shard_map/Oc0/ppermute | solution.py:374
  11.6 24.1 %collective-permute-start = (bf16[128,4096]{1,0:T(8,128)(2,1)}, bf16[128,4096]{1,0:T(8,128)(2,1)S(1)}, u32[]{:S(2)}, u32[]{:S(2)}) collective-permute-start(bf16[128,4096]{1,0:T(8,128)(2,1)} %get-tuple-element.28), channel_id=1, source_target_pairs={{0,1},{1,0},{2,3},{3,2},{4,5},{5,4},{6,7},{7,6},{8,9},{9,8},{10,11... | collective-permute-start | bytes 3145736 | tf_op jit(solution)/shard_map/Tc/ppermute | solution.py:374
  12.2 29.8 %collective-permute-start.1 = (bf16[128,4096]{1,0:T(8,128)(2,1)}, bf16[128,4096]{1,0:T(8,128)(2,1)}, u32[]{:S(2)}, u32[]{:S(2)}) collective-permute-start(bf16[128,4096]{1,0:T(8,128)(2,1)} %get-tuple-element.29), channel_id=1, source_target_pairs={{0,2},{2,0},{1,3},{3,1},{4,6},{6,4},{5,7},{7,5},{8,10},{10,8},{9,1... | collective-permute-start | bytes 3145736 | tf_op jit(solution)/shard_map/Tx/ppermute | solution.py:374
  20.5 15.2 %collective-permute-start.7 = (bf16[512,512]{1,0:T(8,128)(2,1)}, bf16[512,512]{1,0:T(8,128)(2,1)S(1)}, u32[]{:S(2)}, u32[]{:S(2)}) collective-permute-start(bf16[512,512]{1,0:T(8,128)(2,1)} %collective-permute-done.5.refs_6_), channel_id=1, source_target_pairs={{0,4},{4,8},{8,12},{12,0},{1,5},{5,9},{9,13},{13,1},{2,6},{6,10},{... | collective-permute-start | bytes 1572872 | tf_op jit(solution)/shard_map/Zw2/ppermute | solution.py:377
  20.6 15.1 %collective-permute-start.6 = (bf16[512,512]{1,0:T(8,128)(2,1)}, bf16[512,512]{1,0:T(8,128)(2,1)S(1)}, u32[]{:S(2)}, u32[]{:S(2)}) collective-permute-start(bf16[512,512]{1,0:T(8,128)(2,1)} %collective-permute-done.5.refs_6_), channel_id=1, source_target_pairs={{0,16},{16,0},{1,17},{17,1},{2,18},{18,2},{3,19},{19,3},{4,20},{20... | collective-permute-start | bytes 1572872 | tf_op jit(solution)/shard_map/Yw1/ppermute | solution.py:374
  22.2 13.5 %collective-permute-start.10 = (bf16[256,1024]{1,0:T(8,128)(2,1)S(1)}, bf16[256,1024]{1,0:T(8,128)(2,1)S(1)}, u32[]{:S(2)}, u32[]{:S(2)}) collective-permute-start(bf16[256,1024]{1,0:T(8,128)(2,1)S(1)} %collective-permute-done.3.refs_1_), channel_id=1, source_target_pairs={{0,1},{1,0},{2,3},{3,2},{4,5},{5,4},{6,7},{7,6},{8,9},{9,8},{10,11... | collective-permute-start | bytes 1572872 | tf_op jit(solution)/shard_map/Oc0/ppermute | solution.py:374
  35.7 16.7 %collective-permute-start.11 = (bf16[512,512]{1,0:T(8,128)(2,1)S(1)}, bf16[512,512]{1,0:T(8,128)(2,1)S(1)}, u32[]{:S(2)}, u32[]{:S(2)}) collective-permute-start(bf16[512,512]{1,0:T(8,128)(2,1)S(1)} %collective-permute-done.7.refs_8_), channel_id=1, source_target_pairs={{0,4},{4,8},{8,12},{12,0},{1,5},{5,9},{9,13},{13,1},{2,6},{6,10},{... | collective-permute-start | bytes 1572872 | tf_op jit(solution)/shard_map/Zw3/ppermute | solution.py:377
  35.8 16.6 %collective-permute-start.8 = (bf16[512,512]{1,0:T(8,128)(2,1)S(1)}, bf16[512,512]{1,0:T(8,128)(2,1)S(1)}, u32[]{:S(2)}, u32[]{:S(2)}) collective-permute-start(bf16[512,512]{1,0:T(8,128)(2,1)S(1)} %collective-permute-done.7.refs_8_), channel_id=1, source_target_pairs={{0,16},{16,0},{1,17},{17,1},{2,18},{18,2},{3,19},{19,3},{4,20},{20... | collective-permute-start | bytes 1572872 | tf_op jit(solution)/shard_map/Yw2/ppermute | solution.py:374
  37.1 25.7 %collective-permute-start.2 = (bf16[128,4096]{1,0:T(8,128)(2,1)}, bf16[128,4096]{1,0:T(8,128)(2,1)S(1)}, u32[]{:S(2)}, u32[]{:S(2)}) collective-permute-start(bf16[128,4096]{1,0:T(8,128)(2,1)} %get-tuple-element.30), channel_id=1, source_target_pairs={{0,3},{1,2},{2,1},{3,0},{4,7},{5,6},{6,5},{7,4},{8,11},{9,10},{10,... | collective-permute-start | bytes 3145736 | tf_op jit(solution)/shard_map/Txc/ppermute | solution.py:417
  42.0 19.0 %collective-permute-start.4 = (bf16[2,128,1024]{2,1,0:T(8,128)(2,1)S(1)}, bf16[2,128,1024]{2,1,0:T(8,128)(2,1)S(1)}, u32[]{:S(2)}, u32[]{:S(2)}) collective-permute-start(bf16[2,128,1024]{2,1,0:T(8,128)(2,1)S(1)} %pair.1), channel_id=1, source_target_pairs={{0,4},{4,8},{8,12},{12,0},{1,5},{5,9},{9,13},{13,1},{2,6},{6,10},{... | collective-permute-start | bytes 1572872 | tf_op jit(solution)/shard_map/Zo1/ppermute | solution.py:377
  52.4 10.4 %collective-permute-start.12 = (bf16[512,512]{1,0:T(8,128)(2,1)S(1)}, bf16[512,512]{1,0:T(8,128)(2,1)S(1)}, u32[]{:S(2)}, u32[]{:S(2)}) collective-permute-start(bf16[512,512]{1,0:T(8,128)(2,1)S(1)} %collective-permute-done.11.refs_10_), channel_id=1, source_target_pairs={{0,16},{16,0},{1,17},{17,1},{2,18},{18,2},{3,19},{19,3},{4,20},{20... | collective-permute-start | bytes 1572872 | tf_op jit(solution)/shard_map/Yw3/ppermute | solution.py:374
  61.0 13.1 %collective-permute-start.13 = (bf16[2,128,1024]{2,1,0:T(8,128)(2,1)S(1)}, bf16[2,128,1024]{2,1,0:T(8,128)(2,1)S(1)}, u32[]{:S(2)}, u32[]{:S(2)}) collective-permute-start(bf16[2,128,1024]{2,1,0:T(8,128)(2,1)S(1)} %collective-permute-done.4.refs_4_), channel_id=1, source_target_pairs={{0,4},{4,8},{8,12},{12,0},{1,5},{5,9},{9,13},{13,1},{2,6},{6,10},{... | collective-permute-start | bytes 1572872 | tf_op jit(solution)/shard_map/Zo2/ppermute | solution.py:377
  61.0 13.1 %collective-permute-start.14 = (bf16[2,128,1024]{2,1,0:T(8,128)(2,1)S(1)}, bf16[2,128,1024]{2,1,0:T(8,128)(2,1)S(1)}, u32[]{:S(2)}, u32[]{:S(2)}) collective-permute-start(bf16[2,128,1024]{2,1,0:T(8,128)(2,1)S(1)} %collective-permute-done.4.refs_4_), channel_id=1, source_target_pairs={{0,16},{16,0},{1,17},{17,1},{2,18},{18,2},{3,19},{19,3},{4,20},{20... | collective-permute-start | bytes 1572872 | tf_op jit(solution)/shard_map/Yo1/ppermute | solution.py:374
  64.1 26.9 %copy-start.1 = (bf16[1,8192,256]{2,1,0:T(8,128)(2,1)S(1)}, bf16[1,8192,256]{2,1,0:T(8,128)(2,1)}, u32[]{:S(2)}) copy-start(bf16[1,8192,256]{2,1,0:T(8,128)(2,1)} %refs_4_.3) | copy-start | bytes 12582916
  68.0 30.4 %copy-start = (bf16[128,16384]{1,0:T(8,128)(2,1)S(1)}, bf16[128,16384]{1,0:T(8,128)(2,1)}, u32[]{:S(2)}) copy-start(bf16[128,16384]{1,0:T(8,128)(2,1)} %tok.3) | copy-start | bytes 12582916
  74.1 1.9 %collective-permute-start.15 = (f32[2,128,512]{2,1,0:T(8,128)S(1)}, f32[2,128,512]{2,1,0:T(8,128)S(1)}, u32[]{:S(2)}, u32[]{:S(2)}) collective-permute-start(f32[2,128,512]{2,1,0:T(8,128)S(1)} %get-tuple-element.38), channel_id=1, source_target_pairs={{0,1},{1,0},{2,3},{3,2},{4,5},{5,4},{6,7},{7,6},{8,9},{9,8},{10,11... | collective-permute-start | bytes 1572872 | tf_op jit(solution)/shard_map/Pc/ppermute | solution.py:374
  74.1 16.1 %collective-permute-start.17 = (bf16[2,128,1024]{2,1,0:T(8,128)(2,1)S(1)}, bf16[2,128,1024]{2,1,0:T(8,128)(2,1)S(1)}, u32[]{:S(2)}, u32[]{:S(2)}) collective-permute-start(bf16[2,128,1024]{2,1,0:T(8,128)(2,1)S(1)} %collective-permute-done.13.refs_8_), channel_id=1, source_target_pairs={{0,4},{4,8},{8,12},{12,0},{1,5},{5,9},{9,13},{13,1},{2,6},{6,10},{... | collective-permute-start | bytes 1572872 | tf_op jit(solution)/shard_map/Zo3/ppermute | solution.py:377
  76.0 8.4 %collective-permute-start.16 = (f32[128,512]{1,0:T(8,128)S(1)}, f32[128,512]{1,0:T(8,128)S(1)}, u32[]{:S(2)}, u32[]{:S(2)}) collective-permute-start(f32[128,512]{1,0:T(8,128)S(1)} %fusion), channel_id=1, source_target_pairs={{0,2},{2,0},{1,3},{3,1},{4,6},{6,4},{5,7},{7,5},{8,10},{10,8},{9,1... | collective-permute-start | bytes 786440 | tf_op jit(solution)/shard_map/Px/ppermute | solution.py:374
  76.8 21.0 %collective-permute-start.19 = (bf16[2,128,1024]{2,1,0:T(8,128)(2,1)S(1)}, bf16[2,128,1024]{2,1,0:T(8,128)(2,1)S(1)}, u32[]{:S(2)}, u32[]{:S(2)}) collective-permute-start(bf16[2,128,1024]{2,1,0:T(8,128)(2,1)S(1)} %collective-permute-done.13.refs_8_), channel_id=1, source_target_pairs={{0,16},{16,0},{1,17},{17,1},{2,18},{18,2},{3,19},{19,3},{4,20},{20... | collective-permute-start | bytes 1572872 | tf_op jit(solution)/shard_map/Yo2/ppermute | solution.py:374
  84.4 13.9 %collective-permute-start.24 = (bf16[2,128,1024]{2,1,0:T(8,128)(2,1)S(1)}, bf16[2,128,1024]{2,1,0:T(8,128)(2,1)S(1)}, u32[]{:S(2)}, u32[]{:S(2)}) collective-permute-start(bf16[2,128,1024]{2,1,0:T(8,128)(2,1)S(1)} %collective-permute-done.14.refs_5_), channel_id=1, source_target_pairs={{0,1},{1,0},{2,3},{3,2},{4,5},{5,4},{6,7},{7,6},{8,9},{9,8},{10,11... | collective-permute-start | bytes 1572872 | tf_op jit(solution)/shard_map/Oc1/ppermute | solution.py:374
  84.4 14.0 %collective-permute-start.23 = (bf16[2,128,1024]{2,1,0:T(8,128)(2,1)S(1)}, bf16[2,128,1024]{2,1,0:T(8,128)(2,1)S(1)}, u32[]{:S(2)}, u32[]{:S(2)}) collective-permute-start(bf16[2,128,1024]{2,1,0:T(8,128)(2,1)S(1)} %collective-permute-done.4.refs_4_), channel_id=1, source_target_pairs={{0,1},{1,0},{2,3},{3,2},{4,5},{5,4},{6,7},{7,6},{8,9},{9,8},{10,11... | collective-permute-start | bytes 1572872 | tf_op jit(solution)/shard_map/Oc1/ppermute | solution.py:374
  90.2 13.6 %collective-permute-start.21 = (bf16[2,128,1024]{2,1,0:T(8,128)(2,1)S(1)}, bf16[2,128,1024]{2,1,0:T(8,128)(2,1)S(1)}, u32[]{:S(2)}, u32[]{:S(2)}) collective-permute-start(bf16[2,128,1024]{2,1,0:T(8,128)(2,1)S(1)} %collective-permute-done.17.refs_2_), channel_id=1, source_target_pairs={{0,16},{16,0},{1,17},{17,1},{2,18},{18,2},{3,19},{19,3},{4,20},{20... | collective-permute-start | bytes 1572872 | tf_op jit(solution)/shard_map/Yo3/ppermute | solution.py:374
  97.8 6.0 %collective-permute-start.22 = (bf16[2,128,1024]{2,1,0:T(8,128)(2,1)S(1)}, bf16[2,128,1024]{2,1,0:T(8,128)(2,1)S(1)}, u32[]{:S(2)}, u32[]{:S(2)}) collective-permute-start(bf16[2,128,1024]{2,1,0:T(8,128)(2,1)S(1)} %collective-permute-done.17.refs_2_), channel_id=1, source_target_pairs={{0,1},{1,0},{2,3},{3,2},{4,5},{5,4},{6,7},{7,6},{8,9},{9,8},{10,11... | collective-permute-start | bytes 1572872 | tf_op jit(solution)/shard_map/Oc/ppermute | solution.py:374
  97.8 5.9 %collective-permute-start.20 = (bf16[2,128,1024]{2,1,0:T(8,128)(2,1)S(1)}, bf16[2,128,1024]{2,1,0:T(8,128)(2,1)S(1)}, u32[]{:S(2)}, u32[]{:S(2)}) collective-permute-start(bf16[2,128,1024]{2,1,0:T(8,128)(2,1)S(1)} %collective-permute-done.19.refs_9_), channel_id=1, source_target_pairs={{0,1},{1,0},{2,3},{3,2},{4,5},{5,4},{6,7},{7,6},{8,9},{9,8},{10,11... | collective-permute-start | bytes 1572872 | tf_op jit(solution)/shard_map/Oc/ppermute | solution.py:374
  98.3 5.4 %collective-permute-start.18 = (bf16[2,128,1024]{2,1,0:T(8,128)(2,1)S(1)}, bf16[2,128,1024]{2,1,0:T(8,128)(2,1)S(1)}, u32[]{:S(2)}, u32[]{:S(2)}) collective-permute-start(bf16[2,128,1024]{2,1,0:T(8,128)(2,1)S(1)} %collective-permute-done.13.refs_8_), channel_id=1, source_target_pairs={{0,1},{1,0},{2,3},{3,2},{4,5},{5,4},{6,7},{7,6},{8,9},{9,8},{10,11... | collective-permute-start | bytes 1572872 | tf_op jit(solution)/shard_map/Oc/ppermute | solution.py:374
  103.8 1.9 %collective-permute-start.25 = (bf16[2,128,1024]{2,1,0:T(8,128)(2,1)S(1)}, bf16[2,128,1024]{2,1,0:T(8,128)(2,1)S(1)}, u32[]{:S(2)}, u32[]{:S(2)}) collective-permute-start(bf16[2,128,1024]{2,1,0:T(8,128)(2,1)S(1)} %collective-permute-done.21.refs_3_), channel_id=1, source_target_pairs={{0,1},{1,0},{2,3},{3,2},{4,5},{5,4},{6,7},{7,6},{8,9},{9,8},{10,11... | collective-permute-start | bytes 1572872 | tf_op jit(solution)/shard_map/Oc/ppermute | solution.py:374
  (1 other events, 1.2 us)

commit v4 on v3

--- a/solution.py
+++ b/solution.py
@@ -460,8 +460,8 @@
     with jax.named_scope("Px"):
         other = swap(total, "x")
     o_near.append(step_z(o_near[2], "o3"))
-    for s in range(2, nz):
-        o_far.append(step_y(o_near[s], f"o{s}"))
+    o_far.append(step_y(o_near[2], "o2"))
+    last_far = [step_y(o_near[3][0], "o3"), step_z(o_far[2][1], "f3")]
     with jax.named_scope("Oc1"):
         near1_c = swap(tie(o_near[1], other), "c")
         far1_c = swap(tie(o_far[1], other), "c")
@@ -470,7 +470,7 @@
         cached_len,
         parts[0],
         from_c,
-        tie(other, o_near[3]),
+        tie(other, o_near[3], o_far[2]),
         turns,
         cache_kv,
         heads,
@@ -508,7 +508,9 @@
     out = output(att, tokens, *group(early), nz, nr, bs)
     late += blocks(2, 1, over(o_near[2], 1, att), over(o_far[2], 1, att))
     for dc in range(2):
-        late += blocks(3, dc, over(o_near[3], dc, att), over(o_far[3], dc, out))
+        near = over(o_near[3], dc, att)
+        for dx in range(2):
+            late.append(((3, dx, dc), [(near, dx, None), (over(last_far[dx], dc, att), None, None)]))
     return output(att, tokens, *group(late), nz, nr, bs, out)
 
 

time: 109 us -> 107 us (0.982)
  waiting for transfers between devices: 63.1 us -> 60.8 us
    ppermute x6 -> x7, waiting for transfers between devices: 46.4 us -> 42.7 us  [ring(): return lax.ppermute(v, 'z', [(i, (i + 1) % nz) for i in range(nz)])]
    ppermute x19 -> x20, waiting for transfers between devices: 15.9 us -> 17.3 us  [swap(): return lax.ppermute(v, axis, [(0, 1), (1, 0)])]
    ppermute x19 -> x20, starting transfers between devices: 12.1 us -> 12.5 us  [swap(): return lax.ppermute(v, axis, [(0, 1), (1, 0)])]
    ppermute x6 -> x7, starting transfers between devices: 5.5 us -> 5.84 us  [ring(): return lax.ppermute(v, 'z', [(i, (i + 1) % nz) for i in range(nz)])]
  transfers between devices with their start and end apart: 26 -> 28, of which waited for: 12 -> 10; matrix products, arithmetic and copies ran while one was open for 1% -> 1% of each run, Pallas kernels for 18% -> 19%
where the time goes in v4:
time: 107 us
  waiting for transfers between devices  60.8 us (57%)
  Pallas kernels  24.6 us (23%)
  starting transfers between devices  18.3 us (17%)
  local copies, waits for them, and re-layouts  1.28 us (1%)
  other arithmetic  1.13 us (1%)
    ppermute x7, waiting for transfers between devices, ring(): return lax.ppermute(v, 'z', [(i, (i + 1) % nz) for i in range(nz)])  42.7 us
    ppermute x20, waiting for transfers between devices, swap(): return lax.ppermute(v, axis, [(0, 1), (1, 0)])  17.3 us
    ppermute x20, starting transfers between devices, swap(): return lax.ppermute(v, axis, [(0, 1), (1, 0)])  12.5 us
    pallas_call x2, Pallas kernels, output(): pl.pallas_call(functools.partial(out_kernel, plan=plan, nz=nz, nr=nr, bs=...  6.87 us
    pallas_call x1, Pallas kernels, attend(): pl.pallas_call(functools.partial(attend_kernel, heads=heads, head=head, n...  6.77 us
    ppermute x7, starting transfers between devices, ring(): return lax.ppermute(v, 'z', [(i, (i + 1) % nz) for i in range(nz)])  5.84 us
    pallas_call x1, Pallas kernels, normalise(): pl.pallas_call(functools.partial(norm_kernel, nz=nz, nr=nr, bs=bs, block=...  5.02 us
    pallas_call x1, Pallas kernels, project(): pl.pallas_call(functools.partial(project_kernel, halves=halves), in_specs...  3.91 us
  transfers between devices with their start and end apart: 28, of which 10 were waited for; matrix products, arithmetic and copies ran while one was open for 1% of the time, Pallas kernels for 19%

profile of v4, /device:TPU:0, one launch (start us, length us, event | category | flops | bytes accessed | tf_op | source)
XLA Modules:
  0.0 107.2 jit_solution(17105419420665636760)
XLA Ops:
  0.0 2.0 %pick.1 = bf16[512,512]{1,0:T(8,128)(2,1)} custom-call(bf16[1024,256]{1,0:T(8,128)(2,1)} %refs_4_.2, bf16[1024,256]{1,0:T(8,128)(2,1)} %refs_5_.1), custom_call_target="tpu_custom_call" | custom-call | bytes 1048576 | tf_op jit(solution)/shard_map/pick/pallas_call | solution.py:42
  2.0 3.1 %collective-permute-start.5 = (bf16[512,512]{1,0:T(8,128)(2,1)}, bf16[512,512]{1,0:T(8,128)(2,1)}, u32[]{:S(2)}, u32[]{:S(2)}) collective-permute-start(bf16[512,512]{1,0:T(8,128)(2,1)} %pick.1), channel_id=1, source_target_pairs={{0,4},{4,8},{8,12},{12,0},{1,5},{5,9},{9,13},{13,1},{2,6},{6,10},{... | collective-permute-start | bytes 1572872 | tf_op jit(solution)/shard_map/Zw1/ppermute | solution.py:377
  5.1 1.5 %collective-permute-start.3 = (bf16[256,1024]{1,0:T(8,128)(2,1)}, bf16[256,1024]{1,0:T(8,128)(2,1)S(1)}, u32[]{:S(2)}, u32[]{:S(2)}) collective-permute-start(bf16[256,1024]{1,0:T(8,128)(2,1)} %refs_0_.5), channel_id=1, source_target_pairs={{0,2},{2,0},{1,3},{3,1},{4,6},{6,4},{5,7},{7,5},{8,10},{10,8},{9,1... | collective-permute-start | bytes 1572872 | tf_op jit(solution)/shard_map/Ox/ppermute | solution.py:374
  6.6 5.0 %norm.1 = (bf16[128,4096]{1,0:T(8,128)(2,1)}, bf16[128,4096]{1,0:T(8,128)(2,1)}, bf16[128,4096]{1,0:T(8,128)(2,1)}, bf16[128,4096]{1,0:T(8,128)(2,1)}) custom-call(bf16[128,16384]{1,0:T(8,128)(2,1)} %tok.3, f32[1,16384]{1,0:T(1,128)} %bitcast.13), custom_call_target="tpu_custom_call" | custom-call | flops 16777216 | bytes 2097152 | tf_op jit(solution)/shard_map/norm/pallas_call | solution.py:92
  11.6 0.6 collective-permute-start
  12.2 0.5 collective-permute-start.1
  12.7 6.6 %collective-permute-done.5.refs_6_ = bf16[512,512]{1,0:T(8,128)(2,1)} collective-permute-done((bf16[512,512]{1,0:T(8,128)(2,1)}, bf16[512,512]{1,0:T(8,128)(2,1)}, u32[]{:S(2)}, u32[]{:S(2)}) %collective-permute-start.5) | collective-permute-done | bytes 524320 | tf_op jit(solution)/shard_map/Zw1/ppermute | solution.py:377
  19.3 0.7 fusion.2
  20.7 1.6 %collective-permute-start.6 = (bf16[512,512]{1,0:T(8,128)(2,1)}, bf16[512,512]{1,0:T(8,128)(2,1)S(1)}, u32[]{:S(2)}, u32[]{:S(2)}) collective-permute-start(bf16[512,512]{1,0:T(8,128)(2,1)} %collective-permute-done.5.refs_6_), channel_id=1, source_target_pairs={{0,16},{16,0},{1,17},{17,1},{2,18},{18,2},{3,19},{19,3},{4,20},{20... | collective-permute-start | bytes 1572872 | tf_op jit(solution)/shard_map/Yw1/ppermute | solution.py:374
  22.8 13.1 %collective-permute-done.7.refs_8_ = bf16[512,512]{1,0:T(8,128)(2,1)S(1)} collective-permute-done((bf16[512,512]{1,0:T(8,128)(2,1)}, bf16[512,512]{1,0:T(8,128)(2,1)S(1)}, u32[]{:S(2)}, u32[]{:S(2)}) %collective-permute-start.7) | collective-permute-done | bytes 524320 | tf_op jit(solution)/shard_map/Zw2/ppermute | solution.py:377
  35.9 1.3 %collective-permute-start.8 = (bf16[512,512]{1,0:T(8,128)(2,1)S(1)}, bf16[512,512]{1,0:T(8,128)(2,1)S(1)}, u32[]{:S(2)}, u32[]{:S(2)}) collective-permute-start(bf16[512,512]{1,0:T(8,128)(2,1)S(1)} %collective-permute-done.7.refs_8_), channel_id=1, source_target_pairs={{0,16},{16,0},{1,17},{17,1},{2,18},{18,2},{3,19},{19,3},{4,20},{20... | collective-permute-start | bytes 1572872 | tf_op jit(solution)/shard_map/Yw2/ppermute | solution.py:374
  37.3 4.6 %collective-permute-done.1.refs_2_ = bf16[128,4096]{1,0:T(8,128)(2,1)} collective-permute-done((bf16[128,4096]{1,0:T(8,128)(2,1)}, bf16[128,4096]{1,0:T(8,128)(2,1)}, u32[]{:S(2)}, u32[]{:S(2)}) %collective-permute-start.1) | collective-permute-done | bytes 1048608 | tf_op jit(solution)/shard_map/Tx/ppermute | solution.py:374
  41.9 2.4 %collective-permute-start.4 = (bf16[2,128,1024]{2,1,0:T(8,128)(2,1)S(1)}, bf16[2,128,1024]{2,1,0:T(8,128)(2,1)S(1)}, u32[]{:S(2)}, u32[]{:S(2)}) collective-permute-start(bf16[2,128,1024]{2,1,0:T(8,128)(2,1)S(1)} %pair.1), channel_id=1, source_target_pairs={{0,4},{4,8},{8,12},{12,0},{1,5},{5,9},{9,13},{13,1},{2,6},{6,10},{... | collective-permute-start | bytes 1572872 | tf_op jit(solution)/shard_map/Zo1/ppermute | solution.py:377
  44.3 8.2 %collective-permute-done.11.refs_10_ = bf16[512,512]{1,0:T(8,128)(2,1)S(1)} collective-permute-done((bf16[512,512]{1,0:T(8,128)(2,1)S(1)}, bf16[512,512]{1,0:T(8,128)(2,1)S(1)}, u32[]{:S(2)}, u32[]{:S(2)}) %collective-permute-start.11) | collective-permute-done | bytes 524320 | tf_op jit(solution)/shard_map/Zw3/ppermute | solution.py:377
  52.5 1.3 %collective-permute-start.12 = (bf16[512,512]{1,0:T(8,128)(2,1)S(1)}, bf16[512,512]{1,0:T(8,128)(2,1)S(1)}, u32[]{:S(2)}, u32[]{:S(2)}) collective-permute-start(bf16[512,512]{1,0:T(8,128)(2,1)S(1)} %collective-permute-done.11.refs_10_), channel_id=1, source_target_pairs={{0,16},{16,0},{1,17},{17,1},{2,18},{18,2},{3,19},{19,3},{4,20},{20... | collective-permute-start | bytes 1572872 | tf_op jit(solution)/shard_map/Yw3/ppermute | solution.py:374
  53.8 7.3 %collective-permute-done.4.refs_4_ = bf16[2,128,1024]{2,1,0:T(8,128)(2,1)S(1)} collective-permute-done((bf16[2,128,1024]{2,1,0:T(8,128)(2,1)S(1)}, bf16[2,128,1024]{2,1,0:T(8,128)(2,1)S(1)}, u32[]{:S(2)}, u32[]{:S(2)}) %collective-permute-start.4) | collective-permute-done | bytes 524320 | tf_op jit(solution)/shard_map/Zo1/ppermute | solution.py:377
  61.1 1.0 collective-permute-start.14
  62.1 0.8 collective-permute-done.2.refs_3_
  63.0 1.2 %copy-done.5 = bf16[128,4096]{1,0:T(8,128)(2,1)S(1)} copy-done((bf16[128,4096]{1,0:T(8,128)(2,1)S(1)}, bf16[128,4096]{1,0:T(8,128)(2,1)}, u32[]{:S(2)}) %copy-start.5) | copy-done | bytes 1048600
  64.2 3.9 %project.1 = (f32[128,512]{1,0:T(8,128)S(1)}, f32[2,128,512]{2,1,0:T(8,128)S(1)}, f32[128,512]{1,0:T(8,128)S(1)}) custom-call(bf16[128,4096]{1,0:T(8,128)(2,1)S(1)} %copy-done.5, bf16[128,4096]{1,0:T(8,128)(2,1)S(1)} %collective-permute-done.refs_1_, bf16[128,4096]{1,0:T(8,128)(2,1)} %collective-permute-done.1.refs_2_, ...), custom_call_target="tpu_custom_call" | custom-call | flops 2147483648 | bytes 2097152 | tf_op jit(solution)/shard_map/project/pallas_call | solution.py:159
  68.1 6.0 %collective-permute-done.13.refs_8_ = bf16[2,128,1024]{2,1,0:T(8,128)(2,1)S(1)} collective-permute-done((bf16[2,128,1024]{2,1,0:T(8,128)(2,1)S(1)}, bf16[2,128,1024]{2,1,0:T(8,128)(2,1)S(1)}, u32[]{:S(2)}, u32[]{:S(2)}) %collective-permute-start.13) | collective-permute-done | bytes 524320 | tf_op jit(solution)/shard_map/Zo2/ppermute | solution.py:377
  74.2 0.8 collective-permute-start.18
  75.0 1.1 %collective-permute-done.15.refs_1_ = f32[2,128,512]{2,1,0:T(8,128)S(1)} collective-permute-done((f32[2,128,512]{2,1,0:T(8,128)S(1)}, f32[2,128,512]{2,1,0:T(8,128)S(1)}, u32[]{:S(2)}, u32[]{:S(2)}) %collective-permute-start.15) | collective-permute-done | bytes 524320 | tf_op jit(solution)/shard_map/Pc/ppermute | solution.py:374
  76.1 0.8 collective-permute-start.16
  76.9 11.6 %collective-permute-done.18.refs_9_ = bf16[2,128,1024]{2,1,0:T(8,128)(2,1)S(1)} collective-permute-done((bf16[2,128,1024]{2,1,0:T(8,128)(2,1)S(1)}, bf16[2,128,1024]{2,1,0:T(8,128)(2,1)S(1)}, u32[]{:S(2)}, u32[]{:S(2)}) %collective-permute-start.18) | collective-permute-done | bytes 524320 | tf_op jit(solution)/shard_map/Yo2/ppermute | solution.py:374
  88.9 0.5 collective-permute-start.26
  89.4 1.4 %collective-permute-done.17.refs_2_ = bf16[2,128,1024]{2,1,0:T(8,128)(2,1)S(1)} collective-permute-done((bf16[2,128,1024]{2,1,0:T(8,128)(2,1)S(1)}, bf16[2,128,1024]{2,1,0:T(8,128)(2,1)S(1)}, u32[]{:S(2)}, u32[]{:S(2)}) %collective-permute-start.17) | collective-permute-done | bytes 524320 | tf_op jit(solution)/shard_map/Zo3/ppermute | solution.py:377
  90.8 1.3 %collective-permute-start.21 = (bf16[128,1024]{1,0:T(8,128)(2,1)S(1)}, bf16[128,1024]{1,0:T(8,128)(2,1)S(1)}, u32[]{:S(2)}, u32[]{:S(2)}) collective-permute-start(bf16[128,1024]{1,0:T(8,128)(2,1)S(1)} %slice_bitcast_fusion.1), channel_id=1, source_target_pairs={{0,16},{16,0},{1,17},{17,1},{2,18},{18,2},{3,19},{19,3},{4,20},{20... | collective-permute-start | bytes 786440 | tf_op jit(solution)/shard_map/Yo3/ppermute | solution.py:374
  92.1 6.8 %attend.1.att = bf16[128,256]{1,0:T(8,128)(2,1)S(1)} custom-call(s32[16]{0:T(128)S(1)} %copy-done.6, f32[128,512]{1,0:T(8,128)S(1)} %get-tuple-element.37.refs_0_, f32[2,128,512]{2,1,0:T(8,128)S(1)} %collective-permute-done.15.refs_1_, f32[128,512]{1,0:T(8,128)S(1)} %collective-permute-done.16.refs_2_, f32[2,128,128]{2,1,0:T(8,128)S(1)} %pad_maximum_fusion.refs_3_, ...), custom_call_target="tpu_custom_call" | custom-call | flops 1073741824 | bytes 29360128 | tf_op jit(solution)/shard_map/attend/pallas_call | solution.py:246
  99.0 0.5 collective-permute-start.20
  100.1 4.1 %output.2.refs_8_ = bf16[128,16384]{1,0:T(8,128)(2,1)} custom-call(bf16[128,256]{1,0:T(8,128)(2,1)S(1)} %attend.1.att, bf16[128,16384]{1,0:T(8,128)(2,1)S(1)} %copy-done, bf16[256,1024]{1,0:T(8,128)(2,1)S(1)} %copy-done.4, bf16[256,1024]{1,0:T(8,128)(2,1)S(1)} %collective-permute-done.3.refs_1_, bf16[256,1024]{1,0:T(8,128)(2,1)} %collective-permute-done.9.refs_2_, ...), custom_call_target="tpu_custom_call" | custom-call | flops 671088640 | bytes 10485760 | tf_op jit(solution)/shard_map/output/pallas_call | solution.py:332
  104.3 2.7 %output.3 = bf16[128,16384]{1,0:T(8,128)(2,1)} custom-call(bf16[128,256]{1,0:T(8,128)(2,1)S(1)} %attend.1.att, bf16[128,16384]{1,0:T(8,128)(2,1)S(1)} %copy-done, bf16[2,128,1024]{2,1,0:T(8,128)(2,1)S(1)} %collective-permute-done.19.refs_0_, bf16[2,128,1024]{2,1,0:T(8,128)(2,1)S(1)} %collective-permute-done.20.refs_1_, ...), custom_call_target="tpu_custom_call", output_to_operand_aliasing={{}: (10, {})} | custom-call | flops 402653184 | bytes 6291456 | tf_op jit(solution)/shard_map/output/pallas_call | solution.py:332
  (54 shorter events, 1.8 us)
Async XLA Ops:
  0.0 63.0 %copy-start.3 = (bf16[1024,256]{1,0:T(8,128)(2,1)S(1)}, bf16[1024,256]{1,0:T(8,128)(2,1)}, u32[]{:S(2)}) copy-start(bf16[1024,256]{1,0:T(8,128)(2,1)} %refs_5_.1) | copy-start | bytes 1572868
  0.0 63.0 %copy-start.2 = (bf16[1024,256]{1,0:T(8,128)(2,1)S(1)}, bf16[1024,256]{1,0:T(8,128)(2,1)}, u32[]{:S(2)}) copy-start(bf16[1024,256]{1,0:T(8,128)(2,1)} %refs_4_.2) | copy-start | bytes 1572868
  0.0 37.2 %copy-start.4 = (bf16[256,1024]{1,0:T(8,128)(2,1)S(1)}, bf16[256,1024]{1,0:T(8,128)(2,1)}, u32[]{:S(2)}) copy-start(bf16[256,1024]{1,0:T(8,128)(2,1)} %refs_0_.5) | copy-start | bytes 1572868
  2.0 17.3 %collective-permute-start.5 = (bf16[512,512]{1,0:T(8,128)(2,1)}, bf16[512,512]{1,0:T(8,128)(2,1)}, u32[]{:S(2)}, u32[]{:S(2)}) collective-permute-start(bf16[512,512]{1,0:T(8,128)(2,1)} %pick.1), channel_id=1, source_target_pairs={{0,4},{4,8},{8,12},{12,0},{1,5},{5,9},{9,13},{13,1},{2,6},{6,10},{... | collective-permute-start | bytes 1572872 | tf_op jit(solution)/shard_map/Zw1/ppermute | solution.py:377
  5.1 15.6 %collective-permute-start.3 = (bf16[256,1024]{1,0:T(8,128)(2,1)}, bf16[256,1024]{1,0:T(8,128)(2,1)S(1)}, u32[]{:S(2)}, u32[]{:S(2)}) collective-permute-start(bf16[256,1024]{1,0:T(8,128)(2,1)} %refs_0_.5), channel_id=1, source_target_pairs={{0,2},{2,0},{1,3},{3,1},{4,6},{6,4},{5,7},{7,5},{8,10},{10,8},{9,1... | collective-permute-start | bytes 1572872 | tf_op jit(solution)/shard_map/Ox/ppermute | solution.py:374
  6.6 15.7 %collective-permute-start.9 = (bf16[256,1024]{1,0:T(8,128)(2,1)}, bf16[256,1024]{1,0:T(8,128)(2,1)}, u32[]{:S(2)}, u32[]{:S(2)}) collective-permute-start(bf16[256,1024]{1,0:T(8,128)(2,1)} %refs_0_.5), channel_id=1, source_target_pairs={{0,1},{1,0},{2,3},{3,2},{4,5},{5,4},{6,7},{7,6},{8,9},{9,8},{10,11... | collective-permute-start | bytes 1572872 | tf_op jit(solution)/shard_map/Oc0/ppermute | solution.py:374
  11.6 24.2 %collective-permute-start = (bf16[128,4096]{1,0:T(8,128)(2,1)}, bf16[128,4096]{1,0:T(8,128)(2,1)S(1)}, u32[]{:S(2)}, u32[]{:S(2)}) collective-permute-start(bf16[128,4096]{1,0:T(8,128)(2,1)} %get-tuple-element.29), channel_id=1, source_target_pairs={{0,1},{1,0},{2,3},{3,2},{4,5},{5,4},{6,7},{7,6},{8,9},{9,8},{10,11... | collective-permute-start | bytes 3145736 | tf_op jit(solution)/shard_map/Tc/ppermute | solution.py:374
  12.2 29.7 %collective-permute-start.1 = (bf16[128,4096]{1,0:T(8,128)(2,1)}, bf16[128,4096]{1,0:T(8,128)(2,1)}, u32[]{:S(2)}, u32[]{:S(2)}) collective-permute-start(bf16[128,4096]{1,0:T(8,128)(2,1)} %get-tuple-element.30), channel_id=1, source_target_pairs={{0,2},{2,0},{1,3},{3,1},{4,6},{6,4},{5,7},{7,5},{8,10},{10,8},{9,1... | collective-permute-start | bytes 3145736 | tf_op jit(solution)/shard_map/Tx/ppermute | solution.py:374
  20.6 15.2 %collective-permute-start.7 = (bf16[512,512]{1,0:T(8,128)(2,1)}, bf16[512,512]{1,0:T(8,128)(2,1)S(1)}, u32[]{:S(2)}, u32[]{:S(2)}) collective-permute-start(bf16[512,512]{1,0:T(8,128)(2,1)} %collective-permute-done.5.refs_6_), channel_id=1, source_target_pairs={{0,4},{4,8},{8,12},{12,0},{1,5},{5,9},{9,13},{13,1},{2,6},{6,10},{... | collective-permute-start | bytes 1572872 | tf_op jit(solution)/shard_map/Zw2/ppermute | solution.py:377
  20.7 15.1 %collective-permute-start.6 = (bf16[512,512]{1,0:T(8,128)(2,1)}, bf16[512,512]{1,0:T(8,128)(2,1)S(1)}, u32[]{:S(2)}, u32[]{:S(2)}) collective-permute-start(bf16[512,512]{1,0:T(8,128)(2,1)} %collective-permute-done.5.refs_6_), channel_id=1, source_target_pairs={{0,16},{16,0},{1,17},{17,1},{2,18},{18,2},{3,19},{19,3},{4,20},{20... | collective-permute-start | bytes 1572872 | tf_op jit(solution)/shard_map/Yw1/ppermute | solution.py:374
  22.3 13.5 %collective-permute-start.10 = (bf16[256,1024]{1,0:T(8,128)(2,1)S(1)}, bf16[256,1024]{1,0:T(8,128)(2,1)S(1)}, u32[]{:S(2)}, u32[]{:S(2)}) collective-permute-start(bf16[256,1024]{1,0:T(8,128)(2,1)S(1)} %collective-permute-done.3.refs_1_), channel_id=1, source_target_pairs={{0,1},{1,0},{2,3},{3,2},{4,5},{5,4},{6,7},{7,6},{8,9},{9,8},{10,11... | collective-permute-start | bytes 1572872 | tf_op jit(solution)/shard_map/Oc0/ppermute | solution.py:374
  35.8 16.7 %collective-permute-start.11 = (bf16[512,512]{1,0:T(8,128)(2,1)S(1)}, bf16[512,512]{1,0:T(8,128)(2,1)S(1)}, u32[]{:S(2)}, u32[]{:S(2)}) collective-permute-start(bf16[512,512]{1,0:T(8,128)(2,1)S(1)} %collective-permute-done.7.refs_8_), channel_id=1, source_target_pairs={{0,4},{4,8},{8,12},{12,0},{1,5},{5,9},{9,13},{13,1},{2,6},{6,10},{... | collective-permute-start | bytes 1572872 | tf_op jit(solution)/shard_map/Zw3/ppermute | solution.py:377
  35.9 16.6 %collective-permute-start.8 = (bf16[512,512]{1,0:T(8,128)(2,1)S(1)}, bf16[512,512]{1,0:T(8,128)(2,1)S(1)}, u32[]{:S(2)}, u32[]{:S(2)}) collective-permute-start(bf16[512,512]{1,0:T(8,128)(2,1)S(1)} %collective-permute-done.7.refs_8_), channel_id=1, source_target_pairs={{0,16},{16,0},{1,17},{17,1},{2,18},{18,2},{3,19},{19,3},{4,20},{20... | collective-permute-start | bytes 1572872 | tf_op jit(solution)/shard_map/Yw2/ppermute | solution.py:374
  37.2 25.7 %collective-permute-start.2 = (bf16[128,4096]{1,0:T(8,128)(2,1)}, bf16[128,4096]{1,0:T(8,128)(2,1)S(1)}, u32[]{:S(2)}, u32[]{:S(2)}) collective-permute-start(bf16[128,4096]{1,0:T(8,128)(2,1)} %get-tuple-element.31), channel_id=1, source_target_pairs={{0,3},{1,2},{2,1},{3,0},{4,7},{5,6},{6,5},{7,4},{8,11},{9,10},{10,... | collective-permute-start | bytes 3145736 | tf_op jit(solution)/shard_map/Txc/ppermute | solution.py:417
  41.9 19.2 %collective-permute-start.4 = (bf16[2,128,1024]{2,1,0:T(8,128)(2,1)S(1)}, bf16[2,128,1024]{2,1,0:T(8,128)(2,1)S(1)}, u32[]{:S(2)}, u32[]{:S(2)}) collective-permute-start(bf16[2,128,1024]{2,1,0:T(8,128)(2,1)S(1)} %pair.1), channel_id=1, source_target_pairs={{0,4},{4,8},{8,12},{12,0},{1,5},{5,9},{9,13},{13,1},{2,6},{6,10},{... | collective-permute-start | bytes 1572872 | tf_op jit(solution)/shard_map/Zo1/ppermute | solution.py:377
  52.5 10.4 %collective-permute-start.12 = (bf16[512,512]{1,0:T(8,128)(2,1)S(1)}, bf16[512,512]{1,0:T(8,128)(2,1)S(1)}, u32[]{:S(2)}, u32[]{:S(2)}) collective-permute-start(bf16[512,512]{1,0:T(8,128)(2,1)S(1)} %collective-permute-done.11.refs_10_), channel_id=1, source_target_pairs={{0,16},{16,0},{1,17},{17,1},{2,18},{18,2},{3,19},{19,3},{4,20},{20... | collective-permute-start | bytes 1572872 | tf_op jit(solution)/shard_map/Yw3/ppermute | solution.py:374
  61.1 13.1 %collective-permute-start.13 = (bf16[2,128,1024]{2,1,0:T(8,128)(2,1)S(1)}, bf16[2,128,1024]{2,1,0:T(8,128)(2,1)S(1)}, u32[]{:S(2)}, u32[]{:S(2)}) collective-permute-start(bf16[2,128,1024]{2,1,0:T(8,128)(2,1)S(1)} %collective-permute-done.4.refs_4_), channel_id=1, source_target_pairs={{0,4},{4,8},{8,12},{12,0},{1,5},{5,9},{9,13},{13,1},{2,6},{6,10},{... | collective-permute-start | bytes 1572872 | tf_op jit(solution)/shard_map/Zo2/ppermute | solution.py:377
  61.1 13.1 %collective-permute-start.14 = (bf16[2,128,1024]{2,1,0:T(8,128)(2,1)S(1)}, bf16[2,128,1024]{2,1,0:T(8,128)(2,1)S(1)}, u32[]{:S(2)}, u32[]{:S(2)}) collective-permute-start(bf16[2,128,1024]{2,1,0:T(8,128)(2,1)S(1)} %collective-permute-done.4.refs_4_), channel_id=1, source_target_pairs={{0,16},{16,0},{1,17},{17,1},{2,18},{18,2},{3,19},{19,3},{4,20},{20... | collective-permute-start | bytes 1572872 | tf_op jit(solution)/shard_map/Yo1/ppermute | solution.py:374
  68.1 32.0 %copy-start = (bf16[128,16384]{1,0:T(8,128)(2,1)S(1)}, bf16[128,16384]{1,0:T(8,128)(2,1)}, u32[]{:S(2)}) copy-start(bf16[128,16384]{1,0:T(8,128)(2,1)} %tok.3) | copy-start | bytes 12582916
  74.2 1.9 %collective-permute-start.15 = (f32[2,128,512]{2,1,0:T(8,128)S(1)}, f32[2,128,512]{2,1,0:T(8,128)S(1)}, u32[]{:S(2)}, u32[]{:S(2)}) collective-permute-start(f32[2,128,512]{2,1,0:T(8,128)S(1)} %get-tuple-element.39), channel_id=1, source_target_pairs={{0,1},{1,0},{2,3},{3,2},{4,5},{5,4},{6,7},{7,6},{8,9},{9,8},{10,11... | collective-permute-start | bytes 1572872 | tf_op jit(solution)/shard_map/Pc/ppermute | solution.py:374
  74.2 14.3 %collective-permute-start.18 = (bf16[2,128,1024]{2,1,0:T(8,128)(2,1)S(1)}, bf16[2,128,1024]{2,1,0:T(8,128)(2,1)S(1)}, u32[]{:S(2)}, u32[]{:S(2)}) collective-permute-start(bf16[2,128,1024]{2,1,0:T(8,128)(2,1)S(1)} %collective-permute-done.13.refs_8_), channel_id=1, source_target_pairs={{0,16},{16,0},{1,17},{17,1},{2,18},{18,2},{3,19},{19,3},{4,20},{20... | collective-permute-start | bytes 1572872 | tf_op jit(solution)/shard_map/Yo2/ppermute | solution.py:374
  74.9 15.9 %collective-permute-start.17 = (bf16[2,128,1024]{2,1,0:T(8,128)(2,1)S(1)}, bf16[2,128,1024]{2,1,0:T(8,128)(2,1)S(1)}, u32[]{:S(2)}, u32[]{:S(2)}) collective-permute-start(bf16[2,128,1024]{2,1,0:T(8,128)(2,1)S(1)} %collective-permute-done.13.refs_8_), channel_id=1, source_target_pairs={{0,4},{4,8},{8,12},{12,0},{1,5},{5,9},{9,13},{13,1},{2,6},{6,10},{... | collective-permute-start | bytes 1572872 | tf_op jit(solution)/shard_map/Zo3/ppermute | solution.py:377
  76.1 12.7 %collective-permute-start.16 = (f32[128,512]{1,0:T(8,128)S(1)}, f32[128,512]{1,0:T(8,128)S(1)}, u32[]{:S(2)}, u32[]{:S(2)}) collective-permute-start(f32[128,512]{1,0:T(8,128)S(1)} %fusion), channel_id=1, source_target_pairs={{0,2},{2,0},{1,3},{3,1},{4,6},{6,4},{5,7},{7,5},{8,10},{10,8},{9,1... | collective-permute-start | bytes 786440 | tf_op jit(solution)/shard_map/Px/ppermute | solution.py:374
  88.5 10.5 %collective-permute-start.22 = (bf16[128,1024]{1,0:T(8,128)(2,1)S(1)}, bf16[128,1024]{1,0:T(8,128)(2,1)S(1)}, u32[]{:S(2)}, u32[]{:S(2)}) collective-permute-start(bf16[128,1024]{1,0:T(8,128)(2,1)S(1)} %slice_bitcast_fusion), channel_id=1, source_target_pairs={{0,4},{4,8},{8,12},{12,0},{1,5},{5,9},{9,13},{13,1},{2,6},{6,10},{... | collective-permute-start | bytes 786440 | tf_op jit(solution)/shard_map/Zf3/ppermute | solution.py:377
  88.8 10.8 %collective-permute-start.27 = (bf16[2,128,1024]{2,1,0:T(8,128)(2,1)S(1)}, bf16[2,128,1024]{2,1,0:T(8,128)(2,1)S(1)}, u32[]{:S(2)}, u32[]{:S(2)}) collective-permute-start(bf16[2,128,1024]{2,1,0:T(8,128)(2,1)S(1)} %collective-permute-done.14.refs_5_), channel_id=1, source_target_pairs={{0,1},{1,0},{2,3},{3,2},{4,5},{5,4},{6,7},{7,6},{8,9},{9,8},{10,11... | collective-permute-start | bytes 1572872 | tf_op jit(solution)/shard_map/Oc1/ppermute | solution.py:374
  88.9 11.2 %collective-permute-start.26 = (bf16[2,128,1024]{2,1,0:T(8,128)(2,1)S(1)}, bf16[2,128,1024]{2,1,0:T(8,128)(2,1)S(1)}, u32[]{:S(2)}, u32[]{:S(2)}) collective-permute-start(bf16[2,128,1024]{2,1,0:T(8,128)(2,1)S(1)} %collective-permute-done.4.refs_4_), channel_id=1, source_target_pairs={{0,1},{1,0},{2,3},{3,2},{4,5},{5,4},{6,7},{7,6},{8,9},{9,8},{10,11... | collective-permute-start | bytes 1572872 | tf_op jit(solution)/shard_map/Oc1/ppermute | solution.py:374
  90.8 8.7 %collective-permute-start.21 = (bf16[128,1024]{1,0:T(8,128)(2,1)S(1)}, bf16[128,1024]{1,0:T(8,128)(2,1)S(1)}, u32[]{:S(2)}, u32[]{:S(2)}) collective-permute-start(bf16[128,1024]{1,0:T(8,128)(2,1)S(1)} %slice_bitcast_fusion.1), channel_id=1, source_target_pairs={{0,16},{16,0},{1,17},{17,1},{2,18},{18,2},{3,19},{19,3},{4,20},{20... | collective-permute-start | bytes 786440 | tf_op jit(solution)/shard_map/Yo3/ppermute | solution.py:374
  98.9 5.4 %collective-permute-start.23 = (bf16[2,128,1024]{2,1,0:T(8,128)(2,1)S(1)}, bf16[2,128,1024]{2,1,0:T(8,128)(2,1)S(1)}, u32[]{:S(2)}, u32[]{:S(2)}) collective-permute-start(bf16[2,128,1024]{2,1,0:T(8,128)(2,1)S(1)} %collective-permute-done.17.refs_2_), channel_id=1, source_target_pairs={{0,1},{1,0},{2,3},{3,2},{4,5},{5,4},{6,7},{7,6},{8,9},{9,8},{10,11... | collective-permute-start | bytes 1572872 | tf_op jit(solution)/shard_map/Oc/ppermute | solution.py:374
  99.0 5.3 %collective-permute-start.20 = (bf16[2,128,1024]{2,1,0:T(8,128)(2,1)S(1)}, bf16[2,128,1024]{2,1,0:T(8,128)(2,1)S(1)}, u32[]{:S(2)}, u32[]{:S(2)}) collective-permute-start(bf16[2,128,1024]{2,1,0:T(8,128)(2,1)S(1)} %collective-permute-done.18.refs_9_), channel_id=1, source_target_pairs={{0,1},{1,0},{2,3},{3,2},{4,5},{5,4},{6,7},{7,6},{8,9},{9,8},{10,11... | collective-permute-start | bytes 1572872 | tf_op jit(solution)/shard_map/Oc/ppermute | solution.py:374
  99.5 4.8 %collective-permute-start.19 = (bf16[2,128,1024]{2,1,0:T(8,128)(2,1)S(1)}, bf16[2,128,1024]{2,1,0:T(8,128)(2,1)S(1)}, u32[]{:S(2)}, u32[]{:S(2)}) collective-permute-start(bf16[2,128,1024]{2,1,0:T(8,128)(2,1)S(1)} %collective-permute-done.13.refs_8_), channel_id=1, source_target_pairs={{0,1},{1,0},{2,3},{3,2},{4,5},{5,4},{6,7},{7,6},{8,9},{9,8},{10,11... | collective-permute-start | bytes 1572872 | tf_op jit(solution)/shard_map/Oc/ppermute | solution.py:374
  99.6 4.7 %collective-permute-start.25 = (bf16[128,1024]{1,0:T(8,128)(2,1)S(1)}, bf16[128,1024]{1,0:T(8,128)(2,1)S(1)}, u32[]{:S(2)}, u32[]{:S(2)}) collective-permute-start(bf16[128,1024]{1,0:T(8,128)(2,1)S(1)} %collective-permute-done.22.refs_4_), channel_id=1, source_target_pairs={{0,1},{1,0},{2,3},{3,2},{4,5},{5,4},{6,7},{7,6},{8,9},{9,8},{10,11... | collective-permute-start | bytes 786440 | tf_op jit(solution)/shard_map/Oc/ppermute | solution.py:374
  100.0 4.2 %collective-permute-start.24 = (bf16[128,1024]{1,0:T(8,128)(2,1)S(1)}, bf16[128,1024]{1,0:T(8,128)(2,1)S(1)}, u32[]{:S(2)}, u32[]{:S(2)}) collective-permute-start(bf16[128,1024]{1,0:T(8,128)(2,1)S(1)} %collective-permute-done.21.refs_3_), channel_id=1, source_target_pairs={{0,1},{1,0},{2,3},{3,2},{4,5},{5,4},{6,7},{7,6},{8,9},{9,8},{10,11... | collective-permute-start | bytes 786440 | tf_op jit(solution)/shard_map/Oc/ppermute | solution.py:374
  (3 other events, 48.5 us)

commit v5 on v4

--- a/solution.py
+++ b/solution.py
@@ -180,18 +180,45 @@
     return ((z * nr + r) * 2 + x) * 2 + c
 
 
-def attend_kernel(lens, *refs, heads, head, nr):
-    mine, core, other, turns, cache, out, pbuf, kvbuf, psem, sem = refs
+CHUNK = 1024
+
+
+def cache_copies(cache, kvbuf, sem, base):
+    return [
+        pltpu.make_async_copy(
+            cache.at[0, pl.ds(base + i * CHUNK, CHUNK)], kvbuf.at[pl.ds(i * CHUNK, CHUNK)], sem.at[i]
+        )
+        for i in range(kvbuf.shape[0] // CHUNK)
+    ]
+
+
+def scores(q, keys):
+    return lax.dot_general(q, keys, (((1,), (1,)), ((), ())), preferred_element_type=F32)
+
+
+def fold(q, copies, kvbuf, base, length, scale, top, total, acc):
+    head = q.shape[1]
+    for i, cp in enumerate(copies):
+        cp.wait()
+        s = scores(q, kvbuf[pl.ds(i * CHUNK, CHUNK), :head])
+        col = lax.broadcasted_iota(jnp.int32, (1, CHUNK), 1) + (base + i * CHUNK)
+        s = jnp.where(col < length, s, -1e30)
+        new_top = jnp.maximum(top, jnp.max(s, axis=1, keepdims=True))
+        p = jnp.exp2((s - new_top) * scale)
+        fade = jnp.exp2((top - new_top) * scale)
+        top = new_top
+        total = total * fade + jnp.sum(p, axis=1, keepdims=True)
+        acc = acc * fade + jnp.dot(
+            p.astype(BF16), kvbuf[pl.ds(i * CHUNK, CHUNK), head:], preferred_element_type=F32
+        )
+    return top, total, acc
+
+
+def attend_first_kernel(lens, mine, core, other, turns, cache, q_out, state, pbuf, kvbuf, psem, sem, *, heads, scale, nr):
     length = lens[prompt_index(nr)]
-    slots = kvbuf.shape[0]
     rows = mine.shape[0]
-    chunk = 1024
-    copies = [
-        pltpu.make_async_copy(
-            cache.at[0, pl.ds(i * chunk, chunk)], kvbuf.at[pl.ds(i * chunk, chunk)], sem.at[i]
-        )
-        for i in range(slots // chunk)
-    ]
+    head = q_out.shape[1]
+    copies = cache_copies(cache, kvbuf, sem, 0)
     sums = [
         pltpu.make_async_copy(ref, pbuf.at[i], psem.at[i]) for i, ref in enumerate((mine, core.at[0], other))
     ]
@@ -205,61 +232,83 @@
         return (v * turns[0] + pltpu.roll(v, head // 2, 1) * turns[1]).astype(BF16)
 
     q = jnp.concatenate([turn(total[:, i * head : (i + 1) * head]) for i in range(heads)], axis=0)
+    q_out[...] = q
     k_new = turn(total[:, heads * head : (heads + 1) * head])
     v_new = total[:, (heads + 1) * head :].astype(BF16)
-    scale = (head ** -0.5) * 1.4426950408889634
-
-    def scores(keys):
-        return lax.dot_general(q, keys, (((1,), (1,)), ((), ())), preferred_element_type=F32)
-
-    s = scores(k_new)
+    s = scores(q, k_new)
     row = lax.broadcasted_iota(jnp.int32, s.shape, 0) % rows
     col = lax.broadcasted_iota(jnp.int32, s.shape, 1)
     s = jnp.where(col <= row, s, -1e30)
     top = jnp.max(s, axis=1, keepdims=True)
     p = jnp.exp2((s - top) * scale)
-    total_p = jnp.sum(p, axis=1, keepdims=True)
+    sum_p = jnp.sum(p, axis=1, keepdims=True)
     acc = jnp.dot(p.astype(BF16), v_new, preferred_element_type=F32)
-    for i, cp in enumerate(copies):
-        cp.wait()
-        s = scores(kvbuf[pl.ds(i * chunk, chunk), :head])
-        col = lax.broadcasted_iota(jnp.int32, (1, chunk), 1) + i * chunk
-        s = jnp.where(col < length, s, -1e30)
-        new_top = jnp.maximum(top, jnp.max(s, axis=1, keepdims=True))
-        p = jnp.exp2((s - new_top) * scale)
-        fade = jnp.exp2((top - new_top) * scale)
-        top = new_top
-        total_p = total_p * fade + jnp.sum(p, axis=1, keepdims=True)
-        acc = acc * fade + jnp.dot(
-            p.astype(BF16), kvbuf[pl.ds(i * chunk, chunk), head:], preferred_element_type=F32
-        )
-    acc = (acc / total_p).astype(BF16)
+    top, sum_p, acc = fold(q, copies, kvbuf, 0, length, scale, top, sum_p, acc)
+    state[0] = jnp.broadcast_to(top, acc.shape)
+    state[1] = jnp.broadcast_to(sum_p, acc.shape)
+    state[2] = acc
+
+
+def attend_last_kernel(lens, q, state, cache, out, kvbuf, sem, *, heads, scale, nr, base):
+    length = lens[prompt_index(nr)]
+    rows = out.shape[0]
+    head = q.shape[1]
+    copies = cache_copies(cache, kvbuf, sem, base)
+    for cp in copies:
+        cp.start()
+    _, total, acc = fold(
+        q[...], copies, kvbuf, base, length, scale, state[0][:, :1], state[1][:, :1], state[2]
+    )
+    acc = (acc / total).astype(BF16)
     for i in range(heads):
         out[:, i * head : (i + 1) * head] = acc[i * rows : (i + 1) * rows]
 
 
-def attend(lens, mine, core, other, turns, cache, heads, head, nr):
-    vmem = pl.BlockSpec(memory_space=pltpu.VMEM)
+def attend_scale(head):
+    return (head ** -0.5) * 1.4426950408889634
+
+
+def attend_first(lens, mine, core, other, turns, cache, heads, head, nr, count):
+    vmem, anywhere = (pl.BlockSpec(memory_space=m) for m in (pltpu.VMEM, pl.ANY))
     rows = mine.shape[0]
-    slots = cache.shape[1]
-    anywhere = pl.BlockSpec(memory_space=pl.ANY)
     return pl.pallas_call(
-        functools.partial(attend_kernel, heads=heads, head=head, nr=nr),
+        functools.partial(attend_first_kernel, heads=heads, scale=attend_scale(head), nr=nr),
         in_specs=[pl.BlockSpec(memory_space=pltpu.SMEM)] + [anywhere] * 3 + [vmem, anywhere],
-        out_specs=vmem,
-        out_shape=jax.ShapeDtypeStruct((rows, heads * head), BF16),
+        out_specs=[vmem] * 2,
+        out_shape=[
+            jax.ShapeDtypeStruct((heads * rows, head), BF16),
+            jax.ShapeDtypeStruct((3, heads * rows, head), F32),
+        ],
         scratch_shapes=[
             pltpu.VMEM((3,) + mine.shape, F32),
-            pltpu.VMEM(cache.shape[1:], BF16),
+            pltpu.VMEM((count, 2 * head), BF16),
             pltpu.SemaphoreType.DMA((3,)),
-            pltpu.SemaphoreType.DMA((slots // 1024,)),
+            pltpu.SemaphoreType.DMA((count // CHUNK,)),
         ],
         compiler_params=params(20),
         cost_estimate=pl.CostEstimate(
-            flops=4 * rows * heads * head * slots, bytes_accessed=28 * 1024 * 1024, transcendentals=rows * heads * slots
+            flops=4 * rows * heads * head * count, bytes_accessed=14 * 1024 * 1024, transcendentals=rows * heads * count
         ),
-        name="attend",
+        name="attend_first",
     )(lens, mine, core, other, turns, cache)
+
+
+def attend_last(lens, q, state, cache, heads, nr, base):
+    vmem, anywhere = (pl.BlockSpec(memory_space=m) for m in (pltpu.VMEM, pl.ANY))
+    rows, head = q.shape[0] // heads, q.shape[1]
+    count = cache.shape[1] - base
+    return pl.pallas_call(
+        functools.partial(attend_last_kernel, heads=heads, scale=attend_scale(head), nr=nr, base=base),
+        in_specs=[pl.BlockSpec(memory_space=pltpu.SMEM), vmem, vmem, anywhere],
+        out_specs=vmem,
+        out_shape=jax.ShapeDtypeStruct((rows, heads * head), BF16),
+        scratch_shapes=[pltpu.VMEM((count, 2 * head), BF16), pltpu.SemaphoreType.DMA((count // CHUNK,))],
+        compiler_params=params(20),
+        cost_estimate=pl.CostEstimate(
+            flops=4 * rows * heads * head * count, bytes_accessed=14 * 1024 * 1024, transcendentals=rows * heads * count
+        ),
+        name="attend_last",
+    )(lens, q, state, cache)
 
 
 def out_kernel(att, tok, *refs, plan, nz, nr, bs, carry):
@@ -461,22 +510,17 @@
         other = swap(total, "x")
     o_near.append(step_z(o_near[2], "o3"))
     o_far.append(step_y(o_near[2], "o2"))
-    last_far = [step_y(o_near[3][0], "o3"), step_z(o_far[2][1], "f3")]
     with jax.named_scope("Oc1"):
-        near1_c = swap(tie(o_near[1], other), "c")
+        near1_c = swap(tie(o_near[1], total), "c")
         far1_c = swap(tie(o_far[1], other), "c")
 
-    att = attend(
-        cached_len,
-        parts[0],
-        from_c,
-        tie(other, o_near[3], o_far[2]),
-        turns,
-        cache_kv,
-        heads,
-        head,
-        nr,
-    )
+    begun = cache_kv.shape[1] // (2 * CHUNK) * CHUNK
+    q, state = attend_first(cached_len, parts[0], from_c, other, turns, cache_kv, heads, head, nr, begun)
+    last_far = [
+        step_y(tie(o_near[3], state)[0], "o3"),
+        step_z(tie(o_far[2], state)[1], "f3"),
+    ]
+    att = attend_last(cached_len, q, tie(state, o_near[3], o_far[2]), cache_kv, heads, nr, begun)
 
     def over(v, dc, *after):
         if not dc:
@@ -510,7 +554,7 @@
     for dc in range(2):
         near = over(o_near[3], dc, att)
         for dx in range(2):
-            late.append(((3, dx, dc), [(near, dx, None), (over(last_far[dx], dc, att), None, None)]))
+            late.append(((3, dx, dc), [(near, dx, None), (over(last_far[dx], dc, out), None, None)]))
     return output(att, tokens, *group(late), nz, nr, bs, out)
 
 

time: 107 us -> 105 us (0.981)
  waiting for transfers between devices: 60.8 us -> 58.6 us
    ppermute x20, waiting for transfers between devices: 17.3 us -> 14.4 us  [swap(): return lax.ppermute(v, axis, [(0, 1), (1, 0)])]
    pallas_call x1 -> x2, Pallas kernels: 6.77 us -> 7.85 us  [the longest x1 3.94 us: attend_first(): pl.pallas_call(functools.partial(attend_first_kernel, heads=heads, scale=...]
  transfers between devices with their start and end apart: 28 -> 28, of which waited for: 10 -> 13; matrix products, arithmetic and copies ran while one was open for 1% -> 1% of each run, Pallas kernels for 19% -> 20%
where the time goes in v5:
time: 105 us
  waiting for transfers between devices  58.6 us (56%)
  Pallas kernels  25.6 us (24%)
  starting transfers between devices  17.5 us (17%)
  local copies, waits for them, and re-layouts  1.28 us (1%)
  other arithmetic  1.19 us (1%)
  between operations  1.06 us (1%)
    ppermute x7, waiting for transfers between devices, ring(): return lax.ppermute(v, 'z', [(i, (i + 1) % nz) for i in range(nz)])  43.3 us
    ppermute x20, waiting for transfers between devices, swap(): return lax.ppermute(v, axis, [(0, 1), (1, 0)])  14.4 us
    ppermute x20, starting transfers between devices, swap(): return lax.ppermute(v, axis, [(0, 1), (1, 0)])  11.5 us
    pallas_call x2, Pallas kernels, output(): pl.pallas_call(functools.partial(out_kernel, plan=plan, nz=nz, nr=nr, bs=...  6.85 us
    ppermute x7, starting transfers between devices, ring(): return lax.ppermute(v, 'z', [(i, (i + 1) % nz) for i in range(nz)])  5.94 us
    pallas_call x1, Pallas kernels, normalise(): pl.pallas_call(functools.partial(norm_kernel, nz=nz, nr=nr, bs=bs, block=...  5.01 us
    pallas_call x1, Pallas kernels, attend_first(): pl.pallas_call(functools.partial(attend_first_kernel, heads=heads, scale=...  3.94 us
    pallas_call x1, Pallas kernels, project(): pl.pallas_call(functools.partial(project_kernel, halves=halves), in_specs...  3.91 us
  transfers between devices with their start and end apart: 28, of which 13 were waited for; matrix products, arithmetic and copies ran while one was open for 1% of the time, Pallas kernels for 20%

profile of v5, /device:TPU:0, one launch (start us, length us, event | category | flops | bytes accessed | tf_op | source)
XLA Modules:
  0.0 105.2 jit_solution(974228822028582822)
XLA Ops:
  0.0 2.0 %pick.1 = bf16[512,512]{1,0:T(8,128)(2,1)} custom-call(bf16[1024,256]{1,0:T(8,128)(2,1)} %refs_4_.1, bf16[1024,256]{1,0:T(8,128)(2,1)} %refs_5_.1), custom_call_target="tpu_custom_call" | custom-call | bytes 1048576 | tf_op jit(solution)/shard_map/pick/pallas_call | solution.py:42
  2.0 3.1 %collective-permute-start.5 = (bf16[512,512]{1,0:T(8,128)(2,1)}, bf16[512,512]{1,0:T(8,128)(2,1)}, u32[]{:S(2)}, u32[]{:S(2)}) collective-permute-start(bf16[512,512]{1,0:T(8,128)(2,1)} %pick.1), channel_id=1, source_target_pairs={{0,4},{4,8},{8,12},{12,0},{1,5},{5,9},{9,13},{13,1},{2,6},{6,10},{... | collective-permute-start | bytes 1572872 | tf_op jit(solution)/shard_map/Zw1/ppermute | solution.py:426
  5.1 1.5 %collective-permute-start.3 = (bf16[256,1024]{1,0:T(8,128)(2,1)}, bf16[256,1024]{1,0:T(8,128)(2,1)S(1)}, u32[]{:S(2)}, u32[]{:S(2)}) collective-permute-start(bf16[256,1024]{1,0:T(8,128)(2,1)} %refs_0_.5), channel_id=1, source_target_pairs={{0,2},{2,0},{1,3},{3,1},{4,6},{6,4},{5,7},{7,5},{8,10},{10,8},{9,1... | collective-permute-start | bytes 1572872 | tf_op jit(solution)/shard_map/Ox/ppermute | solution.py:423
  6.6 5.0 %norm.1 = (bf16[128,4096]{1,0:T(8,128)(2,1)}, bf16[128,4096]{1,0:T(8,128)(2,1)}, bf16[128,4096]{1,0:T(8,128)(2,1)}, bf16[128,4096]{1,0:T(8,128)(2,1)}) custom-call(bf16[128,16384]{1,0:T(8,128)(2,1)} %tok.3, f32[1,16384]{1,0:T(1,128)} %bitcast.13), custom_call_target="tpu_custom_call" | custom-call | flops 16777216 | bytes 2097152 | tf_op jit(solution)/shard_map/norm/pallas_call | solution.py:92
  11.6 0.6 collective-permute-start
  12.2 0.5 collective-permute-start.1
  12.7 6.6 %collective-permute-done.5.refs_6_ = bf16[512,512]{1,0:T(8,128)(2,1)} collective-permute-done((bf16[512,512]{1,0:T(8,128)(2,1)}, bf16[512,512]{1,0:T(8,128)(2,1)}, u32[]{:S(2)}, u32[]{:S(2)}) %collective-permute-start.5) | collective-permute-done | bytes 524320 | tf_op jit(solution)/shard_map/Zw1/ppermute | solution.py:426
  19.3 0.7 fusion.2
  20.8 1.6 %collective-permute-start.6 = (bf16[512,512]{1,0:T(8,128)(2,1)}, bf16[512,512]{1,0:T(8,128)(2,1)S(1)}, u32[]{:S(2)}, u32[]{:S(2)}) collective-permute-start(bf16[512,512]{1,0:T(8,128)(2,1)} %collective-permute-done.5.refs_6_), channel_id=1, source_target_pairs={{0,16},{16,0},{1,17},{17,1},{2,18},{18,2},{3,19},{19,3},{4,20},{20... | collective-permute-start | bytes 1572872 | tf_op jit(solution)/shard_map/Yw1/ppermute | solution.py:423
  22.8 13.1 %collective-permute-done.7.refs_8_ = bf16[512,512]{1,0:T(8,128)(2,1)S(1)} collective-permute-done((bf16[512,512]{1,0:T(8,128)(2,1)}, bf16[512,512]{1,0:T(8,128)(2,1)S(1)}, u32[]{:S(2)}, u32[]{:S(2)}) %collective-permute-start.7) | collective-permute-done | bytes 524320 | tf_op jit(solution)/shard_map/Zw2/ppermute | solution.py:426
  36.0 1.3 %collective-permute-start.8 = (bf16[512,512]{1,0:T(8,128)(2,1)S(1)}, bf16[512,512]{1,0:T(8,128)(2,1)S(1)}, u32[]{:S(2)}, u32[]{:S(2)}) collective-permute-start(bf16[512,512]{1,0:T(8,128)(2,1)S(1)} %collective-permute-done.7.refs_8_), channel_id=1, source_target_pairs={{0,16},{16,0},{1,17},{17,1},{2,18},{18,2},{3,19},{19,3},{4,20},{20... | collective-permute-start | bytes 1572872 | tf_op jit(solution)/shard_map/Yw2/ppermute | solution.py:423
  37.4 4.4 %collective-permute-done.1.refs_2_ = bf16[128,4096]{1,0:T(8,128)(2,1)} collective-permute-done((bf16[128,4096]{1,0:T(8,128)(2,1)}, bf16[128,4096]{1,0:T(8,128)(2,1)}, u32[]{:S(2)}, u32[]{:S(2)}) %collective-permute-start.1) | collective-permute-done | bytes 1048608 | tf_op jit(solution)/shard_map/Tx/ppermute | solution.py:423
  41.8 2.5 %collective-permute-start.4 = (bf16[2,128,1024]{2,1,0:T(8,128)(2,1)S(1)}, bf16[2,128,1024]{2,1,0:T(8,128)(2,1)S(1)}, u32[]{:S(2)}, u32[]{:S(2)}) collective-permute-start(bf16[2,128,1024]{2,1,0:T(8,128)(2,1)S(1)} %pair.1), channel_id=1, source_target_pairs={{0,4},{4,8},{8,12},{12,0},{1,5},{5,9},{9,13},{13,1},{2,6},{6,10},{... | collective-permute-start | bytes 1572872 | tf_op jit(solution)/shard_map/Zo1/ppermute | solution.py:426
  44.3 8.4 %collective-permute-done.11.refs_10_ = bf16[512,512]{1,0:T(8,128)(2,1)S(1)} collective-permute-done((bf16[512,512]{1,0:T(8,128)(2,1)S(1)}, bf16[512,512]{1,0:T(8,128)(2,1)S(1)}, u32[]{:S(2)}, u32[]{:S(2)}) %collective-permute-start.11) | collective-permute-done | bytes 524320 | tf_op jit(solution)/shard_map/Zw3/ppermute | solution.py:426
  52.6 1.3 %collective-permute-start.12 = (bf16[512,512]{1,0:T(8,128)(2,1)S(1)}, bf16[512,512]{1,0:T(8,128)(2,1)S(1)}, u32[]{:S(2)}, u32[]{:S(2)}) collective-permute-start(bf16[512,512]{1,0:T(8,128)(2,1)S(1)} %collective-permute-done.11.refs_10_), channel_id=1, source_target_pairs={{0,16},{16,0},{1,17},{17,1},{2,18},{18,2},{3,19},{19,3},{4,20},{20... | collective-permute-start | bytes 1572872 | tf_op jit(solution)/shard_map/Yw3/ppermute | solution.py:423
  53.9 7.3 %collective-permute-done.4.refs_4_ = bf16[2,128,1024]{2,1,0:T(8,128)(2,1)S(1)} collective-permute-done((bf16[2,128,1024]{2,1,0:T(8,128)(2,1)S(1)}, bf16[2,128,1024]{2,1,0:T(8,128)(2,1)S(1)}, u32[]{:S(2)}, u32[]{:S(2)}) %collective-permute-start.4) | collective-permute-done | bytes 524320 | tf_op jit(solution)/shard_map/Zo1/ppermute | solution.py:426
  61.2 1.0 collective-permute-start.14
  62.2 0.8 collective-permute-done.2.refs_3_
  63.1 1.2 %copy-done.5 = bf16[128,4096]{1,0:T(8,128)(2,1)S(1)} copy-done((bf16[128,4096]{1,0:T(8,128)(2,1)S(1)}, bf16[128,4096]{1,0:T(8,128)(2,1)}, u32[]{:S(2)}) %copy-start.5) | copy-done | bytes 1048600
  64.3 3.9 %project.1 = (f32[128,512]{1,0:T(8,128)S(1)}, f32[2,128,512]{2,1,0:T(8,128)S(1)}, f32[128,512]{1,0:T(8,128)S(1)}) custom-call(bf16[128,4096]{1,0:T(8,128)(2,1)S(1)} %copy-done.5, bf16[128,4096]{1,0:T(8,128)(2,1)S(1)} %collective-permute-done.refs_1_, bf16[128,4096]{1,0:T(8,128)(2,1)} %collective-permute-done.1.refs_2_, ...), custom_call_target="tpu_custom_call" | custom-call | flops 2147483648 | bytes 2097152 | tf_op jit(solution)/shard_map/project/pallas_call | solution.py:159
  68.2 6.0 %collective-permute-done.13.refs_8_ = bf16[2,128,1024]{2,1,0:T(8,128)(2,1)S(1)} collective-permute-done((bf16[2,128,1024]{2,1,0:T(8,128)(2,1)S(1)}, bf16[2,128,1024]{2,1,0:T(8,128)(2,1)S(1)}, u32[]{:S(2)}, u32[]{:S(2)}) %collective-permute-start.13) | collective-permute-done | bytes 524320 | tf_op jit(solution)/shard_map/Zo2/ppermute | solution.py:426
  74.3 0.8 collective-permute-start.18
  75.1 1.1 %collective-permute-done.15.core = f32[2,128,512]{2,1,0:T(8,128)S(1)} collective-permute-done((f32[2,128,512]{2,1,0:T(8,128)S(1)}, f32[2,128,512]{2,1,0:T(8,128)S(1)}, u32[]{:S(2)}, u32[]{:S(2)}) %collective-permute-start.15) | collective-permute-done | bytes 524320 | tf_op jit(solution)/shard_map/Pc/ppermute | solution.py:423
  76.2 0.8 collective-permute-start.16
  77.0 7.6 %collective-permute-done.16.other = f32[128,512]{1,0:T(8,128)S(1)} collective-permute-done((f32[128,512]{1,0:T(8,128)S(1)}, f32[128,512]{1,0:T(8,128)S(1)}, u32[]{:S(2)}, u32[]{:S(2)}) %collective-permute-start.16) | collective-permute-done | bytes 262176 | tf_op jit(solution)/shard_map/Px/ppermute | solution.py:423
  84.6 3.9 %attend_first.1 = (bf16[256,128]{1,0:T(8,128)(2,1)S(1)}, f32[3,256,128]{2,1,0:T(8,128)S(1)}) custom-call(s32[16]{0:T(128)S(1)} %copy-done.6, f32[128,512]{1,0:T(8,128)S(1)} %get-tuple-element.41.mine, f32[2,128,512]{2,1,0:T(8,128)S(1)} %collective-permute-done.15.core, f32[128,512]{1,0:T(8,128)S(1)} %collective-permute-done.16.other, ...), custom_call_target="tpu_custom_call" | custom-call | flops 536870912 | bytes 14680064 | tf_op jit(solution)/shard_map/attend_first/pallas_call | solution.py:274
  88.6 1.8 %collective-permute-done.17.refs_2_ = bf16[2,128,1024]{2,1,0:T(8,128)(2,1)S(1)} collective-permute-done((bf16[2,128,1024]{2,1,0:T(8,128)(2,1)S(1)}, bf16[2,128,1024]{2,1,0:T(8,128)(2,1)S(1)}, u32[]{:S(2)}, u32[]{:S(2)}) %collective-permute-start.17) | collective-permute-done | bytes 524320 | tf_op jit(solution)/shard_map/Zo3/ppermute | solution.py:426
  90.7 0.8 collective-permute-start.21
  91.5 3.9 %attend_last.1.att = bf16[128,256]{1,0:T(8,128)(2,1)S(1)} custom-call(s32[16]{0:T(128)S(1)} %copy-done.6, bf16[256,128]{1,0:T(8,128)(2,1)S(1)} %get-tuple-element.45.q, f32[3,256,128]{2,1,0:T(8,128)S(1)} %get-tuple-element.47.state, bf16[1,8192,256]{2,1,0:T(8,128)(2,1)S(1)} %copy-done.1), custom_call_target="tpu_custom_call" | custom-call | flops 536870912 | bytes 14680064 | tf_op jit(solution)/shard_map/attend_last/pallas_call | solution.py:300
  96.1 4.1 %output.2.refs_8_ = bf16[128,16384]{1,0:T(8,128)(2,1)} custom-call(bf16[128,256]{1,0:T(8,128)(2,1)S(1)} %attend_last.1.att, bf16[128,16384]{1,0:T(8,128)(2,1)S(1)} %copy-done, bf16[256,1024]{1,0:T(8,128)(2,1)S(1)} %copy-done.4, bf16[256,1024]{1,0:T(8,128)(2,1)S(1)} %collective-permute-done.3.refs_1_, bf16[256,1024]{1,0:T(8,128)(2,1)} %collective-permute-done.9.refs_2_, ...), custom_call_target="tpu_custom_call" | custom-call | flops 671088640 | bytes 10485760 | tf_op jit(solution)/shard_map/output/pallas_call | solution.py:381
  100.9 1.0 collective-permute-done.27.refs_7_
  102.3 2.7 %output.3 = bf16[128,16384]{1,0:T(8,128)(2,1)} custom-call(bf16[128,256]{1,0:T(8,128)(2,1)S(1)} %attend_last.1.att, bf16[128,16384]{1,0:T(8,128)(2,1)S(1)} %copy-done, bf16[2,128,1024]{2,1,0:T(8,128)(2,1)S(1)} %collective-permute-done.19.refs_0_, bf16[2,128,1024]{2,1,0:T(8,128)(2,1)S(1)} %collective-permute-done.20.refs_1_, ...), custom_call_target="tpu_custom_call", output_to_operand_aliasing={{}: (10, {})} | custom-call | flops 402653184 | bytes 6291456 | tf_op jit(solution)/shard_map/output/pallas_call | solution.py:381
  (55 shorter events, 2.7 us)
Async XLA Ops:
  0.0 63.1 %copy-start.3 = (bf16[1024,256]{1,0:T(8,128)(2,1)S(1)}, bf16[1024,256]{1,0:T(8,128)(2,1)}, u32[]{:S(2)}) copy-start(bf16[1024,256]{1,0:T(8,128)(2,1)} %refs_5_.1) | copy-start | bytes 1572868
  0.0 63.1 %copy-start.2 = (bf16[1024,256]{1,0:T(8,128)(2,1)S(1)}, bf16[1024,256]{1,0:T(8,128)(2,1)}, u32[]{:S(2)}) copy-start(bf16[1024,256]{1,0:T(8,128)(2,1)} %refs_4_.1) | copy-start | bytes 1572868
  0.0 37.3 %copy-start.4 = (bf16[256,1024]{1,0:T(8,128)(2,1)S(1)}, bf16[256,1024]{1,0:T(8,128)(2,1)}, u32[]{:S(2)}) copy-start(bf16[256,1024]{1,0:T(8,128)(2,1)} %refs_0_.5) | copy-start | bytes 1572868
  2.0 17.3 %collective-permute-start.5 = (bf16[512,512]{1,0:T(8,128)(2,1)}, bf16[512,512]{1,0:T(8,128)(2,1)}, u32[]{:S(2)}, u32[]{:S(2)}) collective-permute-start(bf16[512,512]{1,0:T(8,128)(2,1)} %pick.1), channel_id=1, source_target_pairs={{0,4},{4,8},{8,12},{12,0},{1,5},{5,9},{9,13},{13,1},{2,6},{6,10},{... | collective-permute-start | bytes 1572872 | tf_op jit(solution)/shard_map/Zw1/ppermute | solution.py:426
  5.1 15.7 %collective-permute-start.3 = (bf16[256,1024]{1,0:T(8,128)(2,1)}, bf16[256,1024]{1,0:T(8,128)(2,1)S(1)}, u32[]{:S(2)}, u32[]{:S(2)}) collective-permute-start(bf16[256,1024]{1,0:T(8,128)(2,1)} %refs_0_.5), channel_id=1, source_target_pairs={{0,2},{2,0},{1,3},{3,1},{4,6},{6,4},{5,7},{7,5},{8,10},{10,8},{9,1... | collective-permute-start | bytes 1572872 | tf_op jit(solution)/shard_map/Ox/ppermute | solution.py:423
  6.5 15.8 %collective-permute-start.9 = (bf16[256,1024]{1,0:T(8,128)(2,1)}, bf16[256,1024]{1,0:T(8,128)(2,1)}, u32[]{:S(2)}, u32[]{:S(2)}) collective-permute-start(bf16[256,1024]{1,0:T(8,128)(2,1)} %refs_0_.5), channel_id=1, source_target_pairs={{0,1},{1,0},{2,3},{3,2},{4,5},{5,4},{6,7},{7,6},{8,9},{9,8},{10,11... | collective-permute-start | bytes 1572872 | tf_op jit(solution)/shard_map/Oc0/ppermute | solution.py:423
  11.6 24.3 %collective-permute-start = (bf16[128,4096]{1,0:T(8,128)(2,1)}, bf16[128,4096]{1,0:T(8,128)(2,1)S(1)}, u32[]{:S(2)}, u32[]{:S(2)}) collective-permute-start(bf16[128,4096]{1,0:T(8,128)(2,1)} %get-tuple-element.33), channel_id=1, source_target_pairs={{0,1},{1,0},{2,3},{3,2},{4,5},{5,4},{6,7},{7,6},{8,9},{9,8},{10,11... | collective-permute-start | bytes 3145736 | tf_op jit(solution)/shard_map/Tc/ppermute | solution.py:423
  12.2 29.6 %collective-permute-start.1 = (bf16[128,4096]{1,0:T(8,128)(2,1)}, bf16[128,4096]{1,0:T(8,128)(2,1)}, u32[]{:S(2)}, u32[]{:S(2)}) collective-permute-start(bf16[128,4096]{1,0:T(8,128)(2,1)} %get-tuple-element.34), channel_id=1, source_target_pairs={{0,2},{2,0},{1,3},{3,1},{4,6},{6,4},{5,7},{7,5},{8,10},{10,8},{9,1... | collective-permute-start | bytes 3145736 | tf_op jit(solution)/shard_map/Tx/ppermute | solution.py:423
  20.7 15.2 %collective-permute-start.7 = (bf16[512,512]{1,0:T(8,128)(2,1)}, bf16[512,512]{1,0:T(8,128)(2,1)S(1)}, u32[]{:S(2)}, u32[]{:S(2)}) collective-permute-start(bf16[512,512]{1,0:T(8,128)(2,1)} %collective-permute-done.5.refs_6_), channel_id=1, source_target_pairs={{0,4},{4,8},{8,12},{12,0},{1,5},{5,9},{9,13},{13,1},{2,6},{6,10},{... | collective-permute-start | bytes 1572872 | tf_op jit(solution)/shard_map/Zw2/ppermute | solution.py:426
  20.8 15.1 %collective-permute-start.6 = (bf16[512,512]{1,0:T(8,128)(2,1)}, bf16[512,512]{1,0:T(8,128)(2,1)S(1)}, u32[]{:S(2)}, u32[]{:S(2)}) collective-permute-start(bf16[512,512]{1,0:T(8,128)(2,1)} %collective-permute-done.5.refs_6_), channel_id=1, source_target_pairs={{0,16},{16,0},{1,17},{17,1},{2,18},{18,2},{3,19},{19,3},{4,20},{20... | collective-permute-start | bytes 1572872 | tf_op jit(solution)/shard_map/Yw1/ppermute | solution.py:423
  22.4 13.5 %collective-permute-start.10 = (bf16[256,1024]{1,0:T(8,128)(2,1)S(1)}, bf16[256,1024]{1,0:T(8,128)(2,1)S(1)}, u32[]{:S(2)}, u32[]{:S(2)}) collective-permute-start(bf16[256,1024]{1,0:T(8,128)(2,1)S(1)} %collective-permute-done.3.refs_1_), channel_id=1, source_target_pairs={{0,1},{1,0},{2,3},{3,2},{4,5},{5,4},{6,7},{7,6},{8,9},{9,8},{10,11... | collective-permute-start | bytes 1572872 | tf_op jit(solution)/shard_map/Oc0/ppermute | solution.py:423
  35.9 16.7 %collective-permute-start.11 = (bf16[512,512]{1,0:T(8,128)(2,1)S(1)}, bf16[512,512]{1,0:T(8,128)(2,1)S(1)}, u32[]{:S(2)}, u32[]{:S(2)}) collective-permute-start(bf16[512,512]{1,0:T(8,128)(2,1)S(1)} %collective-permute-done.7.refs_8_), channel_id=1, source_target_pairs={{0,4},{4,8},{8,12},{12,0},{1,5},{5,9},{9,13},{13,1},{2,6},{6,10},{... | collective-permute-start | bytes 1572872 | tf_op jit(solution)/shard_map/Zw3/ppermute | solution.py:426
  36.0 16.6 %collective-permute-start.8 = (bf16[512,512]{1,0:T(8,128)(2,1)S(1)}, bf16[512,512]{1,0:T(8,128)(2,1)S(1)}, u32[]{:S(2)}, u32[]{:S(2)}) collective-permute-start(bf16[512,512]{1,0:T(8,128)(2,1)S(1)} %collective-permute-done.7.refs_8_), channel_id=1, source_target_pairs={{0,16},{16,0},{1,17},{17,1},{2,18},{18,2},{3,19},{19,3},{4,20},{20... | collective-permute-start | bytes 1572872 | tf_op jit(solution)/shard_map/Yw2/ppermute | solution.py:423
  37.3 25.7 %collective-permute-start.2 = (bf16[128,4096]{1,0:T(8,128)(2,1)}, bf16[128,4096]{1,0:T(8,128)(2,1)S(1)}, u32[]{:S(2)}, u32[]{:S(2)}) collective-permute-start(bf16[128,4096]{1,0:T(8,128)(2,1)} %get-tuple-element.35), channel_id=1, source_target_pairs={{0,3},{1,2},{2,1},{3,0},{4,7},{5,6},{6,5},{7,4},{8,11},{9,10},{10,... | collective-permute-start | bytes 3145736 | tf_op jit(solution)/shard_map/Txc/ppermute | solution.py:466
  41.8 19.4 %collective-permute-start.4 = (bf16[2,128,1024]{2,1,0:T(8,128)(2,1)S(1)}, bf16[2,128,1024]{2,1,0:T(8,128)(2,1)S(1)}, u32[]{:S(2)}, u32[]{:S(2)}) collective-permute-start(bf16[2,128,1024]{2,1,0:T(8,128)(2,1)S(1)} %pair.1), channel_id=1, source_target_pairs={{0,4},{4,8},{8,12},{12,0},{1,5},{5,9},{9,13},{13,1},{2,6},{6,10},{... | collective-permute-start | bytes 1572872 | tf_op jit(solution)/shard_map/Zo1/ppermute | solution.py:426
  52.6 10.4 %collective-permute-start.12 = (bf16[512,512]{1,0:T(8,128)(2,1)S(1)}, bf16[512,512]{1,0:T(8,128)(2,1)S(1)}, u32[]{:S(2)}, u32[]{:S(2)}) collective-permute-start(bf16[512,512]{1,0:T(8,128)(2,1)S(1)} %collective-permute-done.11.refs_10_), channel_id=1, source_target_pairs={{0,16},{16,0},{1,17},{17,1},{2,18},{18,2},{3,19},{19,3},{4,20},{20... | collective-permute-start | bytes 1572872 | tf_op jit(solution)/shard_map/Yw3/ppermute | solution.py:423
  61.2 13.1 %collective-permute-start.13 = (bf16[2,128,1024]{2,1,0:T(8,128)(2,1)S(1)}, bf16[2,128,1024]{2,1,0:T(8,128)(2,1)S(1)}, u32[]{:S(2)}, u32[]{:S(2)}) collective-permute-start(bf16[2,128,1024]{2,1,0:T(8,128)(2,1)S(1)} %collective-permute-done.4.refs_4_), channel_id=1, source_target_pairs={{0,4},{4,8},{8,12},{12,0},{1,5},{5,9},{9,13},{13,1},{2,6},{6,10},{... | collective-permute-start | bytes 1572872 | tf_op jit(solution)/shard_map/Zo2/ppermute | solution.py:426
  61.2 13.1 %collective-permute-start.14 = (bf16[2,128,1024]{2,1,0:T(8,128)(2,1)S(1)}, bf16[2,128,1024]{2,1,0:T(8,128)(2,1)S(1)}, u32[]{:S(2)}, u32[]{:S(2)}) collective-permute-start(bf16[2,128,1024]{2,1,0:T(8,128)(2,1)S(1)} %collective-permute-done.4.refs_4_), channel_id=1, source_target_pairs={{0,16},{16,0},{1,17},{17,1},{2,18},{18,2},{3,19},{19,3},{4,20},{20... | collective-permute-start | bytes 1572872 | tf_op jit(solution)/shard_map/Yo1/ppermute | solution.py:423
  64.3 20.3 %copy-start.1 = (bf16[1,8192,256]{2,1,0:T(8,128)(2,1)S(1)}, bf16[1,8192,256]{2,1,0:T(8,128)(2,1)}, u32[]{:S(2)}) copy-start(bf16[1,8192,256]{2,1,0:T(8,128)(2,1)} %cache.3) | copy-start | bytes 12582916
  74.3 1.9 %collective-permute-start.15 = (f32[2,128,512]{2,1,0:T(8,128)S(1)}, f32[2,128,512]{2,1,0:T(8,128)S(1)}, u32[]{:S(2)}, u32[]{:S(2)}) collective-permute-start(f32[2,128,512]{2,1,0:T(8,128)S(1)} %get-tuple-element.43), channel_id=1, source_target_pairs={{0,1},{1,0},{2,3},{3,2},{4,5},{5,4},{6,7},{7,6},{8,9},{9,8},{10,11... | collective-permute-start | bytes 1572872 | tf_op jit(solution)/shard_map/Pc/ppermute | solution.py:423
  74.3 16.1 %collective-permute-start.17 = (bf16[2,128,1024]{2,1,0:T(8,128)(2,1)S(1)}, bf16[2,128,1024]{2,1,0:T(8,128)(2,1)S(1)}, u32[]{:S(2)}, u32[]{:S(2)}) collective-permute-start(bf16[2,128,1024]{2,1,0:T(8,128)(2,1)S(1)} %collective-permute-done.13.refs_8_), channel_id=1, source_target_pairs={{0,4},{4,8},{8,12},{12,0},{1,5},{5,9},{9,13},{13,1},{2,6},{6,10},{... | collective-permute-start | bytes 1572872 | tf_op jit(solution)/shard_map/Zo3/ppermute | solution.py:426
  74.3 16.1 %collective-permute-start.18 = (bf16[2,128,1024]{2,1,0:T(8,128)(2,1)S(1)}, bf16[2,128,1024]{2,1,0:T(8,128)(2,1)S(1)}, u32[]{:S(2)}, u32[]{:S(2)}) collective-permute-start(bf16[2,128,1024]{2,1,0:T(8,128)(2,1)S(1)} %collective-permute-done.13.refs_8_), channel_id=1, source_target_pairs={{0,16},{16,0},{1,17},{17,1},{2,18},{18,2},{3,19},{19,3},{4,20},{20... | collective-permute-start | bytes 1572872 | tf_op jit(solution)/shard_map/Yo2/ppermute | solution.py:423
  76.2 8.4 %collective-permute-start.16 = (f32[128,512]{1,0:T(8,128)S(1)}, f32[128,512]{1,0:T(8,128)S(1)}, u32[]{:S(2)}, u32[]{:S(2)}) collective-permute-start(f32[128,512]{1,0:T(8,128)S(1)} %fusion), channel_id=1, source_target_pairs={{0,2},{2,0},{1,3},{3,1},{4,6},{6,4},{5,7},{7,5},{8,10},{10,8},{9,1... | collective-permute-start | bytes 786440 | tf_op jit(solution)/shard_map/Px/ppermute | solution.py:423
  77.0 18.5 %collective-permute-start.24 = (bf16[2,128,1024]{2,1,0:T(8,128)(2,1)S(1)}, bf16[2,128,1024]{2,1,0:T(8,128)(2,1)S(1)}, u32[]{:S(2)}, u32[]{:S(2)}) collective-permute-start(bf16[2,128,1024]{2,1,0:T(8,128)(2,1)S(1)} %collective-permute-done.4.refs_4_), channel_id=1, source_target_pairs={{0,1},{1,0},{2,3},{3,2},{4,5},{5,4},{6,7},{7,6},{8,9},{9,8},{10,11... | collective-permute-start | bytes 1572872 | tf_op jit(solution)/shard_map/Oc1/ppermute | solution.py:423
  84.6 11.4 %collective-permute-start.25 = (bf16[2,128,1024]{2,1,0:T(8,128)(2,1)S(1)}, bf16[2,128,1024]{2,1,0:T(8,128)(2,1)S(1)}, u32[]{:S(2)}, u32[]{:S(2)}) collective-permute-start(bf16[2,128,1024]{2,1,0:T(8,128)(2,1)S(1)} %collective-permute-done.14.refs_5_), channel_id=1, source_target_pairs={{0,1},{1,0},{2,3},{3,2},{4,5},{5,4},{6,7},{7,6},{8,9},{9,8},{10,11... | collective-permute-start | bytes 1572872 | tf_op jit(solution)/shard_map/Oc1/ppermute | solution.py:423
  90.4 10.0 %collective-permute-start.22 = (bf16[128,1024]{1,0:T(8,128)(2,1)S(1)}, bf16[128,1024]{1,0:T(8,128)(2,1)S(1)}, u32[]{:S(2)}, u32[]{:S(2)}) collective-permute-start(bf16[128,1024]{1,0:T(8,128)(2,1)S(1)} %slice_bitcast_fusion.1), channel_id=1, source_target_pairs={{0,4},{4,8},{8,12},{12,0},{1,5},{5,9},{9,13},{13,1},{2,6},{6,10},{... | collective-permute-start | bytes 786440 | tf_op jit(solution)/shard_map/Zf3/ppermute | solution.py:426
  90.7 10.1 %collective-permute-start.21 = (bf16[128,1024]{1,0:T(8,128)(2,1)S(1)}, bf16[128,1024]{1,0:T(8,128)(2,1)S(1)}, u32[]{:S(2)}, u32[]{:S(2)}) collective-permute-start(bf16[128,1024]{1,0:T(8,128)(2,1)S(1)} %slice_bitcast_fusion.2), channel_id=1, source_target_pairs={{0,16},{16,0},{1,17},{17,1},{2,18},{18,2},{3,19},{19,3},{4,20},{20... | collective-permute-start | bytes 786440 | tf_op jit(solution)/shard_map/Yo3/ppermute | solution.py:423
  95.5 5.5 %collective-permute-start.23 = (bf16[2,128,1024]{2,1,0:T(8,128)(2,1)S(1)}, bf16[2,128,1024]{2,1,0:T(8,128)(2,1)S(1)}, u32[]{:S(2)}, u32[]{:S(2)}) collective-permute-start(bf16[2,128,1024]{2,1,0:T(8,128)(2,1)S(1)} %collective-permute-done.17.refs_2_), channel_id=1, source_target_pairs={{0,1},{1,0},{2,3},{3,2},{4,5},{5,4},{6,7},{7,6},{8,9},{9,8},{10,11... | collective-permute-start | bytes 1572872 | tf_op jit(solution)/shard_map/Oc/ppermute | solution.py:423
  95.5 5.4 %collective-permute-start.20 = (bf16[2,128,1024]{2,1,0:T(8,128)(2,1)S(1)}, bf16[2,128,1024]{2,1,0:T(8,128)(2,1)S(1)}, u32[]{:S(2)}, u32[]{:S(2)}) collective-permute-start(bf16[2,128,1024]{2,1,0:T(8,128)(2,1)S(1)} %collective-permute-done.18.refs_9_), channel_id=1, source_target_pairs={{0,1},{1,0},{2,3},{3,2},{4,5},{5,4},{6,7},{7,6},{8,9},{9,8},{10,11... | collective-permute-start | bytes 1572872 | tf_op jit(solution)/shard_map/Oc/ppermute | solution.py:423
  96.0 4.9 %collective-permute-start.19 = (bf16[2,128,1024]{2,1,0:T(8,128)(2,1)S(1)}, bf16[2,128,1024]{2,1,0:T(8,128)(2,1)S(1)}, u32[]{:S(2)}, u32[]{:S(2)}) collective-permute-start(bf16[2,128,1024]{2,1,0:T(8,128)(2,1)S(1)} %collective-permute-done.13.refs_8_), channel_id=1, source_target_pairs={{0,1},{1,0},{2,3},{3,2},{4,5},{5,4},{6,7},{7,6},{8,9},{9,8},{10,11... | collective-permute-start | bytes 1572872 | tf_op jit(solution)/shard_map/Oc/ppermute | solution.py:423
  100.4 1.5 %collective-permute-start.27 = (bf16[128,1024]{1,0:T(8,128)(2,1)S(1)}, bf16[128,1024]{1,0:T(8,128)(2,1)S(1)}, u32[]{:S(2)}, u32[]{:S(2)}) collective-permute-start(bf16[128,1024]{1,0:T(8,128)(2,1)S(1)} %collective-permute-done.22.refs_4_), channel_id=1, source_target_pairs={{0,1},{1,0},{2,3},{3,2},{4,5},{5,4},{6,7},{7,6},{8,9},{9,8},{10,11... | collective-permute-start | bytes 786440 | tf_op jit(solution)/shard_map/Oc/ppermute | solution.py:423
  100.8 1.5 %collective-permute-start.26 = (bf16[128,1024]{1,0:T(8,128)(2,1)S(1)}, bf16[128,1024]{1,0:T(8,128)(2,1)S(1)}, u32[]{:S(2)}, u32[]{:S(2)}) collective-permute-start(bf16[128,1024]{1,0:T(8,128)(2,1)S(1)} %collective-permute-done.21.refs_3_), channel_id=1, source_target_pairs={{0,1},{1,0},{2,3},{3,2},{4,5},{5,4},{6,7},{7,6},{8,9},{9,8},{10,11... | collective-permute-start | bytes 786440 | tf_op jit(solution)/shard_map/Oc/ppermute | solution.py:423
  (3 other events, 28.1 us)

commit v6 on v5

--- a/solution.py
+++ b/solution.py
@@ -11,6 +11,10 @@
 F32 = jnp.float32
 BF16 = jnp.bfloat16
 AXES = ("y", "z", "r", "x", "c")
+
+
+def along(v):
+    return v ^ (v >> 1)
 
 
 def params(mib):
@@ -78,7 +82,7 @@
         for k, out in enumerate(outs):
             part = (x ^ (k // 2)) * 2 + (c ^ (k % 2))
             for s in range(nz):
-                zz = lax.rem(z - s + nz, nz)
+                zz = along(lax.rem(along(z) - s + nz, nz))
                 for r in range(nr):
                     cols = pl.ds(pl.multiple_of(((zz * nr + r) * 4 + part) * bs, bs), bs)
                     v = tok[rows, cols].astype(F32) * inv * gain[:, cols]
@@ -325,7 +329,7 @@
     slots = wbuf.shape[0]
 
     def cols(s, dx, dc, r):
-        zz = lax.rem(z - s + nz, nz)
+        zz = along(lax.rem(along(z) - s + nz, nz))
         return pl.ds(pl.multiple_of(((zz * nr + r) * 4 + (x ^ dx) * 2 + (c ^ dc)) * bs, bs), bs)
 
     def load(b):
@@ -423,7 +427,7 @@
         return lax.ppermute(v, axis, [(0, 1), (1, 0)])
 
     def ring(v):
-        return lax.ppermute(v, "z", [(i, (i + 1) % nz) for i in range(nz)])
+        return lax.ppermute(v, "z", [(along(i), along((i + 1) % nz)) for i in range(nz)])
 
     own_q, own_kv, own_o = w_query, w_key_value, w_out
     if nr > 1:

time: 105 us -> 104 us (level)
  waiting for transfers between devices: 58.6 us -> 44.6 us
  starting transfers between devices: 17.5 us -> 30 us
    ppermute x7, waiting for transfers between devices: 43.3 us -> 30.9 us  [ring(): lax.ppermute(v, 'z', [(along(i), along((i + 1) % nz)) for i in range(nz)])]
    ppermute x7, starting transfers between devices: 5.94 us -> 15.7 us  [ring(): lax.ppermute(v, 'z', [(along(i), along((i + 1) % nz)) for i in range(nz)])]
    ppermute x20, waiting for transfers between devices: 14.4 us -> 11.4 us  [swap(): return lax.ppermute(v, axis, [(0, 1), (1, 0)])]
    ppermute x20, starting transfers between devices: 11.5 us -> 14.3 us  [swap(): return lax.ppermute(v, axis, [(0, 1), (1, 0)])]
    ppermute x1, waiting for transfers between devices: 0.83 us -> 2.3 us  [body(): corner = lax.ppermute(toks[3], ('x', 'c'), [(i, i ^ 3) for i in range(4)])]
  transfers between devices with their start and end apart: 28 -> 28, of which waited for: 13 -> 12; matrix products, arithmetic and copies ran while one was open for 1% -> 1% of each run, Pallas kernels for 20% -> 20%
where the time goes in v6:
time: 104 us
  waiting for transfers between devices  44.6 us (43%)
  starting transfers between devices  30 us (29%)
  Pallas kernels  25.6 us (25%)
  local copies, waits for them, and re-layouts  1.28 us (1%)
  other arithmetic  1.19 us (1%)
    ppermute x7, waiting for transfers between devices, ring(): lax.ppermute(v, 'z', [(along(i), along((i + 1) % nz)) for i in range(nz)])  30.9 us
    ppermute x7, starting transfers between devices, ring(): lax.ppermute(v, 'z', [(along(i), along((i + 1) % nz)) for i in range(nz)])  15.7 us
    ppermute x20, starting transfers between devices, swap(): return lax.ppermute(v, axis, [(0, 1), (1, 0)])  14.3 us
    ppermute x20, waiting for transfers between devices, swap(): return lax.ppermute(v, axis, [(0, 1), (1, 0)])  11.4 us
    pallas_call x2, Pallas kernels, output(): pl.pallas_call(functools.partial(out_kernel, plan=plan, nz=nz, nr=nr, bs=...  6.85 us
    pallas_call x1, Pallas kernels, normalise(): pl.pallas_call(functools.partial(norm_kernel, nz=nz, nr=nr, bs=bs, block=...  5.01 us
    pallas_call x1, Pallas kernels, attend_first(): pl.pallas_call(functools.partial(attend_first_kernel, heads=heads, scale=...  3.94 us
    pallas_call x1, Pallas kernels, project(): pl.pallas_call(functools.partial(project_kernel, halves=halves), in_specs...  3.91 us
  transfers between devices with their start and end apart: 28, of which 12 were waited for; matrix products, arithmetic and copies ran while one was open for 1% of the time, Pallas kernels for 20%

profile of v6, /device:TPU:0, one launch (start us, length us, event | category | flops | bytes accessed | tf_op | source)
XLA Modules:
  0.0 103.7 jit_solution(8367248929937957717)
XLA Ops:
  0.0 2.0 %pick.1 = bf16[512,512]{1,0:T(8,128)(2,1)} custom-call(bf16[1024,256]{1,0:T(8,128)(2,1)} %refs_4_.1, bf16[1024,256]{1,0:T(8,128)(2,1)} %refs_5_.1), custom_call_target="tpu_custom_call" | custom-call | bytes 1048576 | tf_op jit(solution)/shard_map/pick/pallas_call | solution.py:46
  2.0 3.1 %collective-permute-start.5 = (bf16[512,512]{1,0:T(8,128)(2,1)}, bf16[512,512]{1,0:T(8,128)(2,1)}, u32[]{:S(2)}, u32[]{:S(2)}) collective-permute-start(bf16[512,512]{1,0:T(8,128)(2,1)} %pick.1), channel_id=1, source_target_pairs={{0,4},{4,12},{12,8},{8,0},{1,5},{5,13},{13,9},{9,1},{2,6},{6,14},{... | collective-permute-start | bytes 1572872 | tf_op jit(solution)/shard_map/Zw1/ppermute | solution.py:430
  5.1 1.5 %collective-permute-start.3 = (bf16[256,1024]{1,0:T(8,128)(2,1)}, bf16[256,1024]{1,0:T(8,128)(2,1)S(1)}, u32[]{:S(2)}, u32[]{:S(2)}) collective-permute-start(bf16[256,1024]{1,0:T(8,128)(2,1)} %refs_0_.5), channel_id=1, source_target_pairs={{0,2},{2,0},{1,3},{3,1},{4,6},{6,4},{5,7},{7,5},{8,10},{10,8},{9,1... | collective-permute-start | bytes 1572872 | tf_op jit(solution)/shard_map/Ox/ppermute | solution.py:427
  6.6 5.0 %norm.1 = (bf16[128,4096]{1,0:T(8,128)(2,1)}, bf16[128,4096]{1,0:T(8,128)(2,1)}, bf16[128,4096]{1,0:T(8,128)(2,1)}, bf16[128,4096]{1,0:T(8,128)(2,1)}) custom-call(bf16[128,16384]{1,0:T(8,128)(2,1)} %tok.3, f32[1,16384]{1,0:T(1,128)} %bitcast.13), custom_call_target="tpu_custom_call" | custom-call | flops 16777216 | bytes 2097152 | tf_op jit(solution)/shard_map/norm/pallas_call | solution.py:96
  12.7 5.6 %collective-permute-done.5.refs_6_ = bf16[512,512]{1,0:T(8,128)(2,1)} collective-permute-done((bf16[512,512]{1,0:T(8,128)(2,1)}, bf16[512,512]{1,0:T(8,128)(2,1)}, u32[]{:S(2)}, u32[]{:S(2)}) %collective-permute-start.5) | collective-permute-done | bytes 524320 | tf_op jit(solution)/shard_map/Zw1/ppermute | solution.py:430
  19.7 0.9 collective-permute-start.7
  20.6 1.5 %collective-permute-start.6 = (bf16[512,512]{1,0:T(8,128)(2,1)}, bf16[512,512]{1,0:T(8,128)(2,1)S(1)}, u32[]{:S(2)}, u32[]{:S(2)}) collective-permute-start(bf16[512,512]{1,0:T(8,128)(2,1)} %collective-permute-done.5.refs_6_), channel_id=1, source_target_pairs={{0,16},{16,0},{1,17},{17,1},{2,18},{18,2},{3,19},{19,3},{4,20},{20... | collective-permute-start | bytes 1572872 | tf_op jit(solution)/shard_map/Yw1/ppermute | solution.py:427
  22.6 11.4 %collective-permute-done.7.refs_8_ = bf16[512,512]{1,0:T(8,128)(2,1)S(1)} collective-permute-done((bf16[512,512]{1,0:T(8,128)(2,1)}, bf16[512,512]{1,0:T(8,128)(2,1)S(1)}, u32[]{:S(2)}, u32[]{:S(2)}) %collective-permute-start.7) | collective-permute-done | bytes 524320 | tf_op jit(solution)/shard_map/Zw2/ppermute | solution.py:430
  34.0 2.7 %collective-permute-start.11 = (bf16[512,512]{1,0:T(8,128)(2,1)S(1)}, bf16[512,512]{1,0:T(8,128)(2,1)S(1)}, u32[]{:S(2)}, u32[]{:S(2)}) collective-permute-start(bf16[512,512]{1,0:T(8,128)(2,1)S(1)} %collective-permute-done.7.refs_8_), channel_id=1, source_target_pairs={{0,4},{4,12},{12,8},{8,0},{1,5},{5,13},{13,9},{9,1},{2,6},{6,14},{... | collective-permute-start | bytes 1572872 | tf_op jit(solution)/shard_map/Zw3/ppermute | solution.py:430
  36.7 1.5 %collective-permute-start.8 = (bf16[512,512]{1,0:T(8,128)(2,1)S(1)}, bf16[512,512]{1,0:T(8,128)(2,1)S(1)}, u32[]{:S(2)}, u32[]{:S(2)}) collective-permute-start(bf16[512,512]{1,0:T(8,128)(2,1)S(1)} %collective-permute-done.7.refs_8_), channel_id=1, source_target_pairs={{0,16},{16,0},{1,17},{17,1},{2,18},{18,2},{3,19},{19,3},{4,20},{20... | collective-permute-start | bytes 1572872 | tf_op jit(solution)/shard_map/Yw2/ppermute | solution.py:427
  38.3 2.9 %collective-permute-done.1.refs_2_ = bf16[128,4096]{1,0:T(8,128)(2,1)} collective-permute-done((bf16[128,4096]{1,0:T(8,128)(2,1)}, bf16[128,4096]{1,0:T(8,128)(2,1)}, u32[]{:S(2)}, u32[]{:S(2)}) %collective-permute-start.1) | collective-permute-done | bytes 1048608 | tf_op jit(solution)/shard_map/Tx/ppermute | solution.py:427
  41.2 3.6 %collective-permute-start.4 = (bf16[2,128,1024]{2,1,0:T(8,128)(2,1)S(1)}, bf16[2,128,1024]{2,1,0:T(8,128)(2,1)S(1)}, u32[]{:S(2)}, u32[]{:S(2)}) collective-permute-start(bf16[2,128,1024]{2,1,0:T(8,128)(2,1)S(1)} %pair.1), channel_id=1, source_target_pairs={{0,4},{4,12},{12,8},{8,0},{1,5},{5,13},{13,9},{9,1},{2,6},{6,14},{... | collective-permute-start | bytes 1572872 | tf_op jit(solution)/shard_map/Zo1/ppermute | solution.py:430
  44.8 5.0 %collective-permute-done.11.refs_10_ = bf16[512,512]{1,0:T(8,128)(2,1)S(1)} collective-permute-done((bf16[512,512]{1,0:T(8,128)(2,1)S(1)}, bf16[512,512]{1,0:T(8,128)(2,1)S(1)}, u32[]{:S(2)}, u32[]{:S(2)}) %collective-permute-start.11) | collective-permute-done | bytes 524320 | tf_op jit(solution)/shard_map/Zw3/ppermute | solution.py:430
  49.8 1.3 %collective-permute-start.12 = (bf16[512,512]{1,0:T(8,128)(2,1)S(1)}, bf16[512,512]{1,0:T(8,128)(2,1)S(1)}, u32[]{:S(2)}, u32[]{:S(2)}) collective-permute-start(bf16[512,512]{1,0:T(8,128)(2,1)S(1)} %collective-permute-done.11.refs_10_), channel_id=1, source_target_pairs={{0,16},{16,0},{1,17},{17,1},{2,18},{18,2},{3,19},{19,3},{4,20},{20... | collective-permute-start | bytes 1572872 | tf_op jit(solution)/shard_map/Yw3/ppermute | solution.py:427
  51.1 7.3 %collective-permute-done.4.refs_4_ = bf16[2,128,1024]{2,1,0:T(8,128)(2,1)S(1)} collective-permute-done((bf16[2,128,1024]{2,1,0:T(8,128)(2,1)S(1)}, bf16[2,128,1024]{2,1,0:T(8,128)(2,1)S(1)}, u32[]{:S(2)}, u32[]{:S(2)}) %collective-permute-start.4) | collective-permute-done | bytes 524320 | tf_op jit(solution)/shard_map/Zo1/ppermute | solution.py:430
  58.4 1.7 %collective-permute-start.13 = (bf16[2,128,1024]{2,1,0:T(8,128)(2,1)S(1)}, bf16[2,128,1024]{2,1,0:T(8,128)(2,1)S(1)}, u32[]{:S(2)}, u32[]{:S(2)}) collective-permute-start(bf16[2,128,1024]{2,1,0:T(8,128)(2,1)S(1)} %collective-permute-done.4.refs_4_), channel_id=1, source_target_pairs={{0,4},{4,12},{12,8},{8,0},{1,5},{5,13},{13,9},{9,1},{2,6},{6,14},{... | collective-permute-start | bytes 1572872 | tf_op jit(solution)/shard_map/Zo2/ppermute | solution.py:430
  60.0 1.5 %collective-permute-start.14 = (bf16[2,128,1024]{2,1,0:T(8,128)(2,1)S(1)}, bf16[2,128,1024]{2,1,0:T(8,128)(2,1)S(1)}, u32[]{:S(2)}, u32[]{:S(2)}) collective-permute-start(bf16[2,128,1024]{2,1,0:T(8,128)(2,1)S(1)} %collective-permute-done.4.refs_4_), channel_id=1, source_target_pairs={{0,16},{16,0},{1,17},{17,1},{2,18},{18,2},{3,19},{19,3},{4,20},{20... | collective-permute-start | bytes 1572872 | tf_op jit(solution)/shard_map/Yo1/ppermute | solution.py:427
  61.6 2.3 %collective-permute-done.2.refs_3_ = bf16[128,4096]{1,0:T(8,128)(2,1)S(1)} collective-permute-done((bf16[128,4096]{1,0:T(8,128)(2,1)}, bf16[128,4096]{1,0:T(8,128)(2,1)S(1)}, u32[]{:S(2)}, u32[]{:S(2)}) %collective-permute-start.2) | collective-permute-done | bytes 1048608 | tf_op jit(solution)/shard_map/Txc/ppermute | solution.py:470
  63.9 1.2 %copy-done.5 = bf16[128,4096]{1,0:T(8,128)(2,1)S(1)} copy-done((bf16[128,4096]{1,0:T(8,128)(2,1)S(1)}, bf16[128,4096]{1,0:T(8,128)(2,1)}, u32[]{:S(2)}) %copy-start.5) | copy-done | bytes 1048600
  65.1 3.9 %project.1 = (f32[128,512]{1,0:T(8,128)S(1)}, f32[2,128,512]{2,1,0:T(8,128)S(1)}, f32[128,512]{1,0:T(8,128)S(1)}) custom-call(bf16[128,4096]{1,0:T(8,128)(2,1)S(1)} %copy-done.5, bf16[128,4096]{1,0:T(8,128)(2,1)S(1)} %collective-permute-done.refs_1_, bf16[128,4096]{1,0:T(8,128)(2,1)} %collective-permute-done.1.refs_2_, ...), custom_call_target="tpu_custom_call" | custom-call | flops 2147483648 | bytes 2097152 | tf_op jit(solution)/shard_map/project/pallas_call | solution.py:163
  69.0 1.5 %collective-permute-done.13.refs_8_ = bf16[2,128,1024]{2,1,0:T(8,128)(2,1)S(1)} collective-permute-done((bf16[2,128,1024]{2,1,0:T(8,128)(2,1)S(1)}, bf16[2,128,1024]{2,1,0:T(8,128)(2,1)S(1)}, u32[]{:S(2)}, u32[]{:S(2)}) %collective-permute-start.13) | collective-permute-done | bytes 524320 | tf_op jit(solution)/shard_map/Zo2/ppermute | solution.py:430
  70.6 2.0 %collective-permute-start.17 = (bf16[2,128,1024]{2,1,0:T(8,128)(2,1)S(1)}, bf16[2,128,1024]{2,1,0:T(8,128)(2,1)S(1)}, u32[]{:S(2)}, u32[]{:S(2)}) collective-permute-start(bf16[2,128,1024]{2,1,0:T(8,128)(2,1)S(1)} %collective-permute-done.13.refs_8_), channel_id=1, source_target_pairs={{0,4},{4,12},{12,8},{8,0},{1,5},{5,13},{13,9},{9,1},{2,6},{6,14},{... | collective-permute-start | bytes 1572872 | tf_op jit(solution)/shard_map/Zo3/ppermute | solution.py:430
  72.6 1.5 %collective-permute-start.18 = (bf16[2,128,1024]{2,1,0:T(8,128)(2,1)S(1)}, bf16[2,128,1024]{2,1,0:T(8,128)(2,1)S(1)}, u32[]{:S(2)}, u32[]{:S(2)}) collective-permute-start(bf16[2,128,1024]{2,1,0:T(8,128)(2,1)S(1)} %collective-permute-done.13.refs_8_), channel_id=1, source_target_pairs={{0,16},{16,0},{1,17},{17,1},{2,18},{18,2},{3,19},{19,3},{4,20},{20... | collective-permute-start | bytes 1572872 | tf_op jit(solution)/shard_map/Yo2/ppermute | solution.py:427
  74.2 1.6 %collective-permute-start.16 = (f32[128,512]{1,0:T(8,128)S(1)}, f32[128,512]{1,0:T(8,128)S(1)}, u32[]{:S(2)}, u32[]{:S(2)}) collective-permute-start(f32[128,512]{1,0:T(8,128)S(1)} %fusion), channel_id=1, source_target_pairs={{0,2},{2,0},{1,3},{3,1},{4,6},{6,4},{5,7},{7,5},{8,10},{10,8},{9,1... | collective-permute-start | bytes 786440 | tf_op jit(solution)/shard_map/Px/ppermute | solution.py:427
  75.8 6.7 %collective-permute-done.16.other = f32[128,512]{1,0:T(8,128)S(1)} collective-permute-done((f32[128,512]{1,0:T(8,128)S(1)}, f32[128,512]{1,0:T(8,128)S(1)}, u32[]{:S(2)}, u32[]{:S(2)}) %collective-permute-start.16) | collective-permute-done | bytes 262176 | tf_op jit(solution)/shard_map/Px/ppermute | solution.py:427
  82.4 3.9 %attend_first.1 = (bf16[256,128]{1,0:T(8,128)(2,1)S(1)}, f32[3,256,128]{2,1,0:T(8,128)S(1)}) custom-call(s32[16]{0:T(128)S(1)} %copy-done.6, f32[128,512]{1,0:T(8,128)S(1)} %get-tuple-element.41.mine, f32[2,128,512]{2,1,0:T(8,128)S(1)} %collective-permute-done.15.core, f32[128,512]{1,0:T(8,128)S(1)} %collective-permute-done.16.other, ...), custom_call_target="tpu_custom_call" | custom-call | flops 536870912 | bytes 14680064 | tf_op jit(solution)/shard_map/attend_first/pallas_call | solution.py:278
  86.7 1.7 %collective-permute-start.22 = (bf16[128,1024]{1,0:T(8,128)(2,1)S(1)}, bf16[128,1024]{1,0:T(8,128)(2,1)S(1)}, u32[]{:S(2)}, u32[]{:S(2)}) collective-permute-start(bf16[128,1024]{1,0:T(8,128)(2,1)S(1)} %slice_bitcast_fusion.1), channel_id=1, source_target_pairs={{0,4},{4,12},{12,8},{8,0},{1,5},{5,13},{13,9},{9,1},{2,6},{6,14},{... | collective-permute-start | bytes 786440 | tf_op jit(solution)/shard_map/Zf3/ppermute | solution.py:430
  88.5 1.6 %collective-permute-start.21 = (bf16[128,1024]{1,0:T(8,128)(2,1)S(1)}, bf16[128,1024]{1,0:T(8,128)(2,1)S(1)}, u32[]{:S(2)}, u32[]{:S(2)}) collective-permute-start(bf16[128,1024]{1,0:T(8,128)(2,1)S(1)} %slice_bitcast_fusion.2), channel_id=1, source_target_pairs={{0,16},{16,0},{1,17},{17,1},{2,18},{18,2},{3,19},{19,3},{4,20},{20... | collective-permute-start | bytes 786440 | tf_op jit(solution)/shard_map/Yo3/ppermute | solution.py:427
  90.1 3.9 %attend_last.1.att = bf16[128,256]{1,0:T(8,128)(2,1)S(1)} custom-call(s32[16]{0:T(128)S(1)} %copy-done.6, bf16[256,128]{1,0:T(8,128)(2,1)S(1)} %get-tuple-element.45.q, f32[3,256,128]{2,1,0:T(8,128)S(1)} %get-tuple-element.47.state, bf16[1,8192,256]{2,1,0:T(8,128)(2,1)S(1)} %copy-done.1), custom_call_target="tpu_custom_call" | custom-call | flops 536870912 | bytes 14680064 | tf_op jit(solution)/shard_map/attend_last/pallas_call | solution.py:304
  94.6 4.1 %output.2.refs_8_ = bf16[128,16384]{1,0:T(8,128)(2,1)} custom-call(bf16[128,256]{1,0:T(8,128)(2,1)S(1)} %attend_last.1.att, bf16[128,16384]{1,0:T(8,128)(2,1)S(1)} %copy-done, bf16[256,1024]{1,0:T(8,128)(2,1)S(1)} %copy-done.4, bf16[256,1024]{1,0:T(8,128)(2,1)S(1)} %collective-permute-done.3.refs_1_, bf16[256,1024]{1,0:T(8,128)(2,1)} %collective-permute-done.9.refs_2_, ...), custom_call_target="tpu_custom_call" | custom-call | flops 671088640 | bytes 10485760 | tf_op jit(solution)/shard_map/output/pallas_call | solution.py:385
  99.4 1.1 %collective-permute-done.27.refs_7_ = bf16[128,1024]{1,0:T(8,128)(2,1)S(1)} collective-permute-done((bf16[128,1024]{1,0:T(8,128)(2,1)S(1)}, bf16[128,1024]{1,0:T(8,128)(2,1)S(1)}, u32[]{:S(2)}, u32[]{:S(2)}) %collective-permute-start.27) | collective-permute-done | bytes 262176 | tf_op jit(solution)/shard_map/Oc/ppermute | solution.py:427
  100.8 2.7 %output.3 = bf16[128,16384]{1,0:T(8,128)(2,1)} custom-call(bf16[128,256]{1,0:T(8,128)(2,1)S(1)} %attend_last.1.att, bf16[128,16384]{1,0:T(8,128)(2,1)S(1)} %copy-done, bf16[2,128,1024]{2,1,0:T(8,128)(2,1)S(1)} %collective-permute-done.19.refs_0_, bf16[2,128,1024]{2,1,0:T(8,128)(2,1)S(1)} %collective-permute-done.20.refs_1_, ...), custom_call_target="tpu_custom_call", output_to_operand_aliasing={{}: (10, {})} | custom-call | flops 402653184 | bytes 6291456 | tf_op jit(solution)/shard_map/output/pallas_call | solution.py:385
  (55 shorter events, 4.4 us)
Async XLA Ops:
  0.0 63.9 %copy-start.3 = (bf16[1024,256]{1,0:T(8,128)(2,1)S(1)}, bf16[1024,256]{1,0:T(8,128)(2,1)}, u32[]{:S(2)}) copy-start(bf16[1024,256]{1,0:T(8,128)(2,1)} %refs_5_.1) | copy-start | bytes 1572868
  0.0 63.9 %copy-start.2 = (bf16[1024,256]{1,0:T(8,128)(2,1)S(1)}, bf16[1024,256]{1,0:T(8,128)(2,1)}, u32[]{:S(2)}) copy-start(bf16[1024,256]{1,0:T(8,128)(2,1)} %refs_4_.1) | copy-start | bytes 1572868
  0.0 38.2 %copy-start.4 = (bf16[256,1024]{1,0:T(8,128)(2,1)S(1)}, bf16[256,1024]{1,0:T(8,128)(2,1)}, u32[]{:S(2)}) copy-start(bf16[256,1024]{1,0:T(8,128)(2,1)} %refs_0_.5) | copy-start | bytes 1572868
  0.0 18.3 %copy-start.6 = (s32[16]{0:T(128)S(1)}, s32[16]{0:T(128)}, u32[]{:S(2)}) copy-start(s32[16]{0:T(128)} %lens.3) | copy-start | bytes 196
  2.0 16.3 %collective-permute-start.5 = (bf16[512,512]{1,0:T(8,128)(2,1)}, bf16[512,512]{1,0:T(8,128)(2,1)}, u32[]{:S(2)}, u32[]{:S(2)}) collective-permute-start(bf16[512,512]{1,0:T(8,128)(2,1)} %pick.1), channel_id=1, source_target_pairs={{0,4},{4,12},{12,8},{8,0},{1,5},{5,13},{13,9},{9,1},{2,6},{6,14},{... | collective-permute-start | bytes 1572872 | tf_op jit(solution)/shard_map/Zw1/ppermute | solution.py:430
  5.1 15.5 %collective-permute-start.3 = (bf16[256,1024]{1,0:T(8,128)(2,1)}, bf16[256,1024]{1,0:T(8,128)(2,1)S(1)}, u32[]{:S(2)}, u32[]{:S(2)}) collective-permute-start(bf16[256,1024]{1,0:T(8,128)(2,1)} %refs_0_.5), channel_id=1, source_target_pairs={{0,2},{2,0},{1,3},{3,1},{4,6},{6,4},{5,7},{7,5},{8,10},{10,8},{9,1... | collective-permute-start | bytes 1572872 | tf_op jit(solution)/shard_map/Ox/ppermute | solution.py:427
  6.5 15.6 %collective-permute-start.9 = (bf16[256,1024]{1,0:T(8,128)(2,1)}, bf16[256,1024]{1,0:T(8,128)(2,1)}, u32[]{:S(2)}, u32[]{:S(2)}) collective-permute-start(bf16[256,1024]{1,0:T(8,128)(2,1)} %refs_0_.5), channel_id=1, source_target_pairs={{0,1},{1,0},{2,3},{3,2},{4,5},{5,4},{6,7},{7,6},{8,9},{9,8},{10,11... | collective-permute-start | bytes 1572872 | tf_op jit(solution)/shard_map/Oc0/ppermute | solution.py:427
  11.6 22.4 %collective-permute-start = (bf16[128,4096]{1,0:T(8,128)(2,1)}, bf16[128,4096]{1,0:T(8,128)(2,1)S(1)}, u32[]{:S(2)}, u32[]{:S(2)}) collective-permute-start(bf16[128,4096]{1,0:T(8,128)(2,1)} %get-tuple-element.33), channel_id=1, source_target_pairs={{0,1},{1,0},{2,3},{3,2},{4,5},{5,4},{6,7},{7,6},{8,9},{9,8},{10,11... | collective-permute-start | bytes 3145736 | tf_op jit(solution)/shard_map/Tc/ppermute | solution.py:427
  12.2 29.1 %collective-permute-start.1 = (bf16[128,4096]{1,0:T(8,128)(2,1)}, bf16[128,4096]{1,0:T(8,128)(2,1)}, u32[]{:S(2)}, u32[]{:S(2)}) collective-permute-start(bf16[128,4096]{1,0:T(8,128)(2,1)} %get-tuple-element.34), channel_id=1, source_target_pairs={{0,2},{2,0},{1,3},{3,1},{4,6},{6,4},{5,7},{7,5},{8,10},{10,8},{9,1... | collective-permute-start | bytes 3145736 | tf_op jit(solution)/shard_map/Tx/ppermute | solution.py:427
  19.7 14.3 %collective-permute-start.7 = (bf16[512,512]{1,0:T(8,128)(2,1)}, bf16[512,512]{1,0:T(8,128)(2,1)S(1)}, u32[]{:S(2)}, u32[]{:S(2)}) collective-permute-start(bf16[512,512]{1,0:T(8,128)(2,1)} %collective-permute-done.5.refs_6_), channel_id=1, source_target_pairs={{0,4},{4,12},{12,8},{8,0},{1,5},{5,13},{13,9},{9,1},{2,6},{6,14},{... | collective-permute-start | bytes 1572872 | tf_op jit(solution)/shard_map/Zw2/ppermute | solution.py:430
  20.6 13.4 %collective-permute-start.6 = (bf16[512,512]{1,0:T(8,128)(2,1)}, bf16[512,512]{1,0:T(8,128)(2,1)S(1)}, u32[]{:S(2)}, u32[]{:S(2)}) collective-permute-start(bf16[512,512]{1,0:T(8,128)(2,1)} %collective-permute-done.5.refs_6_), channel_id=1, source_target_pairs={{0,16},{16,0},{1,17},{17,1},{2,18},{18,2},{3,19},{19,3},{4,20},{20... | collective-permute-start | bytes 1572872 | tf_op jit(solution)/shard_map/Yw1/ppermute | solution.py:427
  22.1 11.9 %collective-permute-start.10 = (bf16[256,1024]{1,0:T(8,128)(2,1)S(1)}, bf16[256,1024]{1,0:T(8,128)(2,1)S(1)}, u32[]{:S(2)}, u32[]{:S(2)}) collective-permute-start(bf16[256,1024]{1,0:T(8,128)(2,1)S(1)} %collective-permute-done.3.refs_1_), channel_id=1, source_target_pairs={{0,1},{1,0},{2,3},{3,2},{4,5},{5,4},{6,7},{7,6},{8,9},{9,8},{10,11... | collective-permute-start | bytes 1572872 | tf_op jit(solution)/shard_map/Oc0/ppermute | solution.py:427
  34.0 15.8 %collective-permute-start.11 = (bf16[512,512]{1,0:T(8,128)(2,1)S(1)}, bf16[512,512]{1,0:T(8,128)(2,1)S(1)}, u32[]{:S(2)}, u32[]{:S(2)}) collective-permute-start(bf16[512,512]{1,0:T(8,128)(2,1)S(1)} %collective-permute-done.7.refs_8_), channel_id=1, source_target_pairs={{0,4},{4,12},{12,8},{8,0},{1,5},{5,13},{13,9},{9,1},{2,6},{6,14},{... | collective-permute-start | bytes 1572872 | tf_op jit(solution)/shard_map/Zw3/ppermute | solution.py:430
  36.7 13.1 %collective-permute-start.8 = (bf16[512,512]{1,0:T(8,128)(2,1)S(1)}, bf16[512,512]{1,0:T(8,128)(2,1)S(1)}, u32[]{:S(2)}, u32[]{:S(2)}) collective-permute-start(bf16[512,512]{1,0:T(8,128)(2,1)S(1)} %collective-permute-done.7.refs_8_), channel_id=1, source_target_pairs={{0,16},{16,0},{1,17},{17,1},{2,18},{18,2},{3,19},{19,3},{4,20},{20... | collective-permute-start | bytes 1572872 | tf_op jit(solution)/shard_map/Yw2/ppermute | solution.py:427
  38.2 25.6 %collective-permute-start.2 = (bf16[128,4096]{1,0:T(8,128)(2,1)}, bf16[128,4096]{1,0:T(8,128)(2,1)S(1)}, u32[]{:S(2)}, u32[]{:S(2)}) collective-permute-start(bf16[128,4096]{1,0:T(8,128)(2,1)} %get-tuple-element.35), channel_id=1, source_target_pairs={{0,3},{1,2},{2,1},{3,0},{4,7},{5,6},{6,5},{7,4},{8,11},{9,10},{10,... | collective-permute-start | bytes 3145736 | tf_op jit(solution)/shard_map/Txc/ppermute | solution.py:470
  41.2 17.1 %collective-permute-start.4 = (bf16[2,128,1024]{2,1,0:T(8,128)(2,1)S(1)}, bf16[2,128,1024]{2,1,0:T(8,128)(2,1)S(1)}, u32[]{:S(2)}, u32[]{:S(2)}) collective-permute-start(bf16[2,128,1024]{2,1,0:T(8,128)(2,1)S(1)} %pair.1), channel_id=1, source_target_pairs={{0,4},{4,12},{12,8},{8,0},{1,5},{5,13},{13,9},{9,1},{2,6},{6,14},{... | collective-permute-start | bytes 1572872 | tf_op jit(solution)/shard_map/Zo1/ppermute | solution.py:430
  49.8 14.0 %collective-permute-start.12 = (bf16[512,512]{1,0:T(8,128)(2,1)S(1)}, bf16[512,512]{1,0:T(8,128)(2,1)S(1)}, u32[]{:S(2)}, u32[]{:S(2)}) collective-permute-start(bf16[512,512]{1,0:T(8,128)(2,1)S(1)} %collective-permute-done.11.refs_10_), channel_id=1, source_target_pairs={{0,16},{16,0},{1,17},{17,1},{2,18},{18,2},{3,19},{19,3},{4,20},{20... | collective-permute-start | bytes 1572872 | tf_op jit(solution)/shard_map/Yw3/ppermute | solution.py:427
  58.4 12.2 %collective-permute-start.13 = (bf16[2,128,1024]{2,1,0:T(8,128)(2,1)S(1)}, bf16[2,128,1024]{2,1,0:T(8,128)(2,1)S(1)}, u32[]{:S(2)}, u32[]{:S(2)}) collective-permute-start(bf16[2,128,1024]{2,1,0:T(8,128)(2,1)S(1)} %collective-permute-done.4.refs_4_), channel_id=1, source_target_pairs={{0,4},{4,12},{12,8},{8,0},{1,5},{5,13},{13,9},{9,1},{2,6},{6,14},{... | collective-permute-start | bytes 1572872 | tf_op jit(solution)/shard_map/Zo2/ppermute | solution.py:430
  60.0 10.6 %collective-permute-start.14 = (bf16[2,128,1024]{2,1,0:T(8,128)(2,1)S(1)}, bf16[2,128,1024]{2,1,0:T(8,128)(2,1)S(1)}, u32[]{:S(2)}, u32[]{:S(2)}) collective-permute-start(bf16[2,128,1024]{2,1,0:T(8,128)(2,1)S(1)} %collective-permute-done.4.refs_4_), channel_id=1, source_target_pairs={{0,16},{16,0},{1,17},{17,1},{2,18},{18,2},{3,19},{19,3},{4,20},{20... | collective-permute-start | bytes 1572872 | tf_op jit(solution)/shard_map/Yo1/ppermute | solution.py:427
  70.6 3.6 %collective-permute-start.15 = (f32[2,128,512]{2,1,0:T(8,128)S(1)}, f32[2,128,512]{2,1,0:T(8,128)S(1)}, u32[]{:S(2)}, u32[]{:S(2)}) collective-permute-start(f32[2,128,512]{2,1,0:T(8,128)S(1)} %get-tuple-element.43), channel_id=1, source_target_pairs={{0,1},{1,0},{2,3},{3,2},{4,5},{5,4},{6,7},{7,6},{8,9},{9,8},{10,11... | collective-permute-start | bytes 1572872 | tf_op jit(solution)/shard_map/Pc/ppermute | solution.py:427
  70.6 15.8 %collective-permute-start.17 = (bf16[2,128,1024]{2,1,0:T(8,128)(2,1)S(1)}, bf16[2,128,1024]{2,1,0:T(8,128)(2,1)S(1)}, u32[]{:S(2)}, u32[]{:S(2)}) collective-permute-start(bf16[2,128,1024]{2,1,0:T(8,128)(2,1)S(1)} %collective-permute-done.13.refs_8_), channel_id=1, source_target_pairs={{0,4},{4,12},{12,8},{8,0},{1,5},{5,13},{13,9},{9,1},{2,6},{6,14},{... | collective-permute-start | bytes 1572872 | tf_op jit(solution)/shard_map/Zo3/ppermute | solution.py:430
  72.6 14.1 %collective-permute-start.18 = (bf16[2,128,1024]{2,1,0:T(8,128)(2,1)S(1)}, bf16[2,128,1024]{2,1,0:T(8,128)(2,1)S(1)}, u32[]{:S(2)}, u32[]{:S(2)}) collective-permute-start(bf16[2,128,1024]{2,1,0:T(8,128)(2,1)S(1)} %collective-permute-done.13.refs_8_), channel_id=1, source_target_pairs={{0,16},{16,0},{1,17},{17,1},{2,18},{18,2},{3,19},{19,3},{4,20},{20... | collective-permute-start | bytes 1572872 | tf_op jit(solution)/shard_map/Yo2/ppermute | solution.py:427
  74.2 8.2 %collective-permute-start.16 = (f32[128,512]{1,0:T(8,128)S(1)}, f32[128,512]{1,0:T(8,128)S(1)}, u32[]{:S(2)}, u32[]{:S(2)}) collective-permute-start(f32[128,512]{1,0:T(8,128)S(1)} %fusion), channel_id=1, source_target_pairs={{0,2},{2,0},{1,3},{3,1},{4,6},{6,4},{5,7},{7,5},{8,10},{10,8},{9,1... | collective-permute-start | bytes 786440 | tf_op jit(solution)/shard_map/Px/ppermute | solution.py:427
  75.8 18.3 %collective-permute-start.24 = (bf16[2,128,1024]{2,1,0:T(8,128)(2,1)S(1)}, bf16[2,128,1024]{2,1,0:T(8,128)(2,1)S(1)}, u32[]{:S(2)}, u32[]{:S(2)}) collective-permute-start(bf16[2,128,1024]{2,1,0:T(8,128)(2,1)S(1)} %collective-permute-done.4.refs_4_), channel_id=1, source_target_pairs={{0,1},{1,0},{2,3},{3,2},{4,5},{5,4},{6,7},{7,6},{8,9},{9,8},{10,11... | collective-permute-start | bytes 1572872 | tf_op jit(solution)/shard_map/Oc1/ppermute | solution.py:427
  82.4 12.1 %collective-permute-start.25 = (bf16[2,128,1024]{2,1,0:T(8,128)(2,1)S(1)}, bf16[2,128,1024]{2,1,0:T(8,128)(2,1)S(1)}, u32[]{:S(2)}, u32[]{:S(2)}) collective-permute-start(bf16[2,128,1024]{2,1,0:T(8,128)(2,1)S(1)} %collective-permute-done.14.refs_5_), channel_id=1, source_target_pairs={{0,1},{1,0},{2,3},{3,2},{4,5},{5,4},{6,7},{7,6},{8,9},{9,8},{10,11... | collective-permute-start | bytes 1572872 | tf_op jit(solution)/shard_map/Oc1/ppermute | solution.py:427
  86.7 12.1 %collective-permute-start.22 = (bf16[128,1024]{1,0:T(8,128)(2,1)S(1)}, bf16[128,1024]{1,0:T(8,128)(2,1)S(1)}, u32[]{:S(2)}, u32[]{:S(2)}) collective-permute-start(bf16[128,1024]{1,0:T(8,128)(2,1)S(1)} %slice_bitcast_fusion.1), channel_id=1, source_target_pairs={{0,4},{4,12},{12,8},{8,0},{1,5},{5,13},{13,9},{9,1},{2,6},{6,14},{... | collective-permute-start | bytes 786440 | tf_op jit(solution)/shard_map/Zf3/ppermute | solution.py:430
  88.5 10.8 %collective-permute-start.21 = (bf16[128,1024]{1,0:T(8,128)(2,1)S(1)}, bf16[128,1024]{1,0:T(8,128)(2,1)S(1)}, u32[]{:S(2)}, u32[]{:S(2)}) collective-permute-start(bf16[128,1024]{1,0:T(8,128)(2,1)S(1)} %slice_bitcast_fusion.2), channel_id=1, source_target_pairs={{0,16},{16,0},{1,17},{17,1},{2,18},{18,2},{3,19},{19,3},{4,20},{20... | collective-permute-start | bytes 786440 | tf_op jit(solution)/shard_map/Yo3/ppermute | solution.py:427
  94.0 5.4 %collective-permute-start.23 = (bf16[2,128,1024]{2,1,0:T(8,128)(2,1)S(1)}, bf16[2,128,1024]{2,1,0:T(8,128)(2,1)S(1)}, u32[]{:S(2)}, u32[]{:S(2)}) collective-permute-start(bf16[2,128,1024]{2,1,0:T(8,128)(2,1)S(1)} %collective-permute-done.17.refs_2_), channel_id=1, source_target_pairs={{0,1},{1,0},{2,3},{3,2},{4,5},{5,4},{6,7},{7,6},{8,9},{9,8},{10,11... | collective-permute-start | bytes 1572872 | tf_op jit(solution)/shard_map/Oc/ppermute | solution.py:427
  94.1 5.3 %collective-permute-start.20 = (bf16[2,128,1024]{2,1,0:T(8,128)(2,1)S(1)}, bf16[2,128,1024]{2,1,0:T(8,128)(2,1)S(1)}, u32[]{:S(2)}, u32[]{:S(2)}) collective-permute-start(bf16[2,128,1024]{2,1,0:T(8,128)(2,1)S(1)} %collective-permute-done.18.refs_9_), channel_id=1, source_target_pairs={{0,1},{1,0},{2,3},{3,2},{4,5},{5,4},{6,7},{7,6},{8,9},{9,8},{10,11... | collective-permute-start | bytes 1572872 | tf_op jit(solution)/shard_map/Oc/ppermute | solution.py:427
  94.6 4.8 %collective-permute-start.19 = (bf16[2,128,1024]{2,1,0:T(8,128)(2,1)S(1)}, bf16[2,128,1024]{2,1,0:T(8,128)(2,1)S(1)}, u32[]{:S(2)}, u32[]{:S(2)}) collective-permute-start(bf16[2,128,1024]{2,1,0:T(8,128)(2,1)S(1)} %collective-permute-done.13.refs_8_), channel_id=1, source_target_pairs={{0,1},{1,0},{2,3},{3,2},{4,5},{5,4},{6,7},{7,6},{8,9},{9,8},{10,11... | collective-permute-start | bytes 1572872 | tf_op jit(solution)/shard_map/Oc/ppermute | solution.py:427
  98.8 1.7 %collective-permute-start.27 = (bf16[128,1024]{1,0:T(8,128)(2,1)S(1)}, bf16[128,1024]{1,0:T(8,128)(2,1)S(1)}, u32[]{:S(2)}, u32[]{:S(2)}) collective-permute-start(bf16[128,1024]{1,0:T(8,128)(2,1)S(1)} %collective-permute-done.22.refs_4_), channel_id=1, source_target_pairs={{0,1},{1,0},{2,3},{3,2},{4,5},{5,4},{6,7},{7,6},{8,9},{9,8},{10,11... | collective-permute-start | bytes 786440 | tf_op jit(solution)/shard_map/Oc/ppermute | solution.py:427
  99.3 1.5 %collective-permute-start.26 = (bf16[128,1024]{1,0:T(8,128)(2,1)S(1)}, bf16[128,1024]{1,0:T(8,128)(2,1)S(1)}, u32[]{:S(2)}, u32[]{:S(2)}) collective-permute-start(bf16[128,1024]{1,0:T(8,128)(2,1)S(1)} %collective-permute-done.21.refs_3_), channel_id=1, source_target_pairs={{0,1},{1,0},{2,3},{3,2},{4,5},{5,4},{6,7},{7,6},{8,9},{9,8},{10,11... | collective-permute-start | bytes 786440 | tf_op jit(solution)/shard_map/Oc/ppermute | solution.py:427
  (3 other events, 26.8 us)
